TPU v7x, 32 devices: a whole 2x2x4 slice. The times are simulated.
32 devices in a mesh: grp: 8 (over z, y), row: 4 (over x, core).
Axes of the slice: x: 2, y: 2, z: 4, core: 2. Of those that a mesh axis runs over, the one named last changes fastest.
Arguments:
- frames: bfloat16 [16384, 1024], P(('grp', 'row')), may hold values from -6 to 6
- time_embed: float32 [8, 4, 1024], P('grp'), may hold values from -6 to 6
- lengths: int32 [8, 4], P('grp'), may hold values from 1 to 1792, 2048 in all within a row
- mod_weight: bfloat16 [1024, 6144], replicated, may hold values from -0.1875 to 0.1875
- mod_bias: float32 [6144], replicated, may hold values from -2 to 2
- query_weight: bfloat16 [1024, 1024], replicated, may hold values from -0.1875 to 0.1875
- query_bias: float32 [1024], replicated, may hold values from -3 to 3
- key_weight: bfloat16 [1024, 1024], replicated, may hold values from -0.1875 to 0.1875
- key_bias: float32 [1024], replicated, may hold values from -3 to 3
- value_weight: bfloat16 [1024, 1024], replicated, may hold values from -0.1875 to 0.1875
- value_bias: float32 [1024], replicated, may hold values from -3 to 3
- out_weight: bfloat16 [1024, 1024], replicated, may hold values from -0.75 to 0.75
- out_bias: float32 [1024], replicated, may hold values from -3 to 3
- up_weight: bfloat16 [1024, 2048], replicated, may hold values from -0.1875 to 0.1875
- up_bias: float32 [2048], replicated, may hold values from -3 to 3
- down_weight: bfloat16 [2048, 1024], replicated, may hold values from -0.125 to 0.125
- down_bias: float32 [1024], replicated, may hold values from -3 to 3
- cotangent: bfloat16 [16384, 1024], P(('grp', 'row')), may hold values from -6 to 6
Outputs:
- output: bfloat16 [16384, 1024], P(('grp', 'row'))
- frames_grad: bfloat16 [16384, 1024], P(('grp', 'row'))
- embed_grad: float32 [8, 4, 1024], P('grp')
- mod_weight_grad: float32 [1024, 6144], P('row')
- mod_bias_grad: float32 [6144], P('row')
- query_weight_grad: float32 [1024, 1024], P('row')
- query_bias_grad: float32 [1024], P('row')
- key_weight_grad: float32 [1024, 1024], P('row')
- key_bias_grad: float32 [1024], P('row')
- value_weight_grad: float32 [1024, 1024], P('row')
- value_bias_grad: float32 [1024], P('row')
- out_weight_grad: float32 [1024, 1024], P('row')
- out_bias_grad: float32 [1024], P('row')
- up_weight_grad: float32 [1024, 2048], P('row')
- up_bias_grad: float32 [2048], P('row')
- down_weight_grad: float32 [2048, 1024], P('row')
- down_bias_grad: float32 [1024], P('row')
Inputs may be any that keep to these rules, and one draw needn't show every extreme that they name: Each row of lengths is one group: its 4 lengths add up to 2048, and the largest is exactly 1792.
All inputs are finite; a program needn't handle non-finite values.
Results may differ from a plain program's by a relative error of at most 0.028.
Values may be sent and summed in bfloat16 or wider, within the bound.
A program may use at most 256 MiB of HBM per device.

v0:
```python
import math

import jax
import jax.numpy as jnp
from jax import lax
from jax.sharding import PartitionSpec as P

D = 1024
HEADS = 16
HEAD_DIM = 64


highest = lax.Precision.HIGHEST


def contract_rows(left, right):
    return lax.dot_general(
        left, right, (((0,), (0,)), ((), ())), preferred_element_type=jnp.float32
    )


def against(left, weight):
    return lax.dot_general(
        left, weight, (((1,), (1,)), ((), ())), preferred_element_type=jnp.float32
    )


def column_sum(tensor):
    return jnp.sum(tensor.astype(jnp.float32), axis=0)


def normalize(tensor):
    centred = tensor - jnp.mean(tensor, axis=-1, keepdims=True)
    factor = lax.rsqrt(jnp.mean(centred * centred, axis=-1, keepdims=True) + 1e-06)
    return (centred * factor, factor)


def normalize_back(grad_normed, normed, factor):
    mean_grad = jnp.mean(grad_normed, axis=-1, keepdims=True)
    mean_cross = jnp.mean(grad_normed * normed, axis=-1, keepdims=True)
    return (grad_normed - mean_grad - normed * mean_cross) * factor


def rotary_tables(position):
    half_dim = HEAD_DIM // 2
    frequency = jnp.exp(
        jnp.arange(half_dim, dtype=jnp.float32) * (-2.0 * math.log(10000.0) / HEAD_DIM)
    )
    angles = position.astype(jnp.float32)[:, None] * frequency[None, :]
    angles = jnp.concatenate([angles, angles], axis=1)
    return (jnp.cos(angles), jnp.sin(angles))


def turn_half(tensor):
    half_dim = tensor.shape[-1] // 2
    return jnp.concatenate([-tensor[..., half_dim:], tensor[..., :half_dim]], axis=-1)


def rotate(tensor, cosine, sine_table):
    return tensor * cosine[:, None, :] + turn_half(tensor) * sine_table[:, None, :]


def rotate_back(tensor, cosine, sine_table):
    return tensor * cosine[:, None, :] - turn_half(tensor * sine_table[:, None, :])


def block_scores(queries, keys_all, seg_query, seg_keys, offset, key_block):
    key_part = lax.dynamic_slice_in_dim(keys_all, offset, key_block, 0).reshape(
        key_block, HEADS, HEAD_DIM
    )
    seg_part = lax.dynamic_slice_in_dim(seg_keys, offset, key_block, 0)
    scores = jnp.einsum(
        "qhd,khd->hqk", queries, key_part, preferred_element_type=jnp.float32
    ) * HEAD_DIM ** (-0.5)
    allowed = (seg_query[:, None] == seg_part[None, :])[None]
    return (jnp.where(allowed, scores, -1e30), key_part)


def value_block(values_all, offset, key_block):
    return lax.dynamic_slice_in_dim(values_all, offset, key_block, 0).reshape(
        key_block, HEADS, HEAD_DIM
    )


def attend_forward(queries, keys_all, values_all, seg_query, seg_keys, key_block):
    row_count = queries.shape[0]
    blocks = keys_all.shape[0] // key_block
    numbers = jnp.arange(blocks, dtype=jnp.int32)

    def running(carry, number):
        top_score, exp_total = carry
        scores, unused = block_scores(
            queries, keys_all, seg_query, seg_keys, number * key_block, key_block
        )
        new_top = jnp.maximum(top_score, jnp.max(scores, axis=-1))
        exp_total = exp_total * jnp.exp(top_score - new_top) + jnp.sum(
            jnp.exp(scores - new_top[..., None]), axis=-1
        )
        return ((new_top, exp_total), None)

    start_top = jnp.full((HEADS, row_count), -1e30, jnp.float32)
    start_total = jnp.zeros((HEADS, row_count), jnp.float32)
    (top_score, exp_total), unused = lax.scan(running, (start_top, start_total), numbers)
    log_total = top_score + jnp.log(exp_total)

    def weighted(mixed_sum, number):
        offset = number * key_block
        scores, unused = block_scores(queries, keys_all, seg_query, seg_keys, offset, key_block)
        weights_low = jnp.exp(scores - log_total[..., None]).astype(jnp.bfloat16)
        update = jnp.einsum(
            "hqk,khd->qhd",
            weights_low,
            value_block(values_all, offset, key_block),
            preferred_element_type=jnp.float32,
        )
        return (mixed_sum + update, None)

    mixed_sum, unused = lax.scan(
        weighted, jnp.zeros((row_count, HEADS, HEAD_DIM), jnp.float32), numbers
    )
    return (log_total, mixed_sum)


def attend_backward(
    queries, keys_all, values_all, seg_query, seg_keys, key_block, log_total, grad_heads, row_dots
):
    row_count = queries.shape[0]
    total_keys = keys_all.shape[0]
    numbers = jnp.arange(total_keys // key_block, dtype=jnp.int32)

    def spread_back(grad_queries, number):
        offset = number * key_block
        scores, key_part = block_scores(queries, keys_all, seg_query, seg_keys, offset, key_block)
        probs_full = jnp.exp(scores - log_total[..., None])
        grad_probs = jnp.einsum(
            "qhd,khd->hqk",
            grad_heads,
            value_block(values_all, offset, key_block),
            preferred_element_type=jnp.float32,
        )
        grad_scores = (probs_full * (grad_probs - row_dots[..., None])).astype(jnp.bfloat16)
        grad_queries = grad_queries + jnp.einsum(
            "hqk,khd->qhd", grad_scores, key_part, preferred_element_type=jnp.float32
        ) * HEAD_DIM ** (-0.5)
        grad_keys = jnp.einsum(
            "hqk,qhd->khd", grad_scores, queries, preferred_element_type=jnp.float32
        ) * HEAD_DIM ** (-0.5)
        grad_values = jnp.einsum(
            "hqk,qhd->khd",
            probs_full.astype(jnp.bfloat16),
            grad_heads,
            preferred_element_type=jnp.float32,
        )
        return (grad_queries, (grad_keys, grad_values))

    grad_queries, stacked = lax.scan(
        spread_back, jnp.zeros((row_count, HEADS, HEAD_DIM), jnp.float32), numbers
    )
    return (grad_queries, stacked[0].reshape(total_keys, D), stacked[1].reshape(total_keys, D))


def local(
    frames,
    time_embed,
    lengths,
    mod_weight,
    mod_bias,
    query_weight,
    query_bias,
    key_weight,
    key_bias,
    value_weight,
    value_bias,
    out_weight,
    out_bias,
    up_weight,
    up_bias,
    down_weight,
    down_bias,
    cotangent,
):
    row_count = frames.shape[0]
    n_row = lax.axis_size("row")
    my_row = lax.axis_index("row")
    group_rows = row_count * n_row
    key_block = min(512, group_rows)
    utt_sizes = lengths[0]
    finish = jnp.cumsum(utt_sizes)
    starts = finish - utt_sizes
    places = jnp.arange(group_rows, dtype=jnp.int32)
    seg_keys = jnp.sum((places[:, None] >= finish[None, :]).astype(jnp.int32), axis=1)
    first_row = my_row * row_count
    seg_query = lax.dynamic_slice_in_dim(seg_keys, first_row, row_count, 0)
    own_places = first_row + jnp.arange(row_count, dtype=jnp.int32)
    is_member = seg_query[:, None] == jnp.arange(utt_sizes.shape[0], dtype=jnp.int32)[None, :]
    position = own_places - jnp.sum(jnp.where(is_member, starts[None, :], 0), axis=1)
    member = is_member.astype(jnp.float32)
    cosine, sine_table = rotary_tables(position)
    embedding = time_embed[0]
    act_low = jax.nn.silu(embedding).astype(jnp.bfloat16)
    modulation = jnp.dot(act_low, mod_weight, preferred_element_type=jnp.float32) + mod_bias
    per_token = jnp.dot(member, modulation, precision=highest, preferred_element_type=jnp.float32)
    shift_attn, scale_attn, gate_attn, shift_ffn, scale_ffn, gate_ffn = jnp.split(
        per_token, 6, axis=1
    )
    residual = frames.astype(jnp.float32)
    normed_attn, factor_attn = normalize(residual)
    mixed_in = (normed_attn * (1.0 + scale_attn) + shift_attn).astype(jnp.bfloat16)
    queries = jnp.dot(mixed_in, query_weight, preferred_element_type=jnp.float32) + query_bias
    keys_pre = jnp.dot(mixed_in, key_weight, preferred_element_type=jnp.float32) + key_bias
    values_own = (
        jnp.dot(mixed_in, value_weight, preferred_element_type=jnp.float32) + value_bias
    ).astype(jnp.bfloat16)
    query_rot = rotate(queries.reshape(row_count, HEADS, HEAD_DIM), cosine, sine_table).astype(
        jnp.bfloat16
    )
    keys_rot = rotate(keys_pre.reshape(row_count, HEADS, HEAD_DIM), cosine, sine_table).astype(
        jnp.bfloat16
    )
    keys_rot = keys_rot.reshape(row_count, D)
    keys_all, values_all = (
        lax.all_gather(keys_rot, "row", axis=0, tiled=True),
        lax.all_gather(values_own, "row", axis=0, tiled=True),
    )
    log_total, attn_heads = attend_forward(
        query_rot, keys_all, values_all, seg_query, seg_keys, key_block
    )
    attn_low = attn_heads.reshape(row_count, D).astype(jnp.bfloat16)
    attended = jnp.dot(attn_low, out_weight, preferred_element_type=jnp.float32) + out_bias
    middle = residual + gate_attn * attended
    normed_ffn, factor_ffn = normalize(middle)
    ffn_in = (normed_ffn * (1.0 + scale_ffn) + shift_ffn).astype(jnp.bfloat16)
    hidden = jnp.dot(ffn_in, up_weight, preferred_element_type=jnp.float32) + up_bias
    active_low = jax.nn.gelu(hidden, approximate=True).astype(jnp.bfloat16)
    branch = jnp.dot(active_low, down_weight, preferred_element_type=jnp.float32) + down_bias
    output = (middle + gate_ffn * branch).astype(jnp.bfloat16)
    upstream = cotangent.astype(jnp.float32)
    grad_branch = (upstream * gate_ffn).astype(jnp.bfloat16)
    grad_gate_ffn = upstream * branch
    grad_active = against(grad_branch, down_weight)
    unused, gelu_pull = jax.vjp(lambda tensor: jax.nn.gelu(tensor, approximate=True), hidden)
    grad_hidden = gelu_pull(grad_active)[0].astype(jnp.bfloat16)
    grad_ffn_in = against(grad_hidden, up_weight)
    grad_scale_ffn = grad_ffn_in * normed_ffn
    grad_middle = upstream + normalize_back(grad_ffn_in * (1.0 + scale_ffn), normed_ffn, factor_ffn)
    grad_attended = (grad_middle * gate_attn).astype(jnp.bfloat16)
    grad_gate_attn = grad_middle * attended
    grad_heads = (
        against(grad_attended, out_weight).astype(jnp.bfloat16).reshape(row_count, HEADS, HEAD_DIM)
    )
    dots_rows = jnp.einsum("qhd,qhd->qh", attn_heads, grad_heads.astype(jnp.float32))
    row_dots = dots_rows.T
    keys_back, values_back = (keys_all, values_all)
    grad_query_rot, grad_keys_all, grad_values_all = attend_backward(
        query_rot,
        keys_back,
        values_back,
        seg_query,
        seg_keys,
        key_block,
        log_total,
        grad_heads,
        row_dots,
    )
    grad_keys_own, grad_values_own = (
        lax.psum_scatter(
            grad_keys_all.astype(jnp.bfloat16), "row", scatter_dimension=0, tiled=True
        ).astype(jnp.float32),
        lax.psum_scatter(
            grad_values_all.astype(jnp.bfloat16), "row", scatter_dimension=0, tiled=True
        ).astype(jnp.float32),
    )
    grad_queries = (
        rotate_back(grad_query_rot, cosine, sine_table).reshape(row_count, D).astype(jnp.bfloat16)
    )
    grad_keys = rotate_back(grad_keys_own.reshape(row_count, HEADS, HEAD_DIM), cosine, sine_table)
    grad_keys = grad_keys.reshape(row_count, D).astype(jnp.bfloat16)
    grad_values = grad_values_own.astype(jnp.bfloat16)
    grad_mixed_in = (
        against(grad_queries, query_weight)
        + against(grad_keys, key_weight)
        + against(grad_values, value_weight)
    )
    grad_frames = grad_middle + normalize_back(
        grad_mixed_in * (1.0 + scale_attn), normed_attn, factor_attn
    )
    grad_tokens = jnp.concatenate(
        [
            grad_mixed_in,
            grad_mixed_in * normed_attn,
            grad_gate_attn,
            grad_ffn_in,
            grad_scale_ffn,
            grad_gate_ffn,
        ],
        axis=1,
    )
    grad_mod_part = lax.dot_general(
        member,
        grad_tokens,
        (((0,), (0,)), ((), ())),
        precision=highest,
        preferred_element_type=jnp.float32,
    )
    grad_modulation = lax.psum(grad_mod_part.astype(jnp.bfloat16), "row")
    grad_activated = against(grad_modulation, mod_weight)
    unused, silu_pull = jax.vjp(jax.nn.silu, embedding)
    grad_embedding = silu_pull(grad_activated)[0]
    slice_width = D // n_row
    act_slice = lax.dynamic_slice_in_dim(act_low, my_row * slice_width, slice_width, 1)
    mod_weight_part = contract_rows(act_slice, grad_modulation)
    mod_bias_part = lax.dynamic_slice_in_dim(
        column_sum(grad_modulation), my_row * 6 * slice_width, 6 * slice_width, 0
    )
    reorder = lambda tensor: tensor
    left_attn = reorder(mixed_in)
    shares = (
        lax.psum_scatter(
            contract_rows(left_attn, grad_queries).astype(jnp.bfloat16),
            "row",
            scatter_dimension=0,
            tiled=True,
        ).astype(jnp.float32),
        lax.psum_scatter(
            contract_rows(left_attn, grad_keys).astype(jnp.bfloat16),
            "row",
            scatter_dimension=0,
            tiled=True,
        ).astype(jnp.float32),
        lax.psum_scatter(
            contract_rows(left_attn, grad_values).astype(jnp.bfloat16),
            "row",
            scatter_dimension=0,
            tiled=True,
        ).astype(jnp.float32),
        lax.psum_scatter(
            contract_rows(reorder(attn_low), grad_attended).astype(jnp.bfloat16),
            "row",
            scatter_dimension=0,
            tiled=True,
        ).astype(jnp.float32),
        lax.psum_scatter(
            contract_rows(reorder(ffn_in), grad_hidden).astype(jnp.bfloat16),
            "row",
            scatter_dimension=0,
            tiled=True,
        ).astype(jnp.float32),
        lax.psum_scatter(
            contract_rows(reorder(active_low), grad_branch).astype(jnp.bfloat16),
            "row",
            scatter_dimension=0,
            tiled=True,
        ).astype(jnp.float32),
        lax.psum_scatter(
            reorder(column_sum(grad_queries)).astype(jnp.bfloat16),
            "row",
            scatter_dimension=0,
            tiled=True,
        ).astype(jnp.float32),
        lax.psum_scatter(
            reorder(column_sum(grad_keys)).astype(jnp.bfloat16),
            "row",
            scatter_dimension=0,
            tiled=True,
        ).astype(jnp.float32),
        lax.psum_scatter(
            reorder(column_sum(grad_values)).astype(jnp.bfloat16),
            "row",
            scatter_dimension=0,
            tiled=True,
        ).astype(jnp.float32),
        lax.psum_scatter(
            reorder(column_sum(grad_attended)).astype(jnp.bfloat16),
            "row",
            scatter_dimension=0,
            tiled=True,
        ).astype(jnp.float32),
        lax.psum_scatter(
            reorder(column_sum(grad_hidden)).astype(jnp.bfloat16),
            "row",
            scatter_dimension=0,
            tiled=True,
        ).astype(jnp.float32),
        lax.psum_scatter(
            reorder(column_sum(grad_branch)).astype(jnp.bfloat16),
            "row",
            scatter_dimension=0,
            tiled=True,
        ).astype(jnp.float32),
    )
    totals = (
        lax.psum(shares[0].astype(jnp.bfloat16), "grp").astype(jnp.float32),
        lax.psum(shares[1].astype(jnp.bfloat16), "grp").astype(jnp.float32),
        lax.psum(shares[2].astype(jnp.bfloat16), "grp").astype(jnp.float32),
        lax.psum(shares[3].astype(jnp.bfloat16), "grp").astype(jnp.float32),
        lax.psum(shares[4].astype(jnp.bfloat16), "grp").astype(jnp.float32),
        lax.psum(shares[5].astype(jnp.bfloat16), "grp").astype(jnp.float32),
        lax.psum(shares[6].astype(jnp.bfloat16), "grp").astype(jnp.float32),
        lax.psum(shares[7].astype(jnp.bfloat16), "grp").astype(jnp.float32),
        lax.psum(shares[8].astype(jnp.bfloat16), "grp").astype(jnp.float32),
        lax.psum(shares[9].astype(jnp.bfloat16), "grp").astype(jnp.float32),
        lax.psum(shares[10].astype(jnp.bfloat16), "grp").astype(jnp.float32),
        lax.psum(shares[11].astype(jnp.bfloat16), "grp").astype(jnp.float32),
        lax.psum(mod_weight_part.astype(jnp.bfloat16), "grp").astype(jnp.float32),
        lax.psum(mod_bias_part.astype(jnp.bfloat16), "grp").astype(jnp.float32),
    )
    return (
        output,
        grad_frames.astype(jnp.bfloat16),
        grad_embedding[None],
        totals[12],
        totals[13],
        totals[0],
        totals[6],
        totals[1],
        totals[7],
        totals[2],
        totals[8],
        totals[3],
        totals[9],
        totals[4],
        totals[10],
        totals[5],
        totals[11],
    )


def solution(mesh):
    placed = (
        P(("grp", "row"), None),
        P("grp", None, None),
        P("grp", None),
        P(),
        P(),
        P(),
        P(),
        P(),
        P(),
        P(),
        P(),
        P(),
        P(),
        P(),
        P(),
        P(),
        P(),
        P(("grp", "row"), None),
    )
    return jax.shard_map(
        local,
        mesh=mesh,
        in_specs=placed,
        out_specs=(
            P(("grp", "row"), None),
            P(("grp", "row"), None),
            P("grp", None, None),
            P("row", None),
            P("row"),
            P("row", None),
            P("row"),
            P("row", None),
            P("row"),
            P("row", None),
            P("row"),
            P("row", None),
            P("row"),
            P("row", None),
            P("row"),
            P("row", None),
            P("row"),
        ),
        check_vma=False,
    )
```

profile of v0, /device:TPU:0, one launch (start us, length us, event | category | flops | bytes accessed | tf_op | source)
XLA Modules:
  0.0 1056.1 jit_solution(15649840232592552470)
XLA Ops:
  17.2 6.3 convolution_add_fusion
  67.8 29.9 %all-gather.5.cloned.1.call-done = bf16[2048,1024]{1,0:T(8,128)(2,1)} async-done(((bf16[512,1024]{1,0:T(8,128)(2,1)}), bf16[2048,1024]{1,0:T(8,128)(2,1)}) %all-gather.5.cloned.1.call-update) | async-done | bytes 4194320 | tf_op jit(solution)/shard_map/all_gather | solution.py:222
  97.7 6.5 copy.96
  104.2 77.6 %while.39 = (s32[]{:T(128)}, f32[16,512]{1,0:T(8,128)S(1)}, f32[16,512]{1,0:T(8,128)S(1)}, s32[512]{0:T(512)S(1)}, s32[4]{0:T(128)S(1)}, /*index=5*/s32[2048]{0:...) while((s32[]{:T(128)}, f32[16,512]{1,0:T(8,128)S(1)}, ...), condition=%wide.region_8.9_spmd.clone, body=%wide.region_5.8_spmd.clone.sunk | while | flops 566534144 | bytes 38969544 | solution.py:103
  107.2 7.3 fusion.159
  114.5 9.2 exponential_reduce_fusion.2
  126.6 7.3 fusion.159
  134.0 9.2 exponential_reduce_fusion.2
  146.1 7.3 fusion.159
  153.3 9.2 exponential_reduce_fusion.2
  165.4 7.3 fusion.159
  172.7 9.2 exponential_reduce_fusion.2
  181.9 6.4 copy.95
  188.4 53.3 %while.40 = (s32[]{:T(128)}, f32[512,16,64]{0,2,1:T(8,128)}, s32[4]{0:T(128)S(1)}, bf16[2048,1024]{0,1:T(8,128)(2,1)}, s32[512]{0:T(512)S(1)}, /*index=5*/s32[20...) while((s32[]{:T(128)}, f32[512,16,64]{0,2,1:T(8,128)}, ...), condition=%wide.region_10.11_spmd.clone, body=%wide.region_9.10_spmd.clone.sunk | while | flops 1091829760 | bytes 12099793 | solution.py:118
  192.9 8.2 bitcast_add_fusion.4
  205.7 8.9 bitcast_add_fusion.4
  219.2 8.9 bitcast_add_fusion.4
  232.6 8.9 bitcast_add_fusion.4
  258.3 9.3 fusion.71
  267.7 6.9 fusion.66
  285.6 165.9 %while.41 = (s32[]{:T(128)}, f32[512,16,64]{0,2,1:T(8,128)}, bf16[4,512,16,64]{1,3,2,0:T(8,128)(2,1)}, bf16[4,512,16,64]{1,3,2,0:T(8,128)(2,1)}, s32[4]{0:T(128)...) while((s32[]{:T(128)}, f32[512,16,64]{0,2,1:T(8,128)}, ...), condition=%wide.region_16.17_spmd.clone, body=%wide.region_15.16_spmd.clone.sunk | while | flops 2728656896 | bytes 121479528 | solution.py:156
  289.9 9.4 fusion.174
  299.2 11.0 %bitcast_dynamic-update-slice_fusion.5 = bf16[4,512,16,64]{1,3,2,0:T(8,128)(2,1)} fusion(bf16[4,512,16,64]{1,3,2,0:T(8,128)(2,1)} %get-tuple-element.818, s32[]{:T(128)S(6)} %copy.138, bf16[512,16,64]{0,2,1:T(8,128)(2,1)} %get-tuple-element.843, f32[16,512,512]{2,1,0:T(8,128)} %fusion.174, f32[16,512]{1,0:T(8,128)S(1)} %get-tuple-element.841, ...), kind=kOutput, calls=%fused_computation.27.clone.1 | convolution fusion | flops 553648128 | bytes 20217860 | tf_op jit(solution)/shard_map/while/body/eval_jaxpr/hqk,qhd->khd/dot_general | solution.py:148
  310.3 9.5 fusion.175
  331.3 9.4 fusion.174
  340.7 11.0 %bitcast_dynamic-update-slice_fusion.5 = bf16[4,512,16,64]{1,3,2,0:T(8,128)(2,1)} fusion(bf16[4,512,16,64]{1,3,2,0:T(8,128)(2,1)} %get-tuple-element.818, s32[]{:T(128)S(6)} %copy.138, bf16[512,16,64]{0,2,1:T(8,128)(2,1)} %get-tuple-element.843, f32[16,512,512]{2,1,0:T(8,128)} %fusion.174, f32[16,512]{1,0:T(8,128)S(1)} %get-tuple-element.841, ...), kind=kOutput, calls=%fused_computation.27.clone.1 | convolution fusion | flops 553648128 | bytes 20217860 | tf_op jit(solution)/shard_map/while/body/eval_jaxpr/hqk,qhd->khd/dot_general | solution.py:148
  351.7 9.5 fusion.175
  372.7 9.4 fusion.174
  382.1 11.0 %bitcast_dynamic-update-slice_fusion.5 = bf16[4,512,16,64]{1,3,2,0:T(8,128)(2,1)} fusion(bf16[4,512,16,64]{1,3,2,0:T(8,128)(2,1)} %get-tuple-element.818, s32[]{:T(128)S(6)} %copy.138, bf16[512,16,64]{0,2,1:T(8,128)(2,1)} %get-tuple-element.843, f32[16,512,512]{2,1,0:T(8,128)} %fusion.174, f32[16,512]{1,0:T(8,128)S(1)} %get-tuple-element.841, ...), kind=kOutput, calls=%fused_computation.27.clone.1 | convolution fusion | flops 553648128 | bytes 20217860 | tf_op jit(solution)/shard_map/while/body/eval_jaxpr/hqk,qhd->khd/dot_general | solution.py:148
  393.1 9.5 fusion.175
  414.1 9.4 fusion.174
  423.5 11.0 %bitcast_dynamic-update-slice_fusion.5 = bf16[4,512,16,64]{1,3,2,0:T(8,128)(2,1)} fusion(bf16[4,512,16,64]{1,3,2,0:T(8,128)(2,1)} %get-tuple-element.818, s32[]{:T(128)S(6)} %copy.138, bf16[512,16,64]{0,2,1:T(8,128)(2,1)} %get-tuple-element.843, f32[16,512,512]{2,1,0:T(8,128)} %fusion.174, f32[16,512]{1,0:T(8,128)S(1)} %get-tuple-element.841, ...), kind=kOutput, calls=%fused_computation.27.clone.1 | convolution fusion | flops 553648128 | bytes 20217860 | tf_op jit(solution)/shard_map/while/body/eval_jaxpr/hqk,qhd->khd/dot_general | solution.py:148
  434.5 9.5 fusion.175
  451.4 5.7 copy.101
  460.6 5.7 copy.100
  476.5 7.5 convolution_convert_fusion.2
  485.2 6.0 convolution_convert_fusion.3
  491.3 14.3 %reduce-scatter.11.cloned.1.call-done = bf16[512,1024]{0,1:T(8,128)(2,1)} async-done(((bf16[2048,1024]{0,1:T(8,128)(2,1)}), bf16[512,1024]{0,1:T(8,128)(2,1)}) %reduce-scatter.11.cloned.1.call-update) | async-done | bytes 1048592 | tf_op jit(solution)/shard_map/reduce_scatter | solution.py:269
  509.4 43.2 %reduce-scatter.9.cloned.1.call-done = bf16[512,1024]{0,1:T(8,128)(2,1)} async-done(((bf16[2048,1024]{0,1:T(8,128)(2,1)}), bf16[512,1024]{0,1:T(8,128)(2,1)}) %reduce-scatter.9.cloned.1.call-update) | async-done | bytes 1048592 | tf_op jit(solution)/shard_map/reduce_scatter | solution.py:266
  596.1 10.8 %all-reduce.8 = (bf16[4,6144]{1,0:T(4,128)(2,1)S(1)}, bf16[1024]{0:T(1024)(128)(2,1)S(1)}, bf16[1024]{0:T(1024)(128)(2,1)S(1)}, bf16[1024]{0:T(1024)(128)(2,1)S(...) all-reduce(bf16[4,6144]{1,0:T(4,128)(2,1)S(1)} %convolution_convert, ...), channel_id=1, replica_groups=mesh['grp'=8,'row'=4] {'row'}, use_global_device_ids=true, to_apply=%region_21.22 | all-reduce | flops 31744 | bytes 126976 | tf_op jit(solution)/shard_map/psum | solution.py:305
  610.3 23.2 %reduce-scatter.23.cloned.1.call-done = bf16[512,1024]{1,0:T(8,128)(2,1)} async-done(((bf16[2048,1024]{1,0:T(8,128)(2,1)}), bf16[512,1024]{1,0:T(8,128)(2,1)}) %reduce-scatter.23.cloned.1.call-update) | async-done | bytes 1048592 | tf_op jit(solution)/shard_map/reduce_scatter | solution.py:348
  633.6 47.1 %reduce-scatter.21.cloned.1.call-done = bf16[256,2048]{1,0:T(8,128)(2,1)} async-done(((bf16[1024,2048]{1,0:T(8,128)(2,1)}), bf16[256,2048]{1,0:T(8,128)(2,1)}) %reduce-scatter.21.cloned.1.call-update) | async-done | bytes 1048592 | tf_op jit(solution)/shard_map/reduce_scatter | solution.py:342
  680.6 34.2 %reduce-scatter.17.cloned.1.call-done = bf16[256,1024]{1,0:T(8,128)(2,1)} async-done(((bf16[1024,1024]{1,0:T(8,128)(2,1)}), bf16[256,1024]{1,0:T(8,128)(2,1)}) %reduce-scatter.17.cloned.1.call-update) | async-done | bytes 524304 | tf_op jit(solution)/shard_map/reduce_scatter | solution.py:330
  714.8 34.0 %reduce-scatter.15.cloned.1.call-done = bf16[256,1024]{1,0:T(8,128)(2,1)} async-done(((bf16[1024,1024]{1,0:T(8,128)(2,1)}), bf16[256,1024]{1,0:T(8,128)(2,1)}) %reduce-scatter.15.cloned.1.call-update) | async-done | bytes 524304 | tf_op jit(solution)/shard_map/reduce_scatter | solution.py:324
  748.8 34.0 %reduce-scatter.13.cloned.1.call-done = bf16[256,1024]{1,0:T(8,128)(2,1)} async-done(((bf16[1024,1024]{1,0:T(8,128)(2,1)}), bf16[256,1024]{1,0:T(8,128)(2,1)}) %reduce-scatter.13.cloned.1.call-update) | async-done | bytes 524304 | tf_op jit(solution)/shard_map/reduce_scatter | solution.py:318
  786.0 22.2 %all-reduce.6 = (bf16[1536]{0:T(1024)(128)(2,1)S(1)}, bf16[256]{0:T(256)(128)(2,1)S(1)}, bf16[256]{0:T(256)(128)(2,1)S(1)}, bf16[256]{0:T(256)(128)(2,1)S(1)}, b...) all-reduce(bf16[1536]{0:T(1024)(128)(2,1)S(1)} %dynamic_slice.65, ...), channel_id=1, replica_groups=mesh['grp'=8,'row'=4] {'grp'}, use_global_device_ids=true, to_apply=%region_24.25 | all-reduce | flops 3328 | bytes 13312 | tf_op jit(solution)/shard_map/psum | solution.py:405
  812.2 8.7 fusion.55
  820.9 214.2 %all-reduce.11.cloned.1.call-done = (bf16[256,6144]{1,0:T(8,128)(2,1)}, bf16[256,1024]{1,0:T(8,128)(2,1)}, bf16[256,1024]{1,0:T(8,128)(2,1)}, bf16[256,1024]{1,0...) async-done(((bf16[256,6144]{1,0:T(8,128)(2,1)}, bf16[256,1024]{1,0:T(8,128)(2,1)}, bf16[256,1024]{1,0:T(8,128)(2,1)}, ...) | async-done | bytes 7340048 | tf_op jit(solution)/shard_map/psum | solution.py:404
  (380 shorter events, 234.5 us)
Async XLA Ops:
  7.2 53.3 %copy-start = (bf16[1024,1024]{1,0:T(8,128)(2,1)S(1)}, bf16[1024,1024]{1,0:T(8,128)(2,1)}, u32[]{:S(2)}) copy-start(bf16[1024,1024]{1,0:T(8,128)(2,1)} %param.33) | copy-start | bytes 6291460
  7.2 5.1 copy-start.48
  7.2 90.5 %all-gather.5.cloned.1.call-start = ((), (), s32[]{:S(2)}) async-start(), calls=%async_computation.9 | async-start | bytes 5242880 | tf_op jit(solution)/shard_map/all_gather | solution.py:222
  10.3 18.3 %copy-start.51 = (f32[512]{0:T(512)}, f32[512]{0:T(512)S(1)}, u32[]{:S(2)}) copy-start(f32[512]{0:T(512)S(1)} %broadcast_multiply_fusion.8) | copy-start | bytes 6148
  12.0 16.6 %copy-start.57 = (f32[512]{0:T(512)}, f32[512]{0:T(512)S(1)}, u32[]{:S(2)}) copy-start(f32[512]{0:T(512)S(1)} %add_rsqrt_fusion.1) | copy-start | bytes 6148
  12.3 4.9 copy-start.50
  12.6 37.8 %copy-start.24 = (f32[512,64]{0,1:T(8,128)}, f32[512,64]{0,1:T(8,128)S(1)}, u32[]{:S(2)}) copy-start(f32[512,64]{0,1:T(8,128)S(1)} %get-tuple-element.521) | copy-start | bytes 393220
  12.7 37.8 %copy-start.31 = (f32[512,64]{0,1:T(8,128)}, f32[512,64]{0,1:T(8,128)S(1)}, u32[]{:S(2)}) copy-start(f32[512,64]{0,1:T(8,128)S(1)} %get-tuple-element.522) | copy-start | bytes 393220
  23.5 9.7 copy-start.9
  28.6 4.6 copy-start.6
  60.4 121.5 %all-gather.3.cloned.1.call-start = ((), (), s32[]{:S(2)}) async-start(), calls=%async_computation.8 | async-start | bytes 5242880 | tf_op jit(solution)/shard_map/all_gather | solution.py:223
  63.9 441.6 %reduce-scatter.11.cloned.1.call-start = ((), (), s32[]{:S(2)}) async-start(), calls=%async_computation.11 | async-start | bytes 5242880 | tf_op jit(solution)/shard_map/reduce_scatter | solution.py:269
  188.4 55.3 %copy-start.55 = (f32[1024]{0:T(1024)S(1)}, f32[1024]{0:T(1024)}, u32[]{:S(2)}) copy-start(f32[1024]{0:T(1024)} %param.36) | copy-start | bytes 12292
  243.6 5.0 copy-start.19
  248.6 26.0 %copy-start.7 = (f32[512,1024]{1,0:T(8,128)}, f32[512,1024]{1,0:T(8,128)S(1)}, u32[]{:S(2)}) copy-start(f32[512,1024]{1,0:T(8,128)S(1)} %get-tuple-element.498) | copy-start | bytes 6291460
  248.6 26.0 %copy-start.53 = (f32[512]{0:T(512)}, f32[512]{0:T(512)S(1)}, u32[]{:S(2)}) copy-start(f32[512]{0:T(512)S(1)} %broadcast_multiply_fusion.7) | copy-start | bytes 6148
  249.0 25.7 %copy-start.59 = (f32[512]{0:T(512)}, f32[512]{0:T(512)S(1)}, u32[]{:S(2)}) copy-start(f32[512]{0:T(512)S(1)} %add_rsqrt_fusion) | copy-start | bytes 6148
  255.4 12.3 %slice-start = ((s8[12582912]{0:T(1024)(128)(4,1)}), s8[4194304]{0:T(1024)(128)(4,1)S(1)}, s32[]{:S(2)}) async-start(s8[12582912]{0:T(1024)(128)(4,1)} %bitcast.239), calls=%async_computation.19 | async-start | bytes 8388608
  258.2 9.4 copy-start.29
  258.3 9.4 slice-start.1
  258.3 9.4 slice-start.2
  258.3 9.4 copy-start.65
  267.6 6.9 copy-start.76
  267.7 7.0 copy-start.17
  310.3 9.6 copy-start.3
  321.4 5.7 copy-start.4
  321.4 5.7 copy-start.2
  351.7 9.6 copy-start.3
  362.8 5.7 copy-start.4
  362.8 5.7 copy-start.2
  393.1 9.6 copy-start.3
  404.2 5.6 copy-start.4
  404.2 5.6 copy-start.2
  434.5 9.6 copy-start.3
  445.6 5.7 copy-start.4
  445.6 5.7 copy-start.2
  460.6 92.1 %reduce-scatter.9.cloned.1.call-start = ((), (), s32[]{:S(2)}) async-start(), calls=%async_computation.10 | async-start | bytes 5242880 | tf_op jit(solution)/shard_map/reduce_scatter | solution.py:266
  470.2 140.1 %reduce-scatter.19.cloned.1.call-start = ((), (), s32[]{:S(2)}) async-start(), calls=%async_computation.15 | async-start | bytes 2621440 | tf_op jit(solution)/shard_map/reduce_scatter | solution.py:336
  475.3 158.2 %reduce-scatter.23.cloned.1.call-start = ((), (), s32[]{:S(2)}) async-start(), calls=%async_computation.17 | async-start | bytes 5242880 | tf_op jit(solution)/shard_map/reduce_scatter | solution.py:348
  484.0 196.6 %reduce-scatter.21.cloned.1.call-start = ((), (), s32[]{:S(2)}) async-start(), calls=%async_computation.16 | async-start | bytes 5242880 | tf_op jit(solution)/shard_map/reduce_scatter | solution.py:342
  491.2 14.3 %copy-start.40 = (bf16[512,1024]{1,0:T(8,128)(2,1)S(1)}, bf16[512,1024]{1,0:T(8,128)(2,1)}, u32[]{:S(2)}) copy-start(bf16[512,1024]{1,0:T(8,128)(2,1)} %copy-done.38) | copy-start | bytes 3145732
  491.2 223.6 %reduce-scatter.17.cloned.1.call-start = ((), (), s32[]{:S(2)}) async-start(), calls=%async_computation.14 | async-start | bytes 2621440 | tf_op jit(solution)/shard_map/reduce_scatter | solution.py:330
  509.4 43.3 %copy-start.32 = (f32[512,64]{0,1:T(8,128)S(1)}, f32[512,64]{0,1:T(8,128)}, u32[]{:S(2)}) copy-start(f32[512,64]{0,1:T(8,128)} %copy-done.31) | copy-start | bytes 393220
  509.4 239.4 %reduce-scatter.15.cloned.1.call-start = ((), (), s32[]{:S(2)}) async-start(), calls=%async_computation.13 | async-start | bytes 2621440 | tf_op jit(solution)/shard_map/reduce_scatter | solution.py:324
  561.8 221.0 %reduce-scatter.13.cloned.1.call-start = ((), (), s32[]{:S(2)}) async-start(), calls=%async_computation.12 | async-start | bytes 2621440 | tf_op jit(solution)/shard_map/reduce_scatter | solution.py:318
  574.4 460.7 %all-reduce.11.cloned.1.call-start = ((), (), s32[]{:S(2)}) async-start(), calls=%async_computation.18 | async-start | bytes 14680064 | tf_op jit(solution)/shard_map/psum | solution.py:404
  782.8 29.4 %copy-start.49 = (f32[1,4,1024]{2,1,0:T(4,128)S(1)}, f32[1,4,1024]{2,1,0:T(4,128)}, u32[]{:S(2)}) copy-start(f32[1,4,1024]{2,1,0:T(4,128)} %param.25) | copy-start | bytes 49156
  1035.1 5.5 copy-start.46
  (56 other events, 136.4 us)
Sparse Core Ops, SparseCore 0:
  60.5 37.1 all-gather.4
  99.9 34.4 all-gather.2
  460.7 44.8 reduce-scatter.10
  508.1 44.5 reduce-scatter.8
  555.0 31.4 reduce-scatter.18
  589.0 44.5 reduce-scatter.22
  636.1 44.4 reduce-scatter.20
  683.3 31.4 reduce-scatter.16
  717.3 31.4 reduce-scatter.14
  751.3 31.4 reduce-scatter.12
  788.7 246.3 all-reduce.10
where the time goes:
time: 1070 us; the launch traced here: 1060 us
  waiting for transfers between devices  474 us (44%)
  matrix products  318 us (30%)
  local copies, waits for them, and re-layouts  106 us (10%)
  other arithmetic  99.1 us (9%)
  blocking collectives  33 us (3%)
  between operations  16.3 us (2%)
    psum x1, waiting for transfers between devices, local(): lax.psum(mod_weight_part.astype(jnp.bfloat16), 'grp').astype(jnp.float32)  214 us
    dot_general x8, matrix products, block_scores(): jnp.einsum('qhd,khd->hqk', queries, key_part, preferred_element_type=jnp....  66.6 us
    reduce_scatter x1, waiting for transfers between devices, local(): lax.psum_scatter(contract_rows(reorder(ffn_in), grad_hidden).astype(jnp.b...  47.1 us
    dot_general x4, matrix products, spread_back(): jnp.einsum('hqk,qhd->khd', probs_full.astype(jnp.bfloat16), grad_heads, p...  44.1 us
    reduce_scatter x1, waiting for transfers between devices, local(): lax.psum_scatter(grad_keys_all.astype(jnp.bfloat16), 'row', scatter_dimen...  43.2 us
    unnamed x166, local copies, waits for them, and re-layouts  41.9 us
    dot_general x7, matrix products, against(): lax.dot_general(left, weight, (((1,), (1,)), ((), ())), preferred_element...  38.7 us
    dot_general x4, matrix products, spread_back(): jnp.einsum('qhd,khd->hqk', grad_heads, value_block(values_all, offset, ke...  38.2 us
  transfers between devices with their start and end apart: 11, of which 9 were waited for; matrix products, arithmetic and copies ran while one was open for 16% of the time, Pallas kernels for 0%

commit v1 on v0

v1 whole, which is shorter than its diff:
```python
import functools
import math

import jax
import jax.numpy as jnp
from jax import lax
from jax.experimental import pallas as pl
from jax.experimental.pallas import tpu as pltpu
from jax.sharding import PartitionSpec as P

D = 1024
HEADS = 16
HEAD_DIM = 64
LONGEST = 1792
TILE = 256
BF = jnp.bfloat16
F32 = jnp.float32

highest = lax.Precision.HIGHEST
VMEM = pltpu.VMEM
SMEM = pltpu.SMEM
LIMIT = 60 << 20


def matdot(left, right, left_dim, right_dim):
    return lax.dot_general(
        left, right, (((left_dim,), (right_dim,)), ((), ())), preferred_element_type=F32
    )


def contract_rows(left, right):
    return matdot(left, right, 0, 0)


def against(left, weight):
    return matdot(left, weight, 1, 1)


def column_sum(tensor):
    return jnp.sum(tensor.astype(F32), axis=0)


def normalize(tensor):
    centred = tensor - jnp.mean(tensor, axis=-1, keepdims=True)
    factor = lax.rsqrt(jnp.mean(centred * centred, axis=-1, keepdims=True) + 1e-06)
    return (centred * factor, factor)


def normalize_back(grad_normed, normed, factor):
    mean_grad = jnp.mean(grad_normed, axis=-1, keepdims=True)
    mean_cross = jnp.mean(grad_normed * normed, axis=-1, keepdims=True)
    return (grad_normed - mean_grad - normed * mean_cross) * factor


def exchange(tensor, axis, bit):
    size = lax.axis_size(axis)
    return lax.ppermute(tensor, axis, [(i, i ^ bit) for i in range(size)])


def add_low(left, right):
    return (left.astype(F32) + right.astype(F32)).astype(BF)


def grp_bit(bit):
    return (lax.axis_index("grp") // bit) % 2


def halve(tensor, dim, bit):
    side = grp_bit(bit)
    half = tensor.shape[dim] // 2
    send = lax.dynamic_slice_in_dim(tensor, (1 - side) * half, half, dim)
    keep = lax.dynamic_slice_in_dim(tensor, side * half, half, dim)
    return add_low(keep, exchange(send, "grp", bit))


def grow(tensor, dim, bit):
    other = exchange(tensor, "grp", bit)
    return jnp.where(
        grp_bit(bit) == 0,
        jnp.concatenate([tensor, other], dim),
        jnp.concatenate([other, tensor], dim),
    )


def bits_of(count):
    return [1 << i for i in range(count.bit_length() - 1)]


def roll_matrix(offset):
    row = lax.broadcasted_iota(jnp.int32, (TILE, 2 * TILE), 0)
    col = lax.broadcasted_iota(jnp.int32, (TILE, 2 * TILE), 1)
    return (col == row + offset).astype(F32).astype(BF)


def project_kernel(
    place, x0, x1, x2, x3, mod_all, mod_long, member, weight_t, bias, cos_t, sin_t,
    mixed_out, qt_out, kt_out, vt_out, k_out, v_out, rows_ref, roll_ref,
):
    step = pl.program_id(0)
    block = x0.shape[0]
    total = 4 * block

    @pl.when(step == 0)
    def _():
        for j, source in enumerate((x0, x1, x2, x3)):
            at = pl.multiple_of((place[0] ^ j) * block, block)
            rows_ref[pl.ds(at, block), :] = source[...]
        rows_ref[pl.ds(total, TILE), :] = rows_ref[pl.ds(0, TILE), :]
        roll_ref[...] = roll_matrix(place[1])

    pair = rows_ref[pl.ds(pl.multiple_of(step * TILE, TILE), 2 * TILE), :]
    normed, _ = normalize(matdot(roll_ref[...], pair, 1, 0))
    last = step == total // TILE - 1

    @pl.when(jnp.logical_not(last))
    def _():
        mixed_out[...] = (normed * (1.0 + mod_long[:, D:]) + mod_long[:, :D]).astype(BF)

    @pl.when(last)
    def _():
        per_row = jnp.zeros((TILE, 2 * D), F32)
        for u in range(mod_all.shape[0]):
            per_row = per_row + member[:, u : u + 1] * mod_all[u : u + 1, :]
        mixed_out[...] = (normed * (1.0 + per_row[:, D:]) + per_row[:, :D]).astype(BF)

    wide = matdot(weight_t[...], mixed_out[...], 1, 1) + bias[...]
    cosine, sine = cos_t[...], sin_t[...]
    half = HEAD_DIM // 2
    width = qt_out.shape[0]

    def turned(base):
        parts = []
        for at in range(base, base + width, HEAD_DIM):
            first, second = wide[at : at + half], wide[at + half : at + HEAD_DIM]
            parts.append(first * cosine - second * sine)
            parts.append(second * cosine + first * sine)
        return jnp.concatenate(parts, 0)

    keys = turned(width)
    values = wide[2 * width :]
    qt_out[...] = turned(0).astype(BF) * jnp.asarray(HEAD_DIM**-0.5, BF)
    kt_out[...] = keys.astype(BF)
    vt_out[...] = values.astype(BF)
    k_out[...] = keys.T.astype(BF)
    v_out[...] = values.T.astype(BF)


def project(place, blocks, mod_all, mod_long, member, weight_t, bias, cos_t, sin_t):
    block = blocks[0].shape[0]
    total = 4 * block
    width = weight_t.shape[0] // 3
    whole = lambda a: pl.BlockSpec(a.shape, lambda i: (0, 0))
    rows = lambda n: pl.BlockSpec((TILE, n), lambda i: (i, 0))
    cols = lambda n: pl.BlockSpec((n, TILE), lambda i: (0, i))
    return pl.pallas_call(
        project_kernel,
        grid=(total // TILE,),
        out_shape=[
            jax.ShapeDtypeStruct((total, D), BF),
            jax.ShapeDtypeStruct((width, total), BF),
            jax.ShapeDtypeStruct((width, total), BF),
            jax.ShapeDtypeStruct((width, total), BF),
            jax.ShapeDtypeStruct((total, width), BF),
            jax.ShapeDtypeStruct((total, width), BF),
        ],
        in_specs=[pl.BlockSpec(memory_space=SMEM)]
        + [whole(a) for a in blocks]
        + [whole(mod_all), whole(mod_long), whole(member), whole(weight_t), whole(bias)]
        + [cols(HEAD_DIM // 2), cols(HEAD_DIM // 2)],
        out_specs=[rows(D), cols(width), cols(width), cols(width), rows(width), rows(width)],
        scratch_shapes=[VMEM((total + TILE, D), BF), VMEM((TILE, 2 * TILE), BF)],
        compiler_params=pltpu.CompilerParams(vmem_limit_bytes=LIMIT),
        cost_estimate=pl.CostEstimate(
            flops=2 * total * D * 3 * width, bytes_accessed=16 << 20, transcendentals=total
        ),
        name="project",
    )(place, *blocks, mod_all, mod_long, member, weight_t, bias, cos_t, sin_t)


def one_head(pair, head):
    part = pair[head * HEAD_DIM : (head + 1) * HEAD_DIM]
    empty = jnp.zeros_like(part)
    return jnp.concatenate([part, empty] if head == 0 else [empty, part], 0)


def unroll(outs, rolled_ref, place, block):
    total = 4 * block
    rolled_ref[:, pl.ds(0, TILE)] = rolled_ref[:, pl.ds(total, TILE)]
    back = roll_matrix(TILE - place[1])
    for j, out in enumerate(outs):
        for part in range(block // TILE):
            at = pl.multiple_of((place[0] ^ j) * block + part * TILE, TILE)
            rows = matdot(back, rolled_ref[:, pl.ds(at, 2 * TILE)], 1, 1)
            out[part * TILE : (part + 1) * TILE, :] = rows.astype(BF)


def attend_kernel(
    place, qt, k, vt, seg_col, seg_row, ot_out, lse_out, o0, o1, o2, o3, rolled_ref
):
    step = pl.program_id(0)
    total = k.shape[0]
    block = total // 4
    last = step == total // TILE - 1

    def run(first, count, allowed):
        outs, tops = [], []
        for head in range(2):
            scores = matdot(k[pl.ds(first, count), :], one_head(qt[...], head), 1, 0)
            if allowed is not None:
                scores = jnp.where(allowed, scores, -1e30)
            top = jnp.max(scores, axis=0, keepdims=True)
            weights = jnp.exp(scores - top)
            exp_sum = jnp.sum(weights, axis=0, keepdims=True)
            mixed = matdot(
                vt[head * HEAD_DIM : (head + 1) * HEAD_DIM, pl.ds(first, count)],
                weights.astype(BF),
                1,
                0,
            )
            outs.append(mixed / exp_sum)
            tops.append(top + jnp.log(exp_sum))
        mixed = jnp.concatenate(outs, 0)
        low = mixed.astype(BF)
        ot_out[...] = low
        lse_out[...] = jnp.concatenate(tops * 4, 0)
        rolled_ref[:, pl.ds(pl.multiple_of(TILE + step * TILE, TILE), TILE)] = low

    @pl.when(jnp.logical_not(last))
    def _():
        run(0, LONGEST, None)

    @pl.when(last)
    def _():
        run(LONGEST, total - LONGEST, seg_col[...] == seg_row[...])
        unroll((o0, o1, o2, o3), rolled_ref, place, block)


def attend(place, pair, qt, k, vt, seg_col, seg_row):
    total = k.shape[0]
    block = total // 4
    whole = lambda a: pl.BlockSpec(a.shape, lambda i: (0, 0))
    return pl.pallas_call(
        attend_kernel,
        grid=(total // TILE,),
        out_shape=[
            jax.ShapeDtypeStruct((128, total), BF),
            jax.ShapeDtypeStruct((8, total), F32),
        ]
        + [jax.ShapeDtypeStruct((block, 128), BF)] * 4,
        in_specs=[
            pl.BlockSpec(memory_space=SMEM),
            pl.BlockSpec((128, TILE), lambda i: (pair, i)),
            pl.BlockSpec((total, 128), lambda i: (0, pair)),
            pl.BlockSpec((128, total), lambda i: (pair, 0)),
            whole(seg_col),
            whole(seg_row),
        ],
        out_specs=[
            pl.BlockSpec((128, TILE), lambda i: (0, i)),
            pl.BlockSpec((8, TILE), lambda i: (0, i)),
        ]
        + [pl.BlockSpec((block, 128), lambda i: (0, 0))] * 4,
        scratch_shapes=[VMEM((128, total + TILE), BF)],
        compiler_params=pltpu.CompilerParams(vmem_limit_bytes=LIMIT),
        cost_estimate=pl.CostEstimate(
            flops=2 * 2 * 2 * total * LONGEST * 256,
            bytes_accessed=4 << 20,
            transcendentals=2 * total * LONGEST,
        ),
        name="attend",
    )(place, qt, k, vt, seg_col, seg_row)


def attend_back_kernel(
    place, qt, k, kt, v, ot, lse, g0, g1, g2, g3, seg_col, seg_row, cos_t, sin_t,
    rolled_out, bias_out, s0, s1, s2, s3,
    grad_rows, grad_t, row_dots, dqt, dkt, dvt, nat_ref,
):
    step = pl.program_id(0)
    total = k.shape[0]
    block = total // 4
    steps = total // TILE
    last = step == steps - 1
    half = HEAD_DIM // 2

    @pl.when(step == 0)
    def _():
        for j, source in enumerate((g0, g1, g2, g3)):
            at = pl.multiple_of((place[0] ^ j) * block, block)
            grad_rows[pl.ds(at, block), :] = source[...]
        grad_rows[pl.ds(total, TILE), :] = grad_rows[pl.ds(0, TILE), :]
        dkt[...] = jnp.zeros_like(dkt)
        dvt[...] = jnp.zeros_like(dvt)

        ahead = roll_matrix(place[1])

        def turn(i, carry):
            cols = pl.ds(pl.multiple_of(i * TILE, TILE), TILE)
            two = grad_rows[pl.ds(pl.multiple_of(i * TILE, TILE), 2 * TILE), :]
            part = matdot(ahead, two, 1, 0).T
            grad_t[:, cols] = part.astype(BF)
            crossed = part * ot[:, cols].astype(F32)
            row_dots[0:1, cols] = jnp.sum(crossed[:HEAD_DIM], axis=0, keepdims=True)
            row_dots[1:2, cols] = jnp.sum(crossed[HEAD_DIM:], axis=0, keepdims=True)
            return carry

        lax.fori_loop(0, steps, turn, 0)

    here = pl.ds(pl.multiple_of(step * TILE, TILE), TILE)

    def run(first, count, allowed):
        keys = pl.ds(first, count)
        for head in range(2):
            mine = slice(head * HEAD_DIM, (head + 1) * HEAD_DIM)
            scores = matdot(k[keys, :], one_head(qt[:, here], head), 1, 0)
            if allowed is not None:
                scores = jnp.where(allowed, scores, -1e30)
            probs = jnp.exp(scores - lse[head : head + 1, here])
            grad_probs = matdot(v[keys, :], one_head(grad_t[:, here], head), 1, 0)
            grad_scores = (probs * (grad_probs - row_dots[head : head + 1, here])).astype(BF)
            dqt[mine, here] = matdot(kt[mine, keys], grad_scores, 1, 0) * HEAD_DIM**-0.5
            dkt[mine, keys] += matdot(qt[mine, here], grad_scores, 1, 1)
            dvt[mine, keys] += matdot(grad_t[mine, here], probs.astype(BF), 1, 1)

    @pl.when(jnp.logical_not(last))
    def _():
        run(0, LONGEST, None)

    @pl.when(last)
    def _():
        run(LONGEST, total - LONGEST, seg_col[...] == seg_row[...])

        def finish(i, sums):
            cols = pl.ds(pl.multiple_of(i * TILE, TILE), TILE)
            cosine, sine = cos_t[:, cols], sin_t[:, cols]

            def turned(ref):
                parts = []
                for at in range(0, 128, HEAD_DIM):
                    first, second = ref[at : at + half, cols], ref[at + half : at + HEAD_DIM, cols]
                    parts.append(first * cosine + second * sine)
                    parts.append(second * cosine - first * sine)
                return jnp.concatenate(parts, 0)

            columns = jnp.concatenate([turned(dqt), turned(dkt), dvt[:, cols]], 0)
            nat_ref[:, pl.ds(pl.multiple_of(TILE + i * TILE, TILE), TILE)] = columns.astype(BF)
            low = columns.T.astype(BF)
            rolled_out[cols, :] = low
            return sums + jnp.sum(low.astype(F32), axis=0, keepdims=True)

        sums = lax.fori_loop(0, steps, finish, jnp.zeros((1, 384), F32))
        bias_out[...] = jnp.broadcast_to(sums, bias_out.shape)
        unroll((s0, s1, s2, s3), nat_ref, place, block)


def attend_back(place, pair, qt, k, kt, v, ot, lse, grads, seg_col, seg_row, cos_t, sin_t):
    total = k.shape[0]
    block = total // 4
    whole = lambda a: pl.BlockSpec(a.shape, lambda i: (0, 0))
    wide = pl.BlockSpec((128, total), lambda i: (pair, 0))
    tall = pl.BlockSpec((total, 128), lambda i: (0, pair))
    return pl.pallas_call(
        attend_back_kernel,
        grid=(total // TILE,),
        out_shape=[
            jax.ShapeDtypeStruct((total, 384), BF),
            jax.ShapeDtypeStruct((8, 384), F32),
        ]
        + [jax.ShapeDtypeStruct((block, 384), BF)] * 4,
        in_specs=[
            pl.BlockSpec(memory_space=SMEM),
            wide,
            tall,
            wide,
            tall,
            whole(ot),
            whole(lse),
        ]
        + [whole(g) for g in grads]
        + [whole(seg_col), whole(seg_row), whole(cos_t), whole(sin_t)],
        out_specs=[
            pl.BlockSpec((total, 384), lambda i: (0, 0)),
            pl.BlockSpec((8, 384), lambda i: (0, 0)),
        ]
        + [pl.BlockSpec((block, 384), lambda i: (0, 0))] * 4,
        scratch_shapes=[
            VMEM((total + TILE, 128), BF),
            VMEM((128, total), BF),
            VMEM((8, total), F32),
            VMEM((128, total), F32),
            VMEM((128, total), F32),
            VMEM((128, total), F32),
            VMEM((384, total + TILE), BF),
        ],
        compiler_params=pltpu.CompilerParams(vmem_limit_bytes=LIMIT),
        cost_estimate=pl.CostEstimate(
            flops=2 * 2 * 5 * total * LONGEST * 256,
            bytes_accessed=8 << 20,
            transcendentals=2 * total * LONGEST,
        ),
        name="attend_back",
    )(place, qt, k, kt, v, ot, lse, *grads, seg_col, seg_row, cos_t, sin_t)


def weight_grad_kernel(place, o, h, a, e_att, e_z, e_b, out):
    out[0, :256] = contract_rows(o[...], e_att[...]).astype(BF)
    out[0, 256:512] = contract_rows(h[...], e_z[:, :D]).astype(BF)
    out[0, 512:768] = contract_rows(h[...], e_z[:, D:]).astype(BF)
    out[0, 768:] = contract_rows(a[...], e_b[...]).astype(BF)


def weight_grads(place, order, o, h, a, e_att, e_z, e_b):
    rows = o.shape[0]
    first, second = order
    pick = lambda i: first + i * (second - first)
    whole = lambda t: pl.BlockSpec(t.shape, lambda i, p: (0, 0))
    return pl.pallas_call(
        weight_grad_kernel,
        grid_spec=pltpu.PrefetchScalarGridSpec(
            num_scalar_prefetch=1,
            grid=(2,),
            in_specs=[
                pl.BlockSpec((rows, 256), lambda i, p: (0, pick(i))),
                pl.BlockSpec((rows, 256), lambda i, p: (0, p[0] ^ pick(i))),
                pl.BlockSpec((rows, 512), lambda i, p: (0, p[0] ^ pick(i))),
                whole(e_att),
                whole(e_z),
                whole(e_b),
            ],
            out_specs=pl.BlockSpec((1, 1280, D), lambda i, p: (i, 0, 0)),
        ),
        out_shape=jax.ShapeDtypeStruct((2, 1280, D), BF),
        compiler_params=pltpu.CompilerParams(vmem_limit_bytes=LIMIT),
        cost_estimate=pl.CostEstimate(
            flops=2 * 2 * rows * 1280 * D, bytes_accessed=12 << 20, transcendentals=0
        ),
        name="weight_grads",
    )(place, o, h, a, e_att, e_z, e_b)


def local(
    frames, time_embed, lengths, mod_weight, mod_bias, query_weight, query_bias, key_weight, key_bias,
    value_weight, value_bias, out_weight, out_bias, up_weight, up_bias, down_weight, down_bias, cotangent,
):
    n_grp = lax.axis_size("grp")
    row_count = frames.shape[0]
    my_row = lax.axis_index("row")
    group_rows = row_count * lax.axis_size("row")
    width = D // 4

    from_core = exchange(frames, "row", 1)
    from_x = exchange(frames, "row", 2)
    from_both = exchange(from_x, "row", 1)

    utt_sizes = lengths[0]
    finish = jnp.cumsum(utt_sizes)
    starts = finish - utt_sizes
    longest = jnp.argmax(utt_sizes)
    offset = starts[longest]
    place = jnp.stack([my_row, offset]).astype(jnp.int32)
    utts = jnp.arange(utt_sizes.shape[0], dtype=jnp.int32)

    def layout(rows):
        segment = jnp.sum((rows[:, None] >= finish[None, :]).astype(jnp.int32), axis=1)
        is_member = segment[:, None] == utts[None, :]
        position = rows - jnp.sum(jnp.where(is_member, starts[None, :], 0), axis=1)
        return segment, is_member.astype(F32), position

    rolled_rows = (jnp.arange(group_rows, dtype=jnp.int32) + offset) % group_rows
    segment, member_rolled, position = layout(rolled_rows)
    half = HEAD_DIM // 2
    frequency = jnp.exp(jnp.arange(half, dtype=F32) * (-2.0 * math.log(10000.0) / HEAD_DIM))
    angles = frequency[:, None] * position.astype(F32)[None, :]
    cos_t, sin_t = jnp.cos(angles), jnp.sin(angles)
    seg_tail = segment[LONGEST:]
    seg_col, seg_row = seg_tail[:, None], seg_tail[None, :]
    own_rows = my_row * row_count + jnp.arange(row_count, dtype=jnp.int32)
    _, member, _ = layout(own_rows)

    col_part = lambda w, j: lax.dynamic_slice_in_dim(w, (my_row ^ j) * width, width, 1)
    q_parts, k_parts, v_parts = (
        [col_part(w, j) for j in range(4)] for w in (query_weight, key_weight, value_weight)
    )
    weight_t = jnp.concatenate([q_parts[0].T, k_parts[0].T, v_parts[0].T], 0)
    own_part = lambda b: lax.dynamic_slice_in_dim(b, my_row * width, width, 0)
    bias_t = jnp.concatenate([own_part(query_bias), own_part(key_bias), own_part(value_bias)])[:, None]
    back_weight = jnp.concatenate(
        [
            part[j][:, pair * 128 : (pair + 1) * 128]
            for pair in range(2)
            for j in range(4)
            for part in (q_parts, k_parts, v_parts)
        ],
        1,
    )
    out_perm = jnp.concatenate(
        [lax.dynamic_slice_in_dim(out_weight, (my_row ^ j) * width, width, 0) for j in range(4)], 0
    )

    embedding = time_embed[0]
    act_low = jax.nn.silu(embedding).astype(BF)
    modulation = jnp.dot(act_low, mod_weight, preferred_element_type=F32) + mod_bias
    mod_long = lax.dynamic_slice_in_dim(modulation[:, : 2 * D], longest, 1, 0)
    act_all = act_low
    for bit in bits_of(n_grp):
        act_all = jnp.concatenate([act_all, exchange(act_all, "grp", bit)], 0)

    mixed, qt, kt, vt, k_rows, v_rows = project(
        place, (frames, from_core, from_x, from_both), modulation[:, : 2 * D], mod_long,
        member_rolled[LONGEST:], weight_t, bias_t, cos_t, sin_t,
    )

    heads_t, log_totals, pieces = [], [], []
    for pair in range(2):
        ot, lse, *outs = attend(place, pair, qt, k_rows, vt, seg_col, seg_row)
        heads_t.append(ot)
        log_totals.append(lse)
        pieces.append([outs[0]] + [exchange(outs[j], "row", j) for j in range(1, 4)])
    attn_low = jnp.concatenate([pieces[pair][j] for j in range(4) for pair in range(2)], 1)

    per_token = jnp.dot(member, modulation, precision=highest, preferred_element_type=F32)
    shift_attn, scale_attn, gate_attn, shift_ffn, scale_ffn, gate_ffn = jnp.split(per_token, 6, axis=1)
    residual = frames.astype(F32)
    normed_attn, factor_attn = normalize(residual)
    attended = jnp.dot(attn_low, out_perm, preferred_element_type=F32) + out_bias
    middle = residual + gate_attn * attended
    normed_ffn, factor_ffn = normalize(middle)
    ffn_in = (normed_ffn * (1.0 + scale_ffn) + shift_ffn).astype(BF)
    hidden = jnp.dot(ffn_in, up_weight, preferred_element_type=F32) + up_bias
    active_low = jax.nn.gelu(hidden, approximate=True).astype(BF)
    branch = jnp.dot(active_low, down_weight, preferred_element_type=F32) + down_bias
    output = (middle + gate_ffn * branch).astype(BF)
    upstream = cotangent.astype(F32)
    grad_branch = (upstream * gate_ffn).astype(BF)
    grad_gate_ffn = upstream * branch
    grad_active = against(grad_branch, down_weight)
    _, gelu_pull = jax.vjp(lambda tensor: jax.nn.gelu(tensor, approximate=True), hidden)
    grad_hidden = gelu_pull(grad_active)[0].astype(BF)
    grad_ffn_in = against(grad_hidden, up_weight)
    grad_scale_ffn = grad_ffn_in * normed_ffn
    grad_middle = upstream + normalize_back(grad_ffn_in * (1.0 + scale_ffn), normed_ffn, factor_ffn)
    grad_attended = (grad_middle * gate_attn).astype(BF)
    grad_gate_attn = grad_middle * attended
    grad_heads = against(grad_attended, out_perm).astype(BF)

    grad_pieces = []
    for pair in range(2):
        cut = [
            grad_heads[:, j * width + pair * 128 : j * width + pair * 128 + 128] for j in range(4)
        ]
        grad_pieces.append([cut[0]] + [exchange(cut[j], "row", j) for j in range(1, 4)])

    operands = (attn_low, ffn_in, active_low, grad_attended, grad_hidden, grad_branch)
    to_core = exchange(weight_grads(place, (1, 3), *operands), "row", 1)
    packed = add_low(weight_grads(place, (0, 2), *operands), to_core)
    cut_row = packed.shape[1] // 2
    upper = add_low(packed[0, :cut_row], exchange(packed[1, :cut_row], "row", 2))
    lower = packed[:, cut_row:]
    for bit in bits_of(n_grp):
        upper = halve(upper, 0, bit)
        lower = halve(lower, 1, bit)
    lower = add_low(lower[0], exchange(lower[1], "row", 2))
    for bit in reversed(bits_of(n_grp)):
        upper = grow(upper, 0, bit)
        lower = grow(lower, 0, bit)
    packed_total = jnp.concatenate([upper, lower], 0).astype(F32)
    out_grad = packed_total[:256]
    up_grad = jnp.concatenate([packed_total[256:512], packed_total[512:768]], 1)
    down_grad = packed_total[768:]

    back_pieces, qkv_grads, qkv_bias = [], [], []
    for pair in range(2):
        rolled, sums, *outs = attend_back(
            place, pair, qt, k_rows, kt, v_rows, heads_t[pair], log_totals[pair], grad_pieces[pair],
            seg_col, seg_row, cos_t, sin_t,
        )
        back_pieces += [outs[0]] + [exchange(outs[j], "row", j) for j in range(1, 4)]
        qkv_bias.append(sums[0].reshape(3, 128))
        total = contract_rows(mixed, rolled).astype(BF).reshape(4, width, 384)
        for bit in bits_of(n_grp):
            total = halve(total, 1, bit)
        shard = lambda j: lax.dynamic_index_in_dim(total, my_row ^ j, 0, keepdims=False)
        total = jnp.stack([shard(0)] + [exchange(shard(j), "row", j) for j in range(1, 4)])
        for bit in reversed(bits_of(n_grp)):
            total = grow(total, 1, bit)
        qkv_grads.append(total)
    by_owner = jnp.stack(qkv_grads)[:, my_row ^ jnp.arange(4)]
    qkv_full = by_owner.transpose(2, 1, 0, 3).reshape(width, 4, 2, 3, 128).astype(F32)
    query_grad, key_grad, value_grad = (qkv_full[:, :, :, i].reshape(width, D) for i in range(3))

    grad_mixed_in = against(jnp.concatenate(back_pieces, 1), back_weight)
    grad_frames = grad_middle + normalize_back(
        grad_mixed_in * (1.0 + scale_attn), normed_attn, factor_attn
    )

    def by_utterance(parts):
        return lax.dot_general(
            member,
            jnp.concatenate(parts, 1),
            (((0,), (0,)), ((), ())),
            precision=highest,
            preferred_element_type=F32,
        )

    def group_sum(tensor):
        for bit in (1, 2):
            tensor = tensor + exchange(tensor, "row", bit)
        return tensor

    late = group_sum(by_utterance([grad_mixed_in, grad_mixed_in * normed_attn]))
    early = group_sum(
        by_utterance([grad_gate_attn, grad_ffn_in, grad_scale_ffn, grad_gate_ffn])
    )
    grad_modulation = jnp.concatenate([late, early], 1).astype(BF)
    grad_activated = against(grad_modulation, mod_weight)
    _, silu_pull = jax.vjp(jax.nn.silu, embedding)
    grad_embedding = silu_pull(grad_activated)[0]
    mod_all = grad_modulation
    for bit in bits_of(n_grp):
        mod_all = jnp.concatenate([mod_all, exchange(mod_all, "grp", bit)], 0)
    act_slice = lax.dynamic_slice_in_dim(act_all, my_row * width, width, 1)
    mod_weight_grad = contract_rows(act_slice, mod_all)
    mod_bias_grad = lax.dynamic_slice_in_dim(column_sum(mod_all), my_row * 6 * width, 6 * width, 0)

    ffn_bias = group_sum(
        jnp.concatenate([column_sum(grad_attended), column_sum(grad_hidden), column_sum(grad_branch)])
    )
    mine = lambda start, size: lax.dynamic_slice_in_dim(ffn_bias, start + my_row * size, size, 0)
    qkv_sum = jnp.stack(qkv_bias, 1).reshape(3 * width)
    biases = jnp.concatenate([qkv_sum, mine(0, width), mine(D, 2 * width), mine(3 * D, width)])
    for bit in bits_of(n_grp):
        biases = biases + exchange(biases, "grp", bit)
    query_b, key_b, value_b, out_b, up_b, down_b = jnp.split(
        biases, [width, 2 * width, 3 * width, 4 * width, 6 * width]
    )
    return (
        output,
        grad_frames.astype(BF),
        grad_embedding[None],
        mod_weight_grad,
        mod_bias_grad,
        query_grad,
        query_b,
        key_grad,
        key_b,
        value_grad,
        value_b,
        out_grad,
        out_b,
        up_grad,
        up_b,
        down_grad,
        down_b,
    )


def solution(mesh):
    placed = (
        (P(("grp", "row"), None), P("grp", None, None), P("grp", None))
        + (P(),) * 14
        + (P(("grp", "row"), None),)
    )
    return jax.shard_map(
        local,
        mesh=mesh,
        in_specs=placed,
        out_specs=(
            P(("grp", "row"), None),
            P(("grp", "row"), None),
            P("grp", None, None),
        )
        + (P("row", None), P("row")) * 7,
        check_vma=False,
    )
```

time: 1070 us -> 539 us (0.50)
  waiting for transfers between devices: 474 us -> 159 us
  matrix products: 318 us -> 67.4 us
  Pallas kernels: 0 us -> 126 us
  starting transfers between devices: 1.07 us -> 53.1 us
  other arithmetic: 99.1 us -> 49.4 us
  local copies, waits for them, and re-layouts: 106 us -> 68.5 us
  blocking collectives: 33 us -> 0 us
  between operations: 16.3 us -> 4.96 us
    dot_general x51 -> x15, matrix products: 318 us -> 67.4 us  [the longest x8 34.3 us: matdot(): lax.dot_general(left, right, (((left_dim,), (right_dim,)), ((), ())), pre...]
    reduce_scatter x8 -> x0, waiting for transfers between devices: 230 us -> none  [the longest x1 47.1 us: local(): lax.psum_scatter(contract_rows(reorder(ffn_in), grad_hidden).astype(jnp.b...]
    psum x1 -> x0, waiting for transfers between devices: 214 us -> none  [local(): lax.psum(mod_weight_part.astype(jnp.bfloat16), 'grp').astype(jnp.float32)]
    ppermute x0 -> x69, waiting for transfers between devices: none -> 159 us  [exchange(): return lax.ppermute(tensor, axis, [(i, i ^ bit) for i in range(size)])]
    pallas_call x0 -> x7, Pallas kernels: none -> 126 us  [the longest x2 54.5 us: attend_back(): pl.pallas_call(attend_back_kernel, grid=(total // TILE,), out_shape=[jax....]
    ppermute x0 -> x69, starting transfers between devices: none -> 53.1 us  [exchange(): return lax.ppermute(tensor, axis, [(i, i ^ bit) for i in range(size)])]
    reduce_sum x12 -> x5, other arithmetic: 45.8 us -> 4.81 us  [the longest x2 4 us: column_sum(): return jnp.sum(tensor.astype(F32), axis=0)]
    psum x2 -> x0, blocking collectives: 33 us -> none  [the longest x1 22.2 us: local(): lax.psum(mod_bias_part.astype(jnp.bfloat16), 'grp').astype(jnp.float32)]
  transfers between devices with their start and end apart: 11 -> 69, of which waited for: 9 -> 31; matrix products, arithmetic and copies ran while one was open for 16% -> 25% of each run, Pallas kernels for 0% -> 12%
where the time goes in v1:
time: 539 us; the launch traced here: 529 us
  waiting for transfers between devices  159 us (29%)
  Pallas kernels  126 us (23%)
  local copies, waits for them, and re-layouts  68.5 us (13%)
  matrix products  67.4 us (13%)
  starting transfers between devices  53.1 us (10%)
  other arithmetic  49.4 us (9%)
    ppermute x69, waiting for transfers between devices, exchange(): return lax.ppermute(tensor, axis, [(i, i ^ bit) for i in range(size)])  159 us
    pallas_call x2, Pallas kernels, attend_back(): pl.pallas_call(attend_back_kernel, grid=(total // TILE,), out_shape=[jax....  54.5 us
    ppermute x69, starting transfers between devices, exchange(): return lax.ppermute(tensor, axis, [(i, i ^ bit) for i in range(size)])  53.1 us
    unnamed x219, local copies, waits for them, and re-layouts  41.5 us
    pallas_call x2, Pallas kernels, attend(): pl.pallas_call(attend_kernel, grid=(total // TILE,), out_shape=[jax.Shape...  38.7 us
    dot_general x8, matrix products, matdot(): lax.dot_general(left, right, (((left_dim,), (right_dim,)), ((), ())), pre...  34.3 us
    pallas_call x1, Pallas kernels, project(): pl.pallas_call(project_kernel, grid=(total // TILE,), out_shape=[jax.Shap...  17 us
    pallas_call x2, Pallas kernels, weight_grads(): pl.pallas_call(weight_grad_kernel, grid_spec=pltpu.PrefetchScalarGridSpec...  16.2 us
  transfers between devices with their start and end apart: 69, of which 31 were waited for; matrix products, arithmetic and copies ran while one was open for 25% of the time, Pallas kernels for 12%

profile of v1, /device:TPU:0, one launch (start us, length us, event | category | flops | bytes accessed | tf_op | source)
XLA Modules:
  0.0 528.9 jit_solution(11298918869762688045)
XLA Ops:
  1.2 2.6 collective-permute-start.1
  13.5 2.7 constant_dynamic-slice_fusion.25
  22.7 6.3 %convolution_add_fusion = f32[4,6144]{1,0:T(4,128)S(1)} fusion(bf16[4,1024]{1,0:T(4,128)(2,1)S(1)} %fusion.54, bf16[1024,6144]{1,0:T(8,128)(2,1)} %param.21, f32[6144]{0:T(1024)S(1)} %copy-done.48), kind=kOutput, calls=%fused_computation.10 | convolution fusion | flops 50356224 | bytes 12713984 | tf_op jit(solution)/shard_map/dot_general | solution.py:502
  39.9 2.9 constant_dynamic-slice_fusion.35
  59.7 2.7 copy-done.49
  69.3 8.1 %fusion.39 = f32[512,6144]{1,0:T(8,128)} fusion(f32[4,6144]{1,0:T(4,128)S(1)} %convolution_add_fusion, s32[512]{0:T(512)S(1)} %convert_reduce_fusion.6), kind=kOutput, calls=%fused_computation.112 | convolution fusion | flops 150996992 | bytes 12683264 | tf_op jit(solution)/shard_map/dot_general | solution.py:521
  83.6 17.0 %project.1 = (bf16[2048,1024]{1,0:T(8,128)(2,1)}, bf16[256,2048]{1,0:T(8,128)(2,1)}, bf16[256,2048]{1,0:T(8,128)(2,1)}, bf16[256,2048]{1,0:T(8,128)(2,1)}, bf16[...) custom-call(s32[2]{0:T(128)} %pad_add_fusion.place, bf16[512,1024]{1,0:T(8,128)(2,1)} %x0.1, ...), custom_call_target="tpu_custom_call" | custom-call | flops 3221225472 | bytes 16777216 | tf_op jit(solution)/shard_map/project/pallas_call | solution.py:155
  100.7 19.3 %attend.3 = (bf16[128,2048]{1,0:T(8,128)(2,1)}, f32[8,2048]{1,0:T(8,128)}, bf16[512,128]{1,0:T(8,128)(2,1)}, bf16[512,128]{1,0:T(8,128)(2,1)}, bf16[512,128]{1,0:T(8,128)(2,1)}, /*index=5*/bf16[512,128]{1,0:T(8,128)(2,1)}) custom-call(s32[2]{0:T(128)} %pad_add_fusion.place, bf16[256,2048]{1,0:T(8,128)(2,1)} %get-tuple-element.49.qt, ...), custom_call_target="tpu_custom_call" | custom-call | flops 7516192768 | bytes 4194304 | tf_op jit(solution)/shard_map/attend/pallas_call | solution.py:242
  120.0 19.4 %attend.2 = (bf16[128,2048]{1,0:T(8,128)(2,1)}, f32[8,2048]{1,0:T(8,128)}, bf16[512,128]{1,0:T(8,128)(2,1)}, bf16[512,128]{1,0:T(8,128)(2,1)}, bf16[512,128]{1,0:T(8,128)(2,1)}, /*index=5*/bf16[512,128]{1,0:T(8,128)(2,1)}) custom-call(s32[2]{0:T(128)} %pad_add_fusion.place, bf16[256,2048]{1,0:T(8,128)(2,1)} %get-tuple-element.49.qt, ...), custom_call_target="tpu_custom_call" | custom-call | flops 7516192768 | bytes 4194304 | tf_op jit(solution)/shard_map/attend/pallas_call | solution.py:242
  146.4 5.6 %collective-permute-done.6 = bf16[512,128]{1,0:T(8,128)(2,1)S(1)} collective-permute-done((bf16[512,128]{1,0:T(8,128)(2,1)S(1)}, bf16[512,128]{1,0:T(8,128)(2,1)S(1)}, u32[]{:S(2)}, u32[]{:S(2)}) %collective-permute-start.6) | collective-permute-done | bytes 131104 | tf_op jit(solution)/shard_map/ppermute | solution.py:57
  153.6 4.5 fusion.74
  159.3 3.9 convert_reduce_fusion.2
  166.1 5.3 convert_reduce_fusion
  171.4 5.9 %fusion.70 = (f32[512]{0:T(512)S(1)}, f32[512]{0:T(512)S(1)}, f32[512,1024]{1,0:T(8,128)S(1)}) fusion(f32[512,6144]{1,0:T(8,128)} %fusion.39, f32[512]{0:T(512)S(1)} %add_rsqrt_fusion.1, f32[512,1024]{1,0:T(8,128)S(1)} %get-tuple-element.142, f32[512]{0:T(512)S(1)} %broadcast_multiply_fusion.5, bf16[512,2048]{1,0:T(8,128)(2,1)S(1)} %get-tuple-element.138.e_z, ...), kind=kOutput, calls=%fused_computation.274 | convolution fusion | flops 2151152640 | bytes 12591104 | tf_op jit(solution)/shard_map/dot_general | solution.py:26
  177.4 7.5 %convert_reduce_fusion.3 = (f32[1024]{0:T(1024)S(1)}, bf16[512,1024]{1,0:T(8,128)(2,1)S(1)}, f32[512,1024]{1,0:T(8,128)S(1)}, bf16[512,1024]{1,0:T(8,128)(2,1)}, f32[512,1024]{1,0:T(8,128)}, /*index=5*/f32[512,1024]{1,0:T(8,128)}) fusion(f32[512,6144]{1,0:T(8,128)} %fusion.39, f32[512]{0:T(512)S(1)} %broadcast_multiply_fusion.3, ...), kind=kOutput, calls=%fused_computation.56 | convolution fusion | flops 2157968384 | bytes 26230784 | tf_op jit(solution)/shard_map/dot_general | solution.py:531
  187.2 8.3 %weight_grads.2 = bf16[2,1280,1024]{2,1,0:T(8,128)(2,1)} custom-call(s32[2]{0:T(128)} %pad_add_fusion.place, bf16[512,1024]{1,0:T(8,128)(2,1)} %copy-done.5, bf16[512,1024]{1,0:T(8,128)(2,1)} %copy-done.2, bf16[512,2048]{1,0:T(8,128)(2,1)} %copy-done, bf16[512,1024]{1,0:T(8,128)(2,1)} %copy-done.3, bf16[512,2048]{1,0:T(8,128)(2,1)} %copy-done.4, ...), custom_call_target="tpu_custom_call" | custom-call | flops 2684354560 | bytes 12582912 | tf_op jit(solution)/shard_map/weight_grads/pallas_call | solution.py:417
  198.1 7.9 %weight_grads.3 = bf16[2,1280,1024]{2,1,0:T(8,128)(2,1)} custom-call(s32[2]{0:T(128)} %pad_add_fusion.place, bf16[512,1024]{1,0:T(8,128)(2,1)} %copy-done.5, bf16[512,1024]{1,0:T(8,128)(2,1)} %copy-done.2, bf16[512,2048]{1,0:T(8,128)(2,1)} %copy-done, bf16[512,1024]{1,0:T(8,128)(2,1)} %copy-done.3, bf16[512,2048]{1,0:T(8,128)(2,1)} %copy-done.4, ...), custom_call_target="tpu_custom_call" | custom-call | flops 2684354560 | bytes 12582912 | tf_op jit(solution)/shard_map/weight_grads/pallas_call | solution.py:417
  209.6 5.6 %collective-permute-done.50 = f32[4096]{0:T(1024)S(1)} collective-permute-done((f32[4096]{0:T(1024)S(1)}, f32[4096]{0:T(1024)S(1)}, u32[]{:S(2)}, u32[]{:S(2)}) %collective-permute-start.50) | collective-permute-done | bytes 16416 | tf_op jit(solution)/shard_map/ppermute | solution.py:57
  217.1 27.1 %attend_back.2 = (bf16[2048,384]{1,0:T(8,128)(2,1)}, f32[8,384]{1,0:T(8,128)}, bf16[512,384]{1,0:T(8,128)(2,1)}, bf16[512,384]{1,0:T(8,128)(2,1)}, bf16[512,384]{1,0:T(8,128)(2,1)}, /*index=5*/bf16[512,384]{1,0:T(8,128)(2,1)}) custom-call(s32[2]{0:T(128)} %pad_add_fusion.place, bf16[256,2048]{1,0:T(8,128)(2,1)} %get-tuple-element.49.qt, ...), custom_call_target="tpu_custom_call" | custom-call | flops 18790481920 | bytes 8388608 | tf_op jit(solution)/shard_map/attend_back/pallas_call | solution.py:362
  245.7 27.3 %attend_back.3 = (bf16[2048,384]{1,0:T(8,128)(2,1)}, f32[8,384]{1,0:T(8,128)}, bf16[512,384]{1,0:T(8,128)(2,1)}, bf16[512,384]{1,0:T(8,128)(2,1)}, bf16[512,384]{1,0:T(8,128)(2,1)}, /*index=5*/bf16[512,384]{1,0:T(8,128)(2,1)}) custom-call(s32[2]{0:T(128)} %pad_add_fusion.place, bf16[256,2048]{1,0:T(8,128)(2,1)} %get-tuple-element.49.qt, ...), custom_call_target="tpu_custom_call" | custom-call | flops 18790481920 | bytes 8388608 | tf_op jit(solution)/shard_map/attend_back/pallas_call | solution.py:362
  275.9 5.2 convolution_convert_fusion.2
  287.4 2.6 collective-permute-start.53
  296.5 6.8 %collective-permute-done.14 = bf16[512,384]{1,0:T(8,128)(2,1)S(1)} collective-permute-done((bf16[512,384]{1,0:T(8,128)(2,1)S(1)}, bf16[512,384]{1,0:T(8,128)(2,1)S(1)}, u32[]{:S(2)}, u32[]{:S(2)}) %collective-permute-start.14) | collective-permute-done | bytes 393248 | tf_op jit(solution)/shard_map/ppermute | solution.py:57
  306.1 3.7 collective-permute-done.19
  310.0 9.3 %collective-permute-done.20 = bf16[512,384]{1,0:T(8,128)(2,1)S(1)} collective-permute-done((bf16[512,384]{1,0:T(8,128)(2,1)S(1)}, bf16[512,384]{1,0:T(8,128)(2,1)S(1)}, u32[]{:S(2)}, u32[]{:S(2)}) %collective-permute-start.20) | collective-permute-done | bytes 393248 | tf_op jit(solution)/shard_map/ppermute | solution.py:57
  319.4 5.5 %fusion.71 = (f32[512]{0:T(512)S(1)}, f32[512]{0:T(512)S(1)}, f32[512,1024]{1,0:T(8,128)S(1)}) fusion(f32[512,6144]{1,0:T(8,128)} %fusion.39, f32[512]{0:T(512)S(1)} %add_rsqrt_fusion, f32[512]{0:T(512)S(1)} %broadcast_multiply_fusion.1, bf16[512,1024]{1,0:T(8,128)(2,1)S(1)} %copy-done.11, bf16[512,3072]{1,0:T(8,128)(2,1)S(1)} %constant_dynamic-update-slice_fusion.8, ...), kind=kOutput, calls=%fused_computation.275 | convolution fusion | flops 3225418752 | bytes 14688256 | tf_op jit(solution)/shard_map/dot_general | solution.py:26
  325.0 3.6 fusion.22
  331.2 2.9 fusion
  338.4 3.0 collective-permute-done.24
  343.0 4.0 fusion.45
  349.3 2.6 collective-permute-start.42
  353.4 4.2 collective-permute-done.42
  357.7 5.2 add_convert_fusion
  366.6 21.7 %collective-permute-done.45 = bf16[32,384]{1,0:T(8,128)(2,1)S(1)} collective-permute-done((bf16[32,384]{1,0:T(8,128)(2,1)S(1)}, bf16[32,384]{1,0:T(8,128)(2,1)S(1)}, u32[]{:S(2)}, u32[]{:S(2)}) %collective-permute-start.45) | collective-permute-done | bytes 24608 | tf_op jit(solution)/shard_map/ppermute | solution.py:57
  397.2 14.7 %collective-permute-done.46 = bf16[4,32,384]{2,1,0:T(8,128)(2,1)S(1)} collective-permute-done((bf16[4,32,384]{2,1,0:T(8,128)(2,1)S(1)}, bf16[4,32,384]{2,1,0:T(8,128)(2,1)S(1)}, u32[]{:S(2)}, u32[]{:S(2)}) %collective-permute-start.46) | collective-permute-done | bytes 98336 | tf_op jit(solution)/shard_map/ppermute | solution.py:57
  412.0 7.3 %collective-permute-done.37 = bf16[4,32,384]{2,1,0:T(8,128)(2,1)S(1)} collective-permute-done((bf16[4,32,384]{2,1,0:T(8,128)(2,1)S(1)}, bf16[4,32,384]{2,1,0:T(8,128)(2,1)S(1)}, u32[]{:S(2)}, u32[]{:S(2)}) %collective-permute-start.37) | collective-permute-done | bytes 98336 | tf_op jit(solution)/shard_map/ppermute | solution.py:57
  421.4 3.8 fusion.49
  431.5 12.1 %collective-permute-done.56 = bf16[320,1024]{1,0:T(8,128)(2,1)S(1)} collective-permute-done((bf16[320,1024]{1,0:T(8,128)(2,1)S(1)}, bf16[320,1024]{1,0:T(8,128)(2,1)S(1)}, u32[]{:S(2)}, u32[]{:S(2)}) %collective-permute-start.56) | collective-permute-done | bytes 655392 | tf_op jit(solution)/shard_map/ppermute | solution.py:57
  446.4 8.8 %collective-permute-done.57 = bf16[160,1024]{1,0:T(8,128)(2,1)S(1)} collective-permute-done((bf16[160,1024]{1,0:T(8,128)(2,1)S(1)}, bf16[160,1024]{1,0:T(8,128)(2,1)S(1)}, u32[]{:S(2)}, u32[]{:S(2)}) %collective-permute-start.57) | collective-permute-done | bytes 327712 | tf_op jit(solution)/shard_map/ppermute | solution.py:57
  455.8 10.9 %collective-permute-done.64 = bf16[2,80,1024]{2,1,0:T(8,128)(2,1)S(1)} collective-permute-done((bf16[2,80,1024]{2,1,0:T(8,128)(2,1)S(1)}, bf16[2,80,1024]{2,1,0:T(8,128)(2,1)S(1)}, u32[]{:S(2)}, u32[]{:S(2)}) %collective-permute-start.64) | collective-permute-done | bytes 327712 | tf_op jit(solution)/shard_map/ppermute | solution.py:57
  468.6 3.6 collective-permute-done.65
  472.6 7.8 %collective-permute-done.59 = bf16[80,1024]{1,0:T(8,128)(2,1)S(1)} collective-permute-done((bf16[80,1024]{1,0:T(8,128)(2,1)S(1)}, bf16[80,1024]{1,0:T(8,128)(2,1)S(1)}, u32[]{:S(2)}, u32[]{:S(2)}) %collective-permute-start.59) | collective-permute-done | bytes 163872 | tf_op jit(solution)/shard_map/ppermute | solution.py:57
  484.9 7.3 %collective-permute-done.60 = bf16[160,1024]{1,0:T(8,128)(2,1)} collective-permute-done((bf16[160,1024]{1,0:T(8,128)(2,1)}, bf16[160,1024]{1,0:T(8,128)(2,1)}, u32[]{:S(2)}, u32[]{:S(2)}) %collective-permute-start.60) | collective-permute-done | bytes 327712 | tf_op jit(solution)/shard_map/ppermute | solution.py:57
  492.2 2.4 maximum_select_fusion.4
  494.8 2.4 collective-permute-done.67
  505.6 2.7 copy.114
  515.0 6.7 %collective-permute-done.68 = bf16[320,1024]{1,0:T(8,128)(2,1)} collective-permute-done((bf16[320,1024]{1,0:T(8,128)(2,1)}, bf16[320,1024]{1,0:T(8,128)(2,1)}, u32[]{:S(2)}, u32[]{:S(2)}) %collective-permute-start.68) | collective-permute-done | bytes 655392 | tf_op jit(solution)/shard_map/ppermute | solution.py:57
  521.7 2.5 maximum_select_fusion.1
  (465 shorter events, 161.0 us)
Async XLA Ops:
  0.7 82.0 %collective-permute-start = (bf16[512,1024]{1,0:T(8,128)(2,1)}, bf16[512,1024]{1,0:T(8,128)(2,1)}, u32[]{:S(2)}, u32[]{:S(2)}) collective-permute-start(bf16[512,1024]{1,0:T(8,128)(2,1)} %x0.1), channel_id=1, source_target_pairs={{0,1},{1,0},{2,3},{3,2},{4,5},{5,4},{6,7},{7,6},{8,9},{9,8},{10,11... | collective-permute-start | bytes 3145736 | tf_op jit(solution)/shard_map/ppermute | solution.py:57
  1.2 65.3 %collective-permute-start.1 = (bf16[512,1024]{1,0:T(8,128)(2,1)}, bf16[512,1024]{1,0:T(8,128)(2,1)}, u32[]{:S(2)}, u32[]{:S(2)}) collective-permute-start(bf16[512,1024]{1,0:T(8,128)(2,1)} %x0.1), channel_id=1, source_target_pairs={{0,2},{1,3},{2,0},{3,1},{4,6},{5,7},{6,4},{7,5},{8,10},{9,11},{10,... | collective-permute-start | bytes 3145736 | tf_op jit(solution)/shard_map/ppermute | solution.py:57
  4.5 72.9 %collective-permute-start.25 = (bf16[4,1024]{1,0:T(4,128)(2,1)S(1)}, bf16[4,1024]{1,0:T(4,128)(2,1)S(1)}, u32[]{:S(2)}, u32[]{:S(2)}) collective-permute-start(bf16[4,1024]{1,0:T(4,128)(2,1)S(1)} %fusion.54), channel_id=1, source_target_pairs={{0,4},{4,0},{8,12},{12,8},{16,20},{20,16},{24,28},{28,24},{1,5},{5... | collective-permute-start | bytes 24584 | tf_op jit(solution)/shard_map/ppermute | solution.py:57
  66.4 16.2 %collective-permute-start.2 = (bf16[512,1024]{1,0:T(8,128)(2,1)}, bf16[512,1024]{1,0:T(8,128)(2,1)S(1)}, u32[]{:S(2)}, u32[]{:S(2)}) collective-permute-start(bf16[512,1024]{1,0:T(8,128)(2,1)} %collective-permute-done.1.x2), channel_id=1, source_target_pairs={{0,1},{1,0},{2,3},{3,2},{4,5},{5,4},{6,7},{7,6},{8,9},{9,8},{10,11... | collective-permute-start | bytes 3145736 | tf_op jit(solution)/shard_map/ppermute | solution.py:57
  140.3 11.7 %collective-permute-start.7 = (bf16[512,128]{1,0:T(8,128)(2,1)}, bf16[512,128]{1,0:T(8,128)(2,1)S(1)}, u32[]{:S(2)}, u32[]{:S(2)}) collective-permute-start(bf16[512,128]{1,0:T(8,128)(2,1)} %get-tuple-element.58), channel_id=1, source_target_pairs={{0,3},{1,2},{2,1},{3,0},{4,7},{5,6},{6,5},{7,4},{8,11},{9,10},{10,... | collective-permute-start | bytes 393224 | tf_op jit(solution)/shard_map/ppermute | solution.py:57
  142.0 10.0 %collective-permute-start.6 = (bf16[512,128]{1,0:T(8,128)(2,1)S(1)}, bf16[512,128]{1,0:T(8,128)(2,1)S(1)}, u32[]{:S(2)}, u32[]{:S(2)}) collective-permute-start(bf16[512,128]{1,0:T(8,128)(2,1)S(1)} %copy-done.67), channel_id=1, source_target_pairs={{0,2},{1,3},{2,0},{3,1},{4,6},{5,7},{6,4},{7,5},{8,10},{9,11},{10,... | collective-permute-start | bytes 393224 | tf_op jit(solution)/shard_map/ppermute | solution.py:57
  143.5 10.0 %collective-permute-start.8 = (bf16[512,128]{1,0:T(8,128)(2,1)S(1)}, bf16[512,128]{1,0:T(8,128)(2,1)S(1)}, u32[]{:S(2)}, u32[]{:S(2)}) collective-permute-start(bf16[512,128]{1,0:T(8,128)(2,1)S(1)} %copy-done.63), channel_id=1, source_target_pairs={{0,3},{1,2},{2,1},{3,0},{4,7},{5,6},{6,5},{7,4},{8,11},{9,10},{10,... | collective-permute-start | bytes 393224 | tf_op jit(solution)/shard_map/ppermute | solution.py:57
  197.6 10.3 %collective-permute-start.49 = (f32[4096]{0:T(1024)S(1)}, f32[4096]{0:T(1024)S(1)}, u32[]{:S(2)}, u32[]{:S(2)}) collective-permute-start(f32[4096]{0:T(1024)S(1)} %pad_maximum_fusion.15), channel_id=1, source_target_pairs={{0,1},{1,0},{2,3},{3,2},{4,5},{5,4},{6,7},{7,6},{8,9},{9,8},{10,11... | collective-permute-start | bytes 49160 | tf_op jit(solution)/shard_map/ppermute | solution.py:57
  206.0 9.9 %collective-permute-start.11 = (bf16[512,128]{1,0:T(8,128)(2,1)S(1)}, bf16[512,128]{1,0:T(8,128)(2,1)S(1)}, u32[]{:S(2)}, u32[]{:S(2)}) collective-permute-start(bf16[512,128]{1,0:T(8,128)(2,1)S(1)} %get-tuple-element.184), channel_id=1, source_target_pairs={{0,3},{1,2},{2,1},{3,0},{4,7},{5,6},{6,5},{7,4},{8,11},{9,10},{10,... | collective-permute-start | bytes 393224 | tf_op jit(solution)/shard_map/ppermute | solution.py:57
  206.2 9.7 %collective-permute-start.10 = (bf16[512,128]{1,0:T(8,128)(2,1)S(1)}, bf16[512,128]{1,0:T(8,128)(2,1)S(1)}, u32[]{:S(2)}, u32[]{:S(2)}) collective-permute-start(bf16[512,128]{1,0:T(8,128)(2,1)S(1)} %get-tuple-element.185), channel_id=1, source_target_pairs={{0,2},{1,3},{2,0},{3,1},{4,6},{5,7},{6,4},{7,5},{8,10},{9,11},{10,... | collective-permute-start | bytes 393224 | tf_op jit(solution)/shard_map/ppermute | solution.py:57
  208.5 36.5 %collective-permute-start.17 = (bf16[512,128]{1,0:T(8,128)(2,1)S(1)}, bf16[512,128]{1,0:T(8,128)(2,1)S(1)}, u32[]{:S(2)}, u32[]{:S(2)}) collective-permute-start(bf16[512,128]{1,0:T(8,128)(2,1)S(1)} %get-tuple-element.180), channel_id=1, source_target_pairs={{0,3},{1,2},{2,1},{3,0},{4,7},{5,6},{6,5},{7,4},{8,11},{9,10},{10,... | collective-permute-start | bytes 393224 | tf_op jit(solution)/shard_map/ppermute | solution.py:57
  215.2 29.8 %collective-permute-start.16 = (bf16[512,128]{1,0:T(8,128)(2,1)S(1)}, bf16[512,128]{1,0:T(8,128)(2,1)S(1)}, u32[]{:S(2)}, u32[]{:S(2)}) collective-permute-start(bf16[512,128]{1,0:T(8,128)(2,1)S(1)} %get-tuple-element.181), channel_id=1, source_target_pairs={{0,2},{1,3},{2,0},{3,1},{4,6},{5,7},{6,4},{7,5},{8,10},{9,11},{10,... | collective-permute-start | bytes 393224 | tf_op jit(solution)/shard_map/ppermute | solution.py:57
  215.9 29.1 %collective-permute-start.15 = (bf16[512,128]{1,0:T(8,128)(2,1)S(1)}, bf16[512,128]{1,0:T(8,128)(2,1)S(1)}, u32[]{:S(2)}, u32[]{:S(2)}) collective-permute-start(bf16[512,128]{1,0:T(8,128)(2,1)S(1)} %get-tuple-element.182), channel_id=1, source_target_pairs={{0,1},{1,0},{2,3},{3,2},{4,5},{5,4},{6,7},{7,6},{8,9},{9,8},{10,11... | collective-permute-start | bytes 393224 | tf_op jit(solution)/shard_map/ppermute | solution.py:57
  216.0 141.7 %collective-permute-start.54 = (bf16[2,1280,1024]{2,1,0:T(8,128)(2,1)}, bf16[2,1280,1024]{2,1,0:T(8,128)(2,1)}, u32[]{:S(2)}, u32[]{:S(2)}) collective-permute-start(bf16[2,1280,1024]{2,1,0:T(8,128)(2,1)} %weight_grads.3), channel_id=1, source_target_pairs={{0,1},{1,0},{2,3},{3,2},{4,5},{5,4},{6,7},{7,6},{8,9},{9,8},{10,11... | collective-permute-start | bytes 15728648 | tf_op jit(solution)/shard_map/ppermute | solution.py:57
  273.8 9.8 %collective-permute-start.51 = (f32[1792]{0:T(1024)S(1)}, f32[1792]{0:T(1024)S(1)}, u32[]{:S(2)}, u32[]{:S(2)}) collective-permute-start(f32[1792]{0:T(1024)S(1)} %pad_maximum_fusion.16), channel_id=1, source_target_pairs={{0,4},{4,0},{8,12},{12,8},{16,20},{20,16},{24,28},{28,24},{1,5},{5... | collective-permute-start | bytes 21512 | tf_op jit(solution)/shard_map/ppermute | solution.py:57
  274.4 18.7 %collective-permute-start.12 = (bf16[512,384]{1,0:T(8,128)(2,1)S(1)}, bf16[512,384]{1,0:T(8,128)(2,1)S(1)}, u32[]{:S(2)}, u32[]{:S(2)}) collective-permute-start(bf16[512,384]{1,0:T(8,128)(2,1)S(1)} %copy-done.59), channel_id=1, source_target_pairs={{0,1},{1,0},{2,3},{3,2},{4,5},{5,4},{6,7},{7,6},{8,9},{9,8},{10,11... | collective-permute-start | bytes 1179656 | tf_op jit(solution)/shard_map/ppermute | solution.py:57
  274.4 21.9 %collective-permute-start.13 = (bf16[512,384]{1,0:T(8,128)(2,1)}, bf16[512,384]{1,0:T(8,128)(2,1)S(1)}, u32[]{:S(2)}, u32[]{:S(2)}) collective-permute-start(bf16[512,384]{1,0:T(8,128)(2,1)} %get-tuple-element.66), channel_id=1, source_target_pairs={{0,2},{1,3},{2,0},{3,1},{4,6},{5,7},{6,4},{7,5},{8,10},{9,11},{10,... | collective-permute-start | bytes 1179656 | tf_op jit(solution)/shard_map/ppermute | solution.py:57
  284.6 11.0 %collective-permute-start.40 = (bf16[4,128,384]{2,1,0:T(8,128)(2,1)S(1)}, bf16[4,128,384]{2,1,0:T(8,128)(2,1)S(1)}, u32[]{:S(2)}, u32[]{:S(2)}) collective-permute-start(bf16[4,128,384]{2,1,0:T(8,128)(2,1)S(1)} %constant_dynamic-slice_fusion.17), channel_id=1, source_target_pairs={{0,4},{4,0},{8,12},{12,8},{16,20},{20,16},{24,28},{28,24},{1,5},{5... | collective-permute-start | bytes 1179656 | tf_op jit(solution)/shard_map/ppermute | solution.py:57
  291.9 11.4 %collective-permute-start.14 = (bf16[512,384]{1,0:T(8,128)(2,1)S(1)}, bf16[512,384]{1,0:T(8,128)(2,1)S(1)}, u32[]{:S(2)}, u32[]{:S(2)}) collective-permute-start(bf16[512,384]{1,0:T(8,128)(2,1)S(1)} %copy-done.56), channel_id=1, source_target_pairs={{0,3},{1,2},{2,1},{3,0},{4,7},{5,6},{6,5},{7,4},{8,11},{9,10},{10,... | collective-permute-start | bytes 1179656 | tf_op jit(solution)/shard_map/ppermute | solution.py:57
  293.1 12.0 %collective-permute-start.18 = (bf16[512,384]{1,0:T(8,128)(2,1)S(1)}, bf16[512,384]{1,0:T(8,128)(2,1)S(1)}, u32[]{:S(2)}, u32[]{:S(2)}) collective-permute-start(bf16[512,384]{1,0:T(8,128)(2,1)S(1)} %copy-done.58), channel_id=1, source_target_pairs={{0,1},{1,0},{2,3},{3,2},{4,5},{5,4},{6,7},{7,6},{8,9},{9,8},{10,11... | collective-permute-start | bytes 1179656 | tf_op jit(solution)/shard_map/ppermute | solution.py:57
  295.7 14.2 %collective-permute-start.19 = (bf16[512,384]{1,0:T(8,128)(2,1)S(1)}, bf16[512,384]{1,0:T(8,128)(2,1)S(1)}, u32[]{:S(2)}, u32[]{:S(2)}) collective-permute-start(bf16[512,384]{1,0:T(8,128)(2,1)S(1)} %copy-done.57), channel_id=1, source_target_pairs={{0,2},{1,3},{2,0},{3,1},{4,6},{5,7},{6,4},{7,5},{8,10},{9,11},{10,... | collective-permute-start | bytes 1179656 | tf_op jit(solution)/shard_map/ppermute | solution.py:57
  296.3 22.9 %collective-permute-start.20 = (bf16[512,384]{1,0:T(8,128)(2,1)S(1)}, bf16[512,384]{1,0:T(8,128)(2,1)S(1)}, u32[]{:S(2)}, u32[]{:S(2)}) collective-permute-start(bf16[512,384]{1,0:T(8,128)(2,1)S(1)} %copy-done.55), channel_id=1, source_target_pairs={{0,3},{1,2},{2,1},{3,0},{4,7},{5,6},{6,5},{7,4},{8,11},{9,10},{10,... | collective-permute-start | bytes 1179656 | tf_op jit(solution)/shard_map/ppermute | solution.py:57
  303.3 30.9 %collective-permute-start.31 = (bf16[4,128,384]{2,1,0:T(8,128)(2,1)S(1)}, bf16[4,128,384]{2,1,0:T(8,128)(2,1)S(1)}, u32[]{:S(2)}, u32[]{:S(2)}) collective-permute-start(bf16[4,128,384]{2,1,0:T(8,128)(2,1)S(1)} %constant_dynamic-slice_fusion.21), channel_id=1, source_target_pairs={{0,4},{4,0},{8,12},{12,8},{16,20},{20,16},{24,28},{28,24},{1,5},{5... | collective-permute-start | bytes 1179656 | tf_op jit(solution)/shard_map/ppermute | solution.py:57
  305.1 43.2 %collective-permute-start.41 = (bf16[4,64,384]{2,1,0:T(8,128)(2,1)S(1)}, bf16[4,64,384]{2,1,0:T(8,128)(2,1)}, u32[]{:S(2)}, u32[]{:S(2)}) collective-permute-start(bf16[4,64,384]{2,1,0:T(8,128)(2,1)S(1)} %constant_dynamic-slice_fusion.16), channel_id=1, source_target_pairs={{0,8},{4,12},{8,0},{12,4},{16,24},{20,28},{24,16},{28,20},{1,9},{5... | collective-permute-start | bytes 589832 | tf_op jit(solution)/shard_map/ppermute | solution.py:57
  335.9 16.0 %collective-permute-start.32 = (bf16[4,64,384]{2,1,0:T(8,128)(2,1)S(1)}, bf16[4,64,384]{2,1,0:T(8,128)(2,1)}, u32[]{:S(2)}, u32[]{:S(2)}) collective-permute-start(bf16[4,64,384]{2,1,0:T(8,128)(2,1)S(1)} %constant_dynamic-slice_fusion.20), channel_id=1, source_target_pairs={{0,8},{4,12},{8,0},{12,4},{16,24},{20,28},{24,16},{28,20},{1,9},{5... | collective-permute-start | bytes 589832 | tf_op jit(solution)/shard_map/ppermute | solution.py:57
  352.9 13.1 %collective-permute-start.33 = (bf16[4,32,384]{2,1,0:T(8,128)(2,1)S(1)}, bf16[4,32,384]{2,1,0:T(8,128)(2,1)S(1)}, u32[]{:S(2)}, u32[]{:S(2)}) collective-permute-start(bf16[4,32,384]{2,1,0:T(8,128)(2,1)S(1)} %constant_dynamic-slice_fusion.19), channel_id=1, source_target_pairs={{0,16},{4,20},{8,24},{12,28},{16,0},{20,4},{24,8},{28,12},{1,17},{... | collective-permute-start | bytes 294920 | tf_op jit(solution)/shard_map/ppermute | solution.py:57
  363.0 62.3 %collective-permute-start.55 = (bf16[640,1024]{1,0:T(8,128)(2,1)S(1)}, bf16[640,1024]{1,0:T(8,128)(2,1)S(1)}, u32[]{:S(2)}, u32[]{:S(2)}) collective-permute-start(bf16[640,1024]{1,0:T(8,128)(2,1)S(1)} %slice_bitcast_fusion), channel_id=1, source_target_pairs={{0,2},{1,3},{2,0},{3,1},{4,6},{5,7},{6,4},{7,5},{8,10},{9,11},{10,... | collective-permute-start | bytes 3932168 | tf_op jit(solution)/shard_map/ppermute | solution.py:57
  363.5 24.8 %collective-permute-start.45 = (bf16[32,384]{1,0:T(8,128)(2,1)S(1)}, bf16[32,384]{1,0:T(8,128)(2,1)S(1)}, u32[]{:S(2)}, u32[]{:S(2)}) collective-permute-start(bf16[32,384]{1,0:T(8,128)(2,1)S(1)} %get-tuple-element.193), channel_id=1, source_target_pairs={{0,3},{1,2},{2,1},{3,0},{4,7},{5,6},{6,5},{7,4},{8,11},{9,10},{10,... | collective-permute-start | bytes 73736 | tf_op jit(solution)/shard_map/ppermute | solution.py:57
  363.6 26.9 %collective-permute-start.44 = (bf16[32,384]{1,0:T(8,128)(2,1)S(1)}, bf16[32,384]{1,0:T(8,128)(2,1)S(1)}, u32[]{:S(2)}, u32[]{:S(2)}) collective-permute-start(bf16[32,384]{1,0:T(8,128)(2,1)S(1)} %get-tuple-element.194), channel_id=1, source_target_pairs={{0,2},{1,3},{2,0},{3,1},{4,6},{5,7},{6,4},{7,5},{8,10},{9,11},{10,... | collective-permute-start | bytes 73736 | tf_op jit(solution)/shard_map/ppermute | solution.py:57
  365.2 26.7 %collective-permute-start.43 = (bf16[32,384]{1,0:T(8,128)(2,1)S(1)}, bf16[32,384]{1,0:T(8,128)(2,1)S(1)}, u32[]{:S(2)}, u32[]{:S(2)}) collective-permute-start(bf16[32,384]{1,0:T(8,128)(2,1)S(1)} %get-tuple-element.195), channel_id=1, source_target_pairs={{0,1},{1,0},{2,3},{3,2},{4,5},{5,4},{6,7},{7,6},{8,9},{9,8},{10,11... | collective-permute-start | bytes 73736 | tf_op jit(solution)/shard_map/ppermute | solution.py:57
  366.0 60.3 %collective-permute-start.62 = (bf16[2,320,1024]{2,1,0:T(8,128)(2,1)S(1)}, bf16[2,320,1024]{2,1,0:T(8,128)(2,1)S(1)}, u32[]{:S(2)}, u32[]{:S(2)}) collective-permute-start(bf16[2,320,1024]{2,1,0:T(8,128)(2,1)S(1)} %constant_dynamic-slice_fusion.10), channel_id=1, source_target_pairs={{0,4},{4,0},{8,12},{12,8},{16,20},{20,16},{24,28},{28,24},{1,5},{5... | collective-permute-start | bytes 3932168 | tf_op jit(solution)/shard_map/ppermute | solution.py:57
  392.0 27.3 %collective-permute-start.27 = (bf16[16,1024]{1,0:T(8,128)(2,1)S(1)}, bf16[16,1024]{1,0:T(8,128)(2,1)S(1)}, u32[]{:S(2)}, u32[]{:S(2)}) collective-permute-start(bf16[16,1024]{1,0:T(8,128)(2,1)S(1)} %copy-done.47), channel_id=1, source_target_pairs={{0,16},{4,20},{8,24},{12,28},{16,0},{20,4},{24,8},{28,12},{1,17},{... | collective-permute-start | bytes 98312 | tf_op jit(solution)/shard_map/ppermute | solution.py:57
  394.3 27.1 %collective-permute-start.30 = (bf16[16,6144]{1,0:T(8,128)(2,1)S(1)}, bf16[16,6144]{1,0:T(8,128)(2,1)S(1)}, u32[]{:S(2)}, u32[]{:S(2)}) collective-permute-start(bf16[16,6144]{1,0:T(8,128)(2,1)S(1)} %pad_maximum_fusion.8), channel_id=1, source_target_pairs={{0,16},{4,20},{8,24},{12,28},{16,0},{20,4},{24,8},{28,12},{1,17},{... | collective-permute-start | bytes 589832 | tf_op jit(solution)/shard_map/ppermute | solution.py:57
  395.9 16.0 %collective-permute-start.46 = (bf16[4,32,384]{2,1,0:T(8,128)(2,1)S(1)}, bf16[4,32,384]{2,1,0:T(8,128)(2,1)S(1)}, u32[]{:S(2)}, u32[]{:S(2)}) collective-permute-start(bf16[4,32,384]{2,1,0:T(8,128)(2,1)S(1)} %pad_maximum_fusion.11), channel_id=1, source_target_pairs={{0,16},{4,20},{8,24},{12,28},{16,0},{20,4},{24,8},{28,12},{1,17},{... | collective-permute-start | bytes 294920 | tf_op jit(solution)/shard_map/ppermute | solution.py:57
  419.3 11.9 %collective-permute-start.38 = (bf16[4,64,384]{2,1,0:T(8,128)(2,1)S(1)}, bf16[4,64,384]{2,1,0:T(8,128)(2,1)S(1)}, u32[]{:S(2)}, u32[]{:S(2)}) collective-permute-start(bf16[4,64,384]{2,1,0:T(8,128)(2,1)S(1)} %maximum_select_fusion.10), channel_id=1, source_target_pairs={{0,8},{4,12},{8,0},{12,4},{16,24},{20,28},{24,16},{28,20},{1,9},{5... | collective-permute-start | bytes 589832 | tf_op jit(solution)/shard_map/ppermute | solution.py:57
  425.8 17.7 %collective-permute-start.56 = (bf16[320,1024]{1,0:T(8,128)(2,1)S(1)}, bf16[320,1024]{1,0:T(8,128)(2,1)S(1)}, u32[]{:S(2)}, u32[]{:S(2)}) collective-permute-start(bf16[320,1024]{1,0:T(8,128)(2,1)S(1)} %constant_dynamic-slice_fusion.13), channel_id=1, source_target_pairs={{0,4},{4,0},{8,12},{12,8},{16,20},{20,16},{24,28},{28,24},{1,5},{5... | collective-permute-start | bytes 1966088 | tf_op jit(solution)/shard_map/ppermute | solution.py:57
  427.0 18.2 %collective-permute-start.63 = (bf16[2,160,1024]{2,1,0:T(8,128)(2,1)S(1)}, bf16[2,160,1024]{2,1,0:T(8,128)(2,1)S(1)}, u32[]{:S(2)}, u32[]{:S(2)}) collective-permute-start(bf16[2,160,1024]{2,1,0:T(8,128)(2,1)S(1)} %constant_dynamic-slice_fusion.9), channel_id=1, source_target_pairs={{0,8},{4,12},{8,0},{12,4},{16,24},{20,28},{24,16},{28,20},{1,9},{5... | collective-permute-start | bytes 1966088 | tf_op jit(solution)/shard_map/ppermute | solution.py:57
  428.0 44.3 %collective-permute-start.48 = (bf16[4,128,384]{2,1,0:T(8,128)(2,1)S(1)}, bf16[4,128,384]{2,1,0:T(8,128)(2,1)S(1)}, u32[]{:S(2)}, u32[]{:S(2)}) collective-permute-start(bf16[4,128,384]{2,1,0:T(8,128)(2,1)S(1)} %maximum_select_fusion.7), channel_id=1, source_target_pairs={{0,4},{4,0},{8,12},{12,8},{16,20},{20,16},{24,28},{28,24},{1,5},{5... | collective-permute-start | bytes 1179656 | tf_op jit(solution)/shard_map/ppermute | solution.py:57
  431.4 52.0 %collective-permute-start.39 = (bf16[4,128,384]{2,1,0:T(8,128)(2,1)S(1)}, bf16[4,128,384]{2,1,0:T(8,128)(2,1)S(1)}, u32[]{:S(2)}, u32[]{:S(2)}) collective-permute-start(bf16[4,128,384]{2,1,0:T(8,128)(2,1)S(1)} %maximum_select_fusion.6), channel_id=1, source_target_pairs={{0,4},{4,0},{8,12},{12,8},{16,20},{20,16},{24,28},{28,24},{1,5},{5... | collective-permute-start | bytes 1179656 | tf_op jit(solution)/shard_map/ppermute | solution.py:57
  443.8 11.4 %collective-permute-start.57 = (bf16[160,1024]{1,0:T(8,128)(2,1)S(1)}, bf16[160,1024]{1,0:T(8,128)(2,1)S(1)}, u32[]{:S(2)}, u32[]{:S(2)}) collective-permute-start(bf16[160,1024]{1,0:T(8,128)(2,1)S(1)} %constant_dynamic-slice_fusion.12), channel_id=1, source_target_pairs={{0,8},{4,12},{8,0},{12,4},{16,24},{20,28},{24,16},{28,20},{1,9},{5... | collective-permute-start | bytes 983048 | tf_op jit(solution)/shard_map/ppermute | solution.py:57
  445.5 21.2 %collective-permute-start.64 = (bf16[2,80,1024]{2,1,0:T(8,128)(2,1)S(1)}, bf16[2,80,1024]{2,1,0:T(8,128)(2,1)S(1)}, u32[]{:S(2)}, u32[]{:S(2)}) collective-permute-start(bf16[2,80,1024]{2,1,0:T(8,128)(2,1)S(1)} %constant_dynamic-slice_fusion.8), channel_id=1, source_target_pairs={{0,16},{4,20},{8,24},{12,28},{16,0},{20,4},{24,8},{28,12},{1,17},{... | collective-permute-start | bytes 983048 | tf_op jit(solution)/shard_map/ppermute | solution.py:57
  455.3 13.1 %collective-permute-start.58 = (bf16[80,1024]{1,0:T(8,128)(2,1)S(1)}, bf16[80,1024]{1,0:T(8,128)(2,1)S(1)}, u32[]{:S(2)}, u32[]{:S(2)}) collective-permute-start(bf16[80,1024]{1,0:T(8,128)(2,1)S(1)} %constant_dynamic-slice_fusion.11), channel_id=1, source_target_pairs={{0,16},{4,20},{8,24},{12,28},{16,0},{20,4},{24,8},{28,12},{1,17},{... | collective-permute-start | bytes 491528 | tf_op jit(solution)/shard_map/ppermute | solution.py:57
  468.5 11.9 %collective-permute-start.59 = (bf16[80,1024]{1,0:T(8,128)(2,1)S(1)}, bf16[80,1024]{1,0:T(8,128)(2,1)S(1)}, u32[]{:S(2)}, u32[]{:S(2)}) collective-permute-start(bf16[80,1024]{1,0:T(8,128)(2,1)S(1)} %add_convert_fusion.11), channel_id=1, source_target_pairs={{0,16},{4,20},{8,24},{12,28},{16,0},{20,4},{24,8},{28,12},{1,17},{... | collective-permute-start | bytes 491528 | tf_op jit(solution)/shard_map/ppermute | solution.py:57
  472.3 10.9 %collective-permute-start.66 = (bf16[80,1024]{1,0:T(8,128)(2,1)S(1)}, bf16[80,1024]{1,0:T(8,128)(2,1)S(1)}, u32[]{:S(2)}, u32[]{:S(2)}) collective-permute-start(bf16[80,1024]{1,0:T(8,128)(2,1)S(1)} %fusion.38), channel_id=1, source_target_pairs={{0,16},{4,20},{8,24},{12,28},{16,0},{20,4},{24,8},{28,12},{1,17},{... | collective-permute-start | bytes 491528 | tf_op jit(solution)/shard_map/ppermute | solution.py:57
  481.2 11.0 %collective-permute-start.60 = (bf16[160,1024]{1,0:T(8,128)(2,1)}, bf16[160,1024]{1,0:T(8,128)(2,1)}, u32[]{:S(2)}, u32[]{:S(2)}) collective-permute-start(bf16[160,1024]{1,0:T(8,128)(2,1)} %maximum_select_fusion.8), channel_id=1, source_target_pairs={{0,8},{4,12},{8,0},{12,4},{16,24},{20,28},{24,16},{28,20},{1,9},{5... | collective-permute-start | bytes 983048 | tf_op jit(solution)/shard_map/ppermute | solution.py:57
  483.2 14.0 %collective-permute-start.67 = (bf16[160,1024]{1,0:T(8,128)(2,1)S(1)}, bf16[160,1024]{1,0:T(8,128)(2,1)}, u32[]{:S(2)}, u32[]{:S(2)}) collective-permute-start(bf16[160,1024]{1,0:T(8,128)(2,1)S(1)} %maximum_select_fusion.9), channel_id=1, source_target_pairs={{0,8},{4,12},{8,0},{12,4},{16,24},{20,28},{24,16},{28,20},{1,9},{5... | collective-permute-start | bytes 983048 | tf_op jit(solution)/shard_map/ppermute | solution.py:57
  494.6 18.0 %collective-permute-start.61 = (bf16[320,1024]{1,0:T(8,128)(2,1)}, bf16[320,1024]{1,0:T(8,128)(2,1)}, u32[]{:S(2)}, u32[]{:S(2)}) collective-permute-start(bf16[320,1024]{1,0:T(8,128)(2,1)} %maximum_select_fusion.4), channel_id=1, source_target_pairs={{0,4},{4,0},{8,12},{12,8},{16,20},{20,16},{24,28},{28,24},{1,5},{5... | collective-permute-start | bytes 1966088 | tf_op jit(solution)/shard_map/ppermute | solution.py:57
  499.4 22.3 %collective-permute-start.68 = (bf16[320,1024]{1,0:T(8,128)(2,1)}, bf16[320,1024]{1,0:T(8,128)(2,1)}, u32[]{:S(2)}, u32[]{:S(2)}) collective-permute-start(bf16[320,1024]{1,0:T(8,128)(2,1)} %maximum_select_fusion.5), channel_id=1, source_target_pairs={{0,4},{4,0},{8,12},{12,8},{16,20},{20,16},{24,28},{28,24},{1,5},{5... | collective-permute-start | bytes 1966088 | tf_op jit(solution)/shard_map/ppermute | solution.py:57
  (100 other events, 825.3 us)

commit v2 on v1

--- a/solution.py
+++ b/solution.py
@@ -20,6 +20,7 @@
 VMEM = pltpu.VMEM
 SMEM = pltpu.SMEM
 LIMIT = 60 << 20
+MESH = pl.DeviceIdType.MESH
 
 
 def matdot(left, right, left_dim, right_dim):
@@ -183,13 +184,13 @@
     return jnp.concatenate([part, empty] if head == 0 else [empty, part], 0)
 
 
-def unroll(outs, rolled_ref, place, block):
+def unroll(outs, rolled_ref, my_row, offset, block):
     total = 4 * block
     rolled_ref[:, pl.ds(0, TILE)] = rolled_ref[:, pl.ds(total, TILE)]
-    back = roll_matrix(TILE - place[1])
+    back = roll_matrix(TILE - offset)
     for j, out in enumerate(outs):
         for part in range(block // TILE):
-            at = pl.multiple_of((place[0] ^ j) * block + part * TILE, TILE)
+            at = pl.multiple_of((my_row ^ j) * block + part * TILE, TILE)
             rows = matdot(back, rolled_ref[:, pl.ds(at, 2 * TILE)], 1, 1)
             out[part * TILE : (part + 1) * TILE, :] = rows.astype(BF)
 
@@ -232,7 +233,7 @@
     @pl.when(last)
     def _():
         run(LONGEST, total - LONGEST, seg_col[...] == seg_row[...])
-        unroll((o0, o1, o2, o3), rolled_ref, place, block)
+        unroll((o0, o1, o2, o3), rolled_ref, place[0], place[1], block)
 
 
 def attend(place, pair, qt, k, vt, seg_col, seg_row):
@@ -273,10 +274,12 @@
 
 def attend_back_kernel(
     place, qt, k, kt, v, ot, lse, g0, g1, g2, g3, seg_col, seg_row, cos_t, sin_t,
-    rolled_out, bias_out, s0, s1, s2, s3,
-    grad_rows, grad_t, row_dots, dqt, dkt, dvt, nat_ref,
+    rolled_out, bias_out, s0, r1, r2, r3,
+    grad_rows, grad_t, row_dots, dqt, dkt, dvt, nat_ref, s1, s2, s3, send_sem, recv_sem,
 ):
     step = pl.program_id(0)
+    my_row = lax.axis_index("row")
+    there = lambda j: {"row": my_row ^ j}
     total = k.shape[0]
     block = total // 4
     steps = total // TILE
@@ -286,9 +289,13 @@
     @pl.when(step == 0)
     def _():
         for j, source in enumerate((g0, g1, g2, g3)):
-            at = pl.multiple_of((place[0] ^ j) * block, block)
+            at = pl.multiple_of((my_row ^ j) * block, block)
             grad_rows[pl.ds(at, block), :] = source[...]
         grad_rows[pl.ds(total, TILE), :] = grad_rows[pl.ds(0, TILE), :]
+        barrier = pltpu.get_barrier_semaphore()
+        for j in range(1, 4):
+            pl.semaphore_signal(barrier, inc=1, device_id=there(j), device_id_type=MESH)
+        pl.semaphore_wait(barrier, 3)
         dkt[...] = jnp.zeros_like(dkt)
         dvt[...] = jnp.zeros_like(dvt)
 
@@ -350,7 +357,17 @@
 
         sums = lax.fori_loop(0, steps, finish, jnp.zeros((1, 384), F32))
         bias_out[...] = jnp.broadcast_to(sums, bias_out.shape)
-        unroll((s0, s1, s2, s3), nat_ref, place, block)
+        unroll((s0, s1, s2, s3), nat_ref, my_row, place[1], block)
+        copies = [
+            pltpu.make_async_remote_copy(
+                src, dst, send_sem.at[j], recv_sem.at[j], device_id=there(j + 1), device_id_type=MESH
+            )
+            for j, (src, dst) in enumerate(((s1, r1), (s2, r2), (s3, r3)))
+        ]
+        for copy in copies:
+            copy.start()
+        for copy in copies:
+            copy.wait()
 
 
 def attend_back(place, pair, qt, k, kt, v, ot, lse, grads, seg_col, seg_row, cos_t, sin_t):
@@ -382,7 +399,8 @@
             pl.BlockSpec((total, 384), lambda i: (0, 0)),
             pl.BlockSpec((8, 384), lambda i: (0, 0)),
         ]
-        + [pl.BlockSpec((block, 384), lambda i: (0, 0))] * 4,
+        + [pl.BlockSpec((block, 384), lambda i: (0, 0))]
+        + [pl.BlockSpec(memory_space=pl.ANY)] * 3,
         scratch_shapes=[
             VMEM((total + TILE, 128), BF),
             VMEM((128, total), BF),
@@ -391,14 +409,21 @@
             VMEM((128, total), F32),
             VMEM((128, total), F32),
             VMEM((384, total + TILE), BF),
+            VMEM((block, 384), BF),
+            VMEM((block, 384), BF),
+            VMEM((block, 384), BF),
+            pltpu.SemaphoreType.DMA((3,)),
+            pltpu.SemaphoreType.DMA((3,)),
         ],
-        compiler_params=pltpu.CompilerParams(vmem_limit_bytes=LIMIT),
+        compiler_params=pltpu.CompilerParams(
+            vmem_limit_bytes=LIMIT, collective_id=1 + pair, has_side_effects=True
+        ),
         cost_estimate=pl.CostEstimate(
             flops=2 * 2 * 5 * total * LONGEST * 256,
             bytes_accessed=8 << 20,
             transcendentals=2 * total * LONGEST,
         ),
-        name="attend_back",
+        name=f"attend_back{pair}",
     )(place, qt, k, kt, v, ot, lse, *grads, seg_col, seg_row, cos_t, sin_t)
 
 
@@ -574,7 +599,7 @@
             place, pair, qt, k_rows, kt, v_rows, heads_t[pair], log_totals[pair], grad_pieces[pair],
             seg_col, seg_row, cos_t, sin_t,
         )
-        back_pieces += [outs[0]] + [exchange(outs[j], "row", j) for j in range(1, 4)]
+        back_pieces += outs
         qkv_bias.append(sums[0].reshape(3, 128))
         total = contract_rows(mixed, rolled).astype(BF).reshape(4, width, 384)
         for bit in bits_of(n_grp):

time: 539 us -> 554 us (1.028)
  Pallas kernels: 126 us -> 165 us
  waiting for transfers between devices: 159 us -> 134 us
    pallas_call x2, Pallas kernels: 54.5 us -> 92.8 us  [attend_back(): pl.pallas_call(attend_back_kernel, grid=(total // TILE,), out_shape=[jax....]
    ppermute x69 -> x63, waiting for transfers between devices: 159 us -> 134 us  [exchange(): return lax.ppermute(tensor, axis, [(i, i ^ bit) for i in range(size)])]
    ppermute x69 -> x63, starting transfers between devices: 53.1 us -> 54.9 us  [exchange(): return lax.ppermute(tensor, axis, [(i, i ^ bit) for i in range(size)])]
    unnamed x219 -> x223, local copies, waits for them, and re-layouts: 41.5 us -> 42.4 us
  transfers between devices with their start and end apart: 69 -> 63, of which waited for: 31 -> 27; matrix products, arithmetic and copies ran while one was open for 25% -> 31% of each run, Pallas kernels for 12% -> 30%
where the time goes in v2:
time: 554 us; the launch traced here: 544 us
  Pallas kernels  165 us (30%)
  waiting for transfers between devices  134 us (24%)
  local copies, waits for them, and re-layouts  69.2 us (12%)
  matrix products  68.3 us (12%)
  starting transfers between devices  54.9 us (10%)
  other arithmetic  47.8 us (9%)
    ppermute x63, waiting for transfers between devices, exchange(): return lax.ppermute(tensor, axis, [(i, i ^ bit) for i in range(size)])  134 us
    pallas_call x2, Pallas kernels, attend_back(): pl.pallas_call(attend_back_kernel, grid=(total // TILE,), out_shape=[jax....  92.8 us
    ppermute x63, starting transfers between devices, exchange(): return lax.ppermute(tensor, axis, [(i, i ^ bit) for i in range(size)])  54.9 us
    unnamed x223, local copies, waits for them, and re-layouts  42.4 us
    pallas_call x2, Pallas kernels, attend(): pl.pallas_call(attend_kernel, grid=(total // TILE,), out_shape=[jax.Shape...  38.7 us
    dot_general x8, matrix products, matdot(): lax.dot_general(left, right, (((left_dim,), (right_dim,)), ((), ())), pre...  35 us
    pallas_call x1, Pallas kernels, project(): pl.pallas_call(project_kernel, grid=(total // TILE,), out_shape=[jax.Shap...  17.1 us
    pallas_call x2, Pallas kernels, weight_grads(): pl.pallas_call(weight_grad_kernel, grid_spec=pltpu.PrefetchScalarGridSpec...  16 us
  transfers between devices with their start and end apart: 63, of which 27 were waited for; matrix products, arithmetic and copies ran while one was open for 31% of the time, Pallas kernels for 30%

profile of v2, /device:TPU:0, one launch (start us, length us, event | category | flops | bytes accessed | tf_op | source)
XLA Modules:
  0.0 543.7 jit_solution(12201911046736092293)
XLA Ops:
  1.2 2.6 collective-permute-start.1
  13.5 2.7 constant_dynamic-slice_fusion.25
  22.8 6.3 %convolution_add_fusion = f32[4,6144]{1,0:T(4,128)S(1)} fusion(bf16[4,1024]{1,0:T(4,128)(2,1)S(1)} %fusion.54, bf16[1024,6144]{1,0:T(8,128)(2,1)} %param.21, f32[6144]{0:T(1024)S(1)} %copy-done.55), kind=kOutput, calls=%fused_computation.10 | convolution fusion | flops 50356224 | bytes 12713984 | tf_op jit(solution)/shard_map/dot_general | solution.py:527
  39.9 2.9 constant_dynamic-slice_fusion.35
  59.7 2.7 copy-done.56
  69.3 8.0 %fusion.39 = f32[512,6144]{1,0:T(8,128)} fusion(f32[4,6144]{1,0:T(4,128)S(1)} %convolution_add_fusion, s32[512]{0:T(512)S(1)} %convert_reduce_fusion.6), kind=kOutput, calls=%fused_computation.112 | convolution fusion | flops 150996992 | bytes 12683264 | tf_op jit(solution)/shard_map/dot_general | solution.py:546
  82.6 2.6 collective-permute-start.21
  86.2 17.1 %project.1 = (bf16[2048,1024]{1,0:T(8,128)(2,1)}, bf16[256,2048]{1,0:T(8,128)(2,1)}, bf16[256,2048]{1,0:T(8,128)(2,1)}, bf16[256,2048]{1,0:T(8,128)(2,1)}, bf16[...) custom-call(s32[2]{0:T(128)} %pad_add_fusion.place, bf16[512,1024]{1,0:T(8,128)(2,1)} %x0.1, ...), custom_call_target="tpu_custom_call" | custom-call | flops 3221225472 | bytes 16777216 | tf_op jit(solution)/shard_map/project/pallas_call | solution.py:156
  103.3 19.3 %attend.3 = (bf16[128,2048]{1,0:T(8,128)(2,1)}, f32[8,2048]{1,0:T(8,128)}, bf16[512,128]{1,0:T(8,128)(2,1)}, bf16[512,128]{1,0:T(8,128)(2,1)}, bf16[512,128]{1,0:T(8,128)(2,1)}, /*index=5*/bf16[512,128]{1,0:T(8,128)(2,1)}) custom-call(s32[2]{0:T(128)} %pad_add_fusion.place, bf16[256,2048]{1,0:T(8,128)(2,1)} %get-tuple-element.49.qt, ...), custom_call_target="tpu_custom_call" | custom-call | flops 7516192768 | bytes 4194304 | tf_op jit(solution)/shard_map/attend/pallas_call | solution.py:243
  122.6 19.4 %attend.2 = (bf16[128,2048]{1,0:T(8,128)(2,1)}, f32[8,2048]{1,0:T(8,128)}, bf16[512,128]{1,0:T(8,128)(2,1)}, bf16[512,128]{1,0:T(8,128)(2,1)}, bf16[512,128]{1,0:T(8,128)(2,1)}, /*index=5*/bf16[512,128]{1,0:T(8,128)(2,1)}) custom-call(s32[2]{0:T(128)} %pad_add_fusion.place, bf16[256,2048]{1,0:T(8,128)(2,1)} %get-tuple-element.49.qt, ...), custom_call_target="tpu_custom_call" | custom-call | flops 7516192768 | bytes 4194304 | tf_op jit(solution)/shard_map/attend/pallas_call | solution.py:243
  148.8 5.6 %collective-permute-done.6 = bf16[512,128]{1,0:T(8,128)(2,1)S(1)} collective-permute-done((bf16[512,128]{1,0:T(8,128)(2,1)S(1)}, bf16[512,128]{1,0:T(8,128)(2,1)S(1)}, u32[]{:S(2)}, u32[]{:S(2)}) %collective-permute-start.6) | collective-permute-done | bytes 131104 | tf_op jit(solution)/shard_map/ppermute | solution.py:58
  156.4 4.6 fusion.74
  162.3 3.9 convert_reduce_fusion.2
  169.1 5.3 convert_reduce_fusion
  174.4 5.9 %fusion.70 = (f32[512]{0:T(512)S(1)}, f32[512]{0:T(512)S(1)}, f32[512,1024]{1,0:T(8,128)S(1)}) fusion(f32[512,6144]{1,0:T(8,128)} %fusion.39, f32[512]{0:T(512)S(1)} %add_rsqrt_fusion.1, f32[512,1024]{1,0:T(8,128)S(1)} %get-tuple-element.142, f32[512]{0:T(512)S(1)} %broadcast_multiply_fusion.5, bf16[512,2048]{1,0:T(8,128)(2,1)S(1)} %get-tuple-element.138.e_z, ...), kind=kOutput, calls=%fused_computation.274 | convolution fusion | flops 2151152640 | bytes 12591104 | tf_op jit(solution)/shard_map/dot_general | solution.py:27
  180.4 7.5 %convert_reduce_fusion.3 = (f32[1024]{0:T(1024)S(1)}, bf16[512,1024]{1,0:T(8,128)(2,1)S(1)}, f32[512,1024]{1,0:T(8,128)S(1)}, bf16[512,1024]{1,0:T(8,128)(2,1)}, f32[512,1024]{1,0:T(8,128)}, /*index=5*/f32[512,1024]{1,0:T(8,128)}) fusion(f32[512,6144]{1,0:T(8,128)} %fusion.39, f32[512]{0:T(512)S(1)} %broadcast_multiply_fusion.3, ...), kind=kOutput, calls=%fused_computation.56 | convolution fusion | flops 2157968384 | bytes 26230784 | tf_op jit(solution)/shard_map/dot_general | solution.py:556
  190.2 8.1 %weight_grads.2 = bf16[2,1280,1024]{2,1,0:T(8,128)(2,1)} custom-call(s32[2]{0:T(128)} %pad_add_fusion.place, bf16[512,1024]{1,0:T(8,128)(2,1)} %copy-done.5, bf16[512,1024]{1,0:T(8,128)(2,1)} %copy-done.2, bf16[512,2048]{1,0:T(8,128)(2,1)} %copy-done, bf16[512,1024]{1,0:T(8,128)(2,1)} %copy-done.3, bf16[512,2048]{1,0:T(8,128)(2,1)} %copy-done.4, ...), custom_call_target="tpu_custom_call" | custom-call | flops 2684354560 | bytes 12582912 | tf_op jit(solution)/shard_map/weight_grads/pallas_call | solution.py:442
  200.7 7.9 %weight_grads.3 = bf16[2,1280,1024]{2,1,0:T(8,128)(2,1)} custom-call(s32[2]{0:T(128)} %pad_add_fusion.place, bf16[512,1024]{1,0:T(8,128)(2,1)} %copy-done.5, bf16[512,1024]{1,0:T(8,128)(2,1)} %copy-done.2, bf16[512,2048]{1,0:T(8,128)(2,1)} %copy-done, bf16[512,1024]{1,0:T(8,128)(2,1)} %copy-done.3, bf16[512,2048]{1,0:T(8,128)(2,1)} %copy-done.4, ...), custom_call_target="tpu_custom_call" | custom-call | flops 2684354560 | bytes 12582912 | tf_op jit(solution)/shard_map/weight_grads/pallas_call | solution.py:442
  211.1 6.5 %collective-permute-done.44 = f32[4096]{0:T(1024)S(1)} collective-permute-done((f32[4096]{0:T(1024)S(1)}, f32[4096]{0:T(1024)S(1)}, u32[]{:S(2)}, u32[]{:S(2)}) %collective-permute-start.44) | collective-permute-done | bytes 16416 | tf_op jit(solution)/shard_map/ppermute | solution.py:58
  220.3 46.3 %attend_back0.1 = (bf16[2048,384]{1,0:T(8,128)(2,1)}, f32[8,384]{1,0:T(8,128)}, bf16[512,384]{1,0:T(8,128)(2,1)}, bf16[512,384]{1,0:T(8,128)(2,1)}, bf16[512,384]{1,0:T(8,128)(2,1)}, /*index=5*/bf16[512,384]{1,0:T(8,128)(2,1)}) custom-call(s32[2]{0:T(128)} %pad_add_fusion.place, bf16[256,2048]{1,0:T(8,128)(2,1)} %get-tuple-element.49.qt, ...), custom_call_target="tpu_custom_call" | custom-call | flops 18790481920 | bytes 8388608 | tf_op jit(solution)/shard_map/attend_back0/pallas_call | solution.py:379
  268.0 46.5 %attend_back1.1 = (bf16[2048,384]{1,0:T(8,128)(2,1)}, f32[8,384]{1,0:T(8,128)}, bf16[512,384]{1,0:T(8,128)(2,1)}, bf16[512,384]{1,0:T(8,128)(2,1)}, bf16[512,384]{1,0:T(8,128)(2,1)}, /*index=5*/bf16[512,384]{1,0:T(8,128)(2,1)}) custom-call(s32[2]{0:T(128)} %pad_add_fusion.place, bf16[256,2048]{1,0:T(8,128)(2,1)} %get-tuple-element.49.qt, ...), custom_call_target="tpu_custom_call" | custom-call | flops 18790481920 | bytes 8388608 | tf_op jit(solution)/shard_map/attend_back1/pallas_call | solution.py:379
  315.9 5.2 convolution_convert_fusion.2
  325.6 5.5 %fusion.71 = (f32[512]{0:T(512)S(1)}, f32[512]{0:T(512)S(1)}, f32[512,1024]{1,0:T(8,128)S(1)}) fusion(f32[512,6144]{1,0:T(8,128)} %fusion.39, f32[512]{0:T(512)S(1)} %add_rsqrt_fusion, f32[512]{0:T(512)S(1)} %broadcast_multiply_fusion.1, bf16[512,1024]{1,0:T(8,128)(2,1)S(1)} %copy-done.11, bf16[512,3072]{1,0:T(8,128)(2,1)S(1)} %constant_dynamic-update-slice_fusion.8, ...), kind=kOutput, calls=%fused_computation.275 | convolution fusion | flops 3225418752 | bytes 14688256 | tf_op jit(solution)/shard_map/dot_general | solution.py:27
  331.2 3.8 fusion.22
  337.4 2.9 fusion
  341.4 2.8 collective-permute-done.46
  345.2 3.6 collective-permute-done.47
  351.4 3.7 collective-permute-done.18
  357.9 9.5 %collective-permute-done.22 = bf16[4,6144]{1,0:T(4,128)(2,1)S(1)} collective-permute-done((bf16[4,6144]{1,0:T(4,128)(2,1)S(1)}, bf16[4,6144]{1,0:T(4,128)(2,1)S(1)}, u32[]{:S(2)}, u32[]{:S(2)}) %collective-permute-start.22) | collective-permute-done | bytes 49184 | tf_op jit(solution)/shard_map/ppermute | solution.py:58
  368.4 4.0 fusion.45
  375.3 5.6 %collective-permute-done.24 = bf16[16,6144]{1,0:T(8,128)(2,1)S(1)} collective-permute-done((bf16[16,6144]{1,0:T(8,128)(2,1)S(1)}, bf16[16,6144]{1,0:T(8,128)(2,1)S(1)}, u32[]{:S(2)}, u32[]{:S(2)}) %collective-permute-start.24) | collective-permute-done | bytes 196640 | tf_op jit(solution)/shard_map/ppermute | solution.py:58
  380.9 4.5 fusion.49
  386.3 5.3 add_convert_fusion
  398.7 19.8 %collective-permute-done.39 = bf16[32,384]{1,0:T(8,128)(2,1)S(1)} collective-permute-done((bf16[32,384]{1,0:T(8,128)(2,1)S(1)}, bf16[32,384]{1,0:T(8,128)(2,1)S(1)}, u32[]{:S(2)}, u32[]{:S(2)}) %collective-permute-start.39) | collective-permute-done | bytes 24608 | tf_op jit(solution)/shard_map/ppermute | solution.py:58
  426.1 6.9 %collective-permute-done.40 = bf16[4,32,384]{2,1,0:T(8,128)(2,1)S(1)} collective-permute-done((bf16[4,32,384]{2,1,0:T(8,128)(2,1)S(1)}, bf16[4,32,384]{2,1,0:T(8,128)(2,1)S(1)}, u32[]{:S(2)}, u32[]{:S(2)}) %collective-permute-start.40) | collective-permute-done | bytes 98336 | tf_op jit(solution)/shard_map/ppermute | solution.py:58
  442.7 2.5 collective-permute-done.32
  446.9 6.7 %collective-permute-done.50 = bf16[320,1024]{1,0:T(8,128)(2,1)S(1)} collective-permute-done((bf16[320,1024]{1,0:T(8,128)(2,1)S(1)}, bf16[320,1024]{1,0:T(8,128)(2,1)S(1)}, u32[]{:S(2)}, u32[]{:S(2)}) %collective-permute-start.50) | collective-permute-done | bytes 655392 | tf_op jit(solution)/shard_map/ppermute | solution.py:58
  455.4 3.8 collective-permute-done.57
  460.3 9.4 %collective-permute-done.51 = bf16[160,1024]{1,0:T(8,128)(2,1)S(1)} collective-permute-done((bf16[160,1024]{1,0:T(8,128)(2,1)S(1)}, bf16[160,1024]{1,0:T(8,128)(2,1)S(1)}, u32[]{:S(2)}, u32[]{:S(2)}) %collective-permute-start.51) | collective-permute-done | bytes 327712 | tf_op jit(solution)/shard_map/ppermute | solution.py:58
  470.0 9.7 %collective-permute-done.58 = bf16[2,80,1024]{2,1,0:T(8,128)(2,1)S(1)} collective-permute-done((bf16[2,80,1024]{2,1,0:T(8,128)(2,1)S(1)}, bf16[2,80,1024]{2,1,0:T(8,128)(2,1)S(1)}, u32[]{:S(2)}, u32[]{:S(2)}) %collective-permute-start.58) | collective-permute-done | bytes 327712 | tf_op jit(solution)/shard_map/ppermute | solution.py:58
  481.9 3.3 collective-permute-done.59
  485.6 9.8 %collective-permute-done.53 = bf16[80,1024]{1,0:T(8,128)(2,1)S(1)} collective-permute-done((bf16[80,1024]{1,0:T(8,128)(2,1)S(1)}, bf16[80,1024]{1,0:T(8,128)(2,1)S(1)}, u32[]{:S(2)}, u32[]{:S(2)}) %collective-permute-start.53) | collective-permute-done | bytes 163872 | tf_op jit(solution)/shard_map/ppermute | solution.py:58
  499.9 7.3 %collective-permute-done.54 = bf16[160,1024]{1,0:T(8,128)(2,1)} collective-permute-done((bf16[160,1024]{1,0:T(8,128)(2,1)}, bf16[160,1024]{1,0:T(8,128)(2,1)}, u32[]{:S(2)}, u32[]{:S(2)}) %collective-permute-start.54) | collective-permute-done | bytes 327712 | tf_op jit(solution)/shard_map/ppermute | solution.py:58
  507.1 2.4 maximum_select_fusion.4
  517.8 2.4 copy.110
  521.9 2.7 copy.114
  529.9 6.9 %collective-permute-done.62 = bf16[320,1024]{1,0:T(8,128)(2,1)} collective-permute-done((bf16[320,1024]{1,0:T(8,128)(2,1)}, bf16[320,1024]{1,0:T(8,128)(2,1)}, u32[]{:S(2)}, u32[]{:S(2)}) %collective-permute-start.62) | collective-permute-done | bytes 655392 | tf_op jit(solution)/shard_map/ppermute | solution.py:58
  536.8 2.5 maximum_select_fusion.1
  (457 shorter events, 155.0 us)
Async XLA Ops:
  0.7 84.6 %collective-permute-start = (bf16[512,1024]{1,0:T(8,128)(2,1)}, bf16[512,1024]{1,0:T(8,128)(2,1)}, u32[]{:S(2)}, u32[]{:S(2)}) collective-permute-start(bf16[512,1024]{1,0:T(8,128)(2,1)} %x0.1), channel_id=1, source_target_pairs={{0,1},{1,0},{2,3},{3,2},{4,5},{5,4},{6,7},{7,6},{8,9},{9,8},{10,11... | collective-permute-start | bytes 3145736 | tf_op jit(solution)/shard_map/ppermute | solution.py:58
  1.2 65.3 %collective-permute-start.1 = (bf16[512,1024]{1,0:T(8,128)(2,1)}, bf16[512,1024]{1,0:T(8,128)(2,1)}, u32[]{:S(2)}, u32[]{:S(2)}) collective-permute-start(bf16[512,1024]{1,0:T(8,128)(2,1)} %x0.1), channel_id=1, source_target_pairs={{0,2},{1,3},{2,0},{3,1},{4,6},{5,7},{6,4},{7,5},{8,10},{9,11},{10,... | collective-permute-start | bytes 3145736 | tf_op jit(solution)/shard_map/ppermute | solution.py:58
  4.5 72.9 %collective-permute-start.19 = (bf16[4,1024]{1,0:T(4,128)(2,1)S(1)}, bf16[4,1024]{1,0:T(4,128)(2,1)S(1)}, u32[]{:S(2)}, u32[]{:S(2)}) collective-permute-start(bf16[4,1024]{1,0:T(4,128)(2,1)S(1)} %fusion.54), channel_id=1, source_target_pairs={{0,4},{4,0},{8,12},{12,8},{16,20},{20,16},{24,28},{28,24},{1,5},{5... | collective-permute-start | bytes 24584 | tf_op jit(solution)/shard_map/ppermute | solution.py:58
  66.4 18.8 %collective-permute-start.2 = (bf16[512,1024]{1,0:T(8,128)(2,1)}, bf16[512,1024]{1,0:T(8,128)(2,1)S(1)}, u32[]{:S(2)}, u32[]{:S(2)}) collective-permute-start(bf16[512,1024]{1,0:T(8,128)(2,1)} %collective-permute-done.1.x2), channel_id=1, source_target_pairs={{0,1},{1,0},{2,3},{3,2},{4,5},{5,4},{6,7},{7,6},{8,9},{9,8},{10,11... | collective-permute-start | bytes 3145736 | tf_op jit(solution)/shard_map/ppermute | solution.py:58
  82.6 292.7 %collective-permute-start.21 = (bf16[16,1024]{1,0:T(8,128)(2,1)}, bf16[16,1024]{1,0:T(8,128)(2,1)}, u32[]{:S(2)}, u32[]{:S(2)}) collective-permute-start(bf16[16,1024]{1,0:T(8,128)(2,1)} %pad_maximum_fusion.13), channel_id=1, source_target_pairs={{0,16},{4,20},{8,24},{12,28},{16,0},{20,4},{24,8},{28,12},{1,17},{... | collective-permute-start | bytes 98312 | tf_op jit(solution)/shard_map/ppermute | solution.py:58
  142.8 11.6 %collective-permute-start.7 = (bf16[512,128]{1,0:T(8,128)(2,1)}, bf16[512,128]{1,0:T(8,128)(2,1)S(1)}, u32[]{:S(2)}, u32[]{:S(2)}) collective-permute-start(bf16[512,128]{1,0:T(8,128)(2,1)} %get-tuple-element.58), channel_id=1, source_target_pairs={{0,3},{1,2},{2,1},{3,0},{4,7},{5,6},{6,5},{7,4},{8,11},{9,10},{10,... | collective-permute-start | bytes 393224 | tf_op jit(solution)/shard_map/ppermute | solution.py:58
  145.4 9.0 %collective-permute-start.6 = (bf16[512,128]{1,0:T(8,128)(2,1)S(1)}, bf16[512,128]{1,0:T(8,128)(2,1)S(1)}, u32[]{:S(2)}, u32[]{:S(2)}) collective-permute-start(bf16[512,128]{1,0:T(8,128)(2,1)S(1)} %copy-done.68), channel_id=1, source_target_pairs={{0,2},{1,3},{2,0},{3,1},{4,6},{5,7},{6,4},{7,5},{8,10},{9,11},{10,... | collective-permute-start | bytes 393224 | tf_op jit(solution)/shard_map/ppermute | solution.py:58
  146.1 10.2 %collective-permute-start.8 = (bf16[512,128]{1,0:T(8,128)(2,1)S(1)}, bf16[512,128]{1,0:T(8,128)(2,1)S(1)}, u32[]{:S(2)}, u32[]{:S(2)}) collective-permute-start(bf16[512,128]{1,0:T(8,128)(2,1)S(1)} %copy-done.64), channel_id=1, source_target_pairs={{0,3},{1,2},{2,1},{3,0},{4,7},{5,6},{6,5},{7,4},{8,11},{9,10},{10,... | collective-permute-start | bytes 393224 | tf_op jit(solution)/shard_map/ppermute | solution.py:58
  200.4 10.1 %collective-permute-start.43 = (f32[4096]{0:T(1024)S(1)}, f32[4096]{0:T(1024)S(1)}, u32[]{:S(2)}, u32[]{:S(2)}) collective-permute-start(f32[4096]{0:T(1024)S(1)} %pad_maximum_fusion.15), channel_id=1, source_target_pairs={{0,1},{1,0},{2,3},{3,2},{4,5},{5,4},{6,7},{7,6},{8,9},{9,8},{10,11... | collective-permute-start | bytes 49160 | tf_op jit(solution)/shard_map/ppermute | solution.py:58
  208.6 9.1 %collective-permute-start.11 = (bf16[512,128]{1,0:T(8,128)(2,1)S(1)}, bf16[512,128]{1,0:T(8,128)(2,1)S(1)}, u32[]{:S(2)}, u32[]{:S(2)}) collective-permute-start(bf16[512,128]{1,0:T(8,128)(2,1)S(1)} %get-tuple-element.184), channel_id=1, source_target_pairs={{0,3},{1,2},{2,1},{3,0},{4,7},{5,6},{6,5},{7,4},{8,11},{9,10},{10,... | collective-permute-start | bytes 393224 | tf_op jit(solution)/shard_map/ppermute | solution.py:58
  209.0 10.2 %collective-permute-start.10 = (bf16[512,128]{1,0:T(8,128)(2,1)S(1)}, bf16[512,128]{1,0:T(8,128)(2,1)S(1)}, u32[]{:S(2)}, u32[]{:S(2)}) collective-permute-start(bf16[512,128]{1,0:T(8,128)(2,1)S(1)} %get-tuple-element.185), channel_id=1, source_target_pairs={{0,2},{1,3},{2,0},{3,1},{4,6},{5,7},{6,4},{7,5},{8,10},{9,11},{10,... | collective-permute-start | bytes 393224 | tf_op jit(solution)/shard_map/ppermute | solution.py:58
  210.5 9.1 %collective-permute-start.9 = (bf16[512,128]{1,0:T(8,128)(2,1)S(1)}, bf16[512,128]{1,0:T(8,128)(2,1)S(1)}, u32[]{:S(2)}, u32[]{:S(2)}) collective-permute-start(bf16[512,128]{1,0:T(8,128)(2,1)S(1)} %get-tuple-element.186), channel_id=1, source_target_pairs={{0,1},{1,0},{2,3},{3,2},{4,5},{5,4},{6,7},{7,6},{8,9},{9,8},{10,11... | collective-permute-start | bytes 393224 | tf_op jit(solution)/shard_map/ppermute | solution.py:58
  217.5 49.7 %collective-permute-start.14 = (bf16[512,128]{1,0:T(8,128)(2,1)S(1)}, bf16[512,128]{1,0:T(8,128)(2,1)S(1)}, u32[]{:S(2)}, u32[]{:S(2)}) collective-permute-start(bf16[512,128]{1,0:T(8,128)(2,1)S(1)} %get-tuple-element.180), channel_id=1, source_target_pairs={{0,3},{1,2},{2,1},{3,0},{4,7},{5,6},{6,5},{7,4},{8,11},{9,10},{10,... | collective-permute-start | bytes 393224 | tf_op jit(solution)/shard_map/ppermute | solution.py:58
  217.7 49.6 %collective-permute-start.13 = (bf16[512,128]{1,0:T(8,128)(2,1)S(1)}, bf16[512,128]{1,0:T(8,128)(2,1)S(1)}, u32[]{:S(2)}, u32[]{:S(2)}) collective-permute-start(bf16[512,128]{1,0:T(8,128)(2,1)S(1)} %get-tuple-element.181), channel_id=1, source_target_pairs={{0,2},{1,3},{2,0},{3,1},{4,6},{5,7},{6,4},{7,5},{8,10},{9,11},{10,... | collective-permute-start | bytes 393224 | tf_op jit(solution)/shard_map/ppermute | solution.py:58
  219.1 48.2 %collective-permute-start.12 = (bf16[512,128]{1,0:T(8,128)(2,1)S(1)}, bf16[512,128]{1,0:T(8,128)(2,1)S(1)}, u32[]{:S(2)}, u32[]{:S(2)}) collective-permute-start(bf16[512,128]{1,0:T(8,128)(2,1)S(1)} %get-tuple-element.182), channel_id=1, source_target_pairs={{0,1},{1,0},{2,3},{3,2},{4,5},{5,4},{6,7},{7,6},{8,9},{9,8},{10,11... | collective-permute-start | bytes 393224 | tf_op jit(solution)/shard_map/ppermute | solution.py:58
  219.6 166.7 %collective-permute-start.48 = (bf16[2,1280,1024]{2,1,0:T(8,128)(2,1)}, bf16[2,1280,1024]{2,1,0:T(8,128)(2,1)}, u32[]{:S(2)}, u32[]{:S(2)}) collective-permute-start(bf16[2,1280,1024]{2,1,0:T(8,128)(2,1)} %weight_grads.3), channel_id=1, source_target_pairs={{0,1},{1,0},{2,3},{3,2},{4,5},{5,4},{6,7},{7,6},{8,9},{9,8},{10,11... | collective-permute-start | bytes 15728648 | tf_op jit(solution)/shard_map/ppermute | solution.py:58
  315.3 25.1 %collective-permute-start.45 = (f32[1792]{0:T(1024)S(1)}, f32[1792]{0:T(1024)S(1)}, u32[]{:S(2)}, u32[]{:S(2)}) collective-permute-start(f32[1792]{0:T(1024)S(1)} %pad_maximum_fusion.16), channel_id=1, source_target_pairs={{0,4},{4,0},{8,12},{12,8},{16,20},{20,16},{24,28},{28,24},{1,5},{5... | collective-permute-start | bytes 21512 | tf_op jit(solution)/shard_map/ppermute | solution.py:58
  336.5 8.0 %collective-permute-start.15 = (f32[4,2048]{1,0:T(4,128)S(1)}, f32[4,2048]{1,0:T(4,128)S(1)}, u32[]{:S(2)}, u32[]{:S(2)}) collective-permute-start(f32[4,2048]{1,0:T(4,128)S(1)} %fusion.15), channel_id=1, source_target_pairs={{0,1},{1,0},{2,3},{3,2},{4,5},{5,4},{6,7},{7,6},{8,9},{9,8},{10,11... | collective-permute-start | bytes 98312 | tf_op jit(solution)/shard_map/ppermute | solution.py:58
  340.4 9.9 %collective-permute-start.17 = (f32[4,4096]{1,0:T(4,128)S(1)}, f32[4,4096]{1,0:T(4,128)S(1)}, u32[]{:S(2)}, u32[]{:S(2)}) collective-permute-start(f32[4,4096]{1,0:T(4,128)S(1)} %fusion), channel_id=1, source_target_pairs={{0,1},{1,0},{2,3},{3,2},{4,5},{5,4},{6,7},{7,6},{8,9},{9,8},{10,11... | collective-permute-start | bytes 196616 | tf_op jit(solution)/shard_map/ppermute | solution.py:58
  348.7 24.1 %collective-permute-start.34 = (bf16[4,128,384]{2,1,0:T(8,128)(2,1)S(1)}, bf16[4,128,384]{2,1,0:T(8,128)(2,1)S(1)}, u32[]{:S(2)}, u32[]{:S(2)}) collective-permute-start(bf16[4,128,384]{2,1,0:T(8,128)(2,1)S(1)} %constant_dynamic-slice_fusion.17), channel_id=1, source_target_pairs={{0,4},{4,0},{8,12},{12,8},{16,20},{20,16},{24,28},{28,24},{1,5},{5... | collective-permute-start | bytes 1179656 | tf_op jit(solution)/shard_map/ppermute | solution.py:58
  350.3 24.0 %collective-permute-start.25 = (bf16[4,128,384]{2,1,0:T(8,128)(2,1)S(1)}, bf16[4,128,384]{2,1,0:T(8,128)(2,1)S(1)}, u32[]{:S(2)}, u32[]{:S(2)}) collective-permute-start(bf16[4,128,384]{2,1,0:T(8,128)(2,1)S(1)} %constant_dynamic-slice_fusion.21), channel_id=1, source_target_pairs={{0,4},{4,0},{8,12},{12,8},{16,20},{20,16},{24,28},{28,24},{1,5},{5... | collective-permute-start | bytes 1179656 | tf_op jit(solution)/shard_map/ppermute | solution.py:58
  355.2 12.2 %collective-permute-start.22 = (bf16[4,6144]{1,0:T(4,128)(2,1)S(1)}, bf16[4,6144]{1,0:T(4,128)(2,1)S(1)}, u32[]{:S(2)}, u32[]{:S(2)}) collective-permute-start(bf16[4,6144]{1,0:T(4,128)(2,1)S(1)} %pad_maximum_fusion.12), channel_id=1, source_target_pairs={{0,4},{4,0},{8,12},{12,8},{16,20},{20,16},{24,28},{28,24},{1,5},{5... | collective-permute-start | bytes 147464 | tf_op jit(solution)/shard_map/ppermute | solution.py:58
  372.4 8.5 %collective-permute-start.24 = (bf16[16,6144]{1,0:T(8,128)(2,1)S(1)}, bf16[16,6144]{1,0:T(8,128)(2,1)S(1)}, u32[]{:S(2)}, u32[]{:S(2)}) collective-permute-start(bf16[16,6144]{1,0:T(8,128)(2,1)S(1)} %pad_maximum_fusion.8), channel_id=1, source_target_pairs={{0,16},{4,20},{8,24},{12,28},{16,0},{20,4},{24,8},{28,12},{1,17},{... | collective-permute-start | bytes 589832 | tf_op jit(solution)/shard_map/ppermute | solution.py:58
  373.0 12.4 %collective-permute-start.35 = (bf16[4,64,384]{2,1,0:T(8,128)(2,1)S(1)}, bf16[4,64,384]{2,1,0:T(8,128)(2,1)S(1)}, u32[]{:S(2)}, u32[]{:S(2)}) collective-permute-start(bf16[4,64,384]{2,1,0:T(8,128)(2,1)S(1)} %constant_dynamic-slice_fusion.16), channel_id=1, source_target_pairs={{0,8},{4,12},{8,0},{12,4},{16,24},{20,28},{24,16},{28,20},{1,9},{5... | collective-permute-start | bytes 589832 | tf_op jit(solution)/shard_map/ppermute | solution.py:58
  374.4 11.8 %collective-permute-start.26 = (bf16[4,64,384]{2,1,0:T(8,128)(2,1)S(1)}, bf16[4,64,384]{2,1,0:T(8,128)(2,1)S(1)}, u32[]{:S(2)}, u32[]{:S(2)}) collective-permute-start(bf16[4,64,384]{2,1,0:T(8,128)(2,1)S(1)} %constant_dynamic-slice_fusion.20), channel_id=1, source_target_pairs={{0,8},{4,12},{8,0},{12,4},{16,24},{20,28},{24,16},{28,20},{1,9},{5... | collective-permute-start | bytes 589832 | tf_op jit(solution)/shard_map/ppermute | solution.py:58
  385.5 9.2 %collective-permute-start.36 = (bf16[4,32,384]{2,1,0:T(8,128)(2,1)S(1)}, bf16[4,32,384]{2,1,0:T(8,128)(2,1)S(1)}, u32[]{:S(2)}, u32[]{:S(2)}) collective-permute-start(bf16[4,32,384]{2,1,0:T(8,128)(2,1)S(1)} %constant_dynamic-slice_fusion.15), channel_id=1, source_target_pairs={{0,16},{4,20},{8,24},{12,28},{16,0},{20,4},{24,8},{28,12},{1,17},{... | collective-permute-start | bytes 294920 | tf_op jit(solution)/shard_map/ppermute | solution.py:58
  391.7 43.6 %collective-permute-start.49 = (bf16[640,1024]{1,0:T(8,128)(2,1)S(1)}, bf16[640,1024]{1,0:T(8,128)(2,1)S(1)}, u32[]{:S(2)}, u32[]{:S(2)}) collective-permute-start(bf16[640,1024]{1,0:T(8,128)(2,1)S(1)} %slice_bitcast_fusion), channel_id=1, source_target_pairs={{0,2},{1,3},{2,0},{3,1},{4,6},{5,7},{6,4},{7,5},{8,10},{9,11},{10,... | collective-permute-start | bytes 3932168 | tf_op jit(solution)/shard_map/ppermute | solution.py:58
  395.1 42.4 %collective-permute-start.56 = (bf16[2,320,1024]{2,1,0:T(8,128)(2,1)S(1)}, bf16[2,320,1024]{2,1,0:T(8,128)(2,1)S(1)}, u32[]{:S(2)}, u32[]{:S(2)}) collective-permute-start(bf16[2,320,1024]{2,1,0:T(8,128)(2,1)S(1)} %constant_dynamic-slice_fusion.10), channel_id=1, source_target_pairs={{0,4},{4,0},{8,12},{12,8},{16,20},{20,16},{24,28},{28,24},{1,5},{5... | collective-permute-start | bytes 3932168 | tf_op jit(solution)/shard_map/ppermute | solution.py:58
  396.7 21.8 %collective-permute-start.39 = (bf16[32,384]{1,0:T(8,128)(2,1)S(1)}, bf16[32,384]{1,0:T(8,128)(2,1)S(1)}, u32[]{:S(2)}, u32[]{:S(2)}) collective-permute-start(bf16[32,384]{1,0:T(8,128)(2,1)S(1)} %get-tuple-element.193), channel_id=1, source_target_pairs={{0,3},{1,2},{2,1},{3,0},{4,7},{5,6},{6,5},{7,4},{8,11},{9,10},{10,... | collective-permute-start | bytes 73736 | tf_op jit(solution)/shard_map/ppermute | solution.py:58
  396.8 24.0 %collective-permute-start.38 = (bf16[32,384]{1,0:T(8,128)(2,1)S(1)}, bf16[32,384]{1,0:T(8,128)(2,1)S(1)}, u32[]{:S(2)}, u32[]{:S(2)}) collective-permute-start(bf16[32,384]{1,0:T(8,128)(2,1)S(1)} %get-tuple-element.194), channel_id=1, source_target_pairs={{0,2},{1,3},{2,0},{3,1},{4,6},{5,7},{6,4},{7,5},{8,10},{9,11},{10,... | collective-permute-start | bytes 73736 | tf_op jit(solution)/shard_map/ppermute | solution.py:58
  398.3 23.0 %collective-permute-start.37 = (bf16[32,384]{1,0:T(8,128)(2,1)S(1)}, bf16[32,384]{1,0:T(8,128)(2,1)S(1)}, u32[]{:S(2)}, u32[]{:S(2)}) collective-permute-start(bf16[32,384]{1,0:T(8,128)(2,1)S(1)} %get-tuple-element.195), channel_id=1, source_target_pairs={{0,1},{1,0},{2,3},{3,2},{4,5},{5,4},{6,7},{7,6},{8,9},{9,8},{10,11... | collective-permute-start | bytes 73736 | tf_op jit(solution)/shard_map/ppermute | solution.py:58
  422.3 10.7 %collective-permute-start.40 = (bf16[4,32,384]{2,1,0:T(8,128)(2,1)S(1)}, bf16[4,32,384]{2,1,0:T(8,128)(2,1)S(1)}, u32[]{:S(2)}, u32[]{:S(2)}) collective-permute-start(bf16[4,32,384]{2,1,0:T(8,128)(2,1)S(1)} %pad_maximum_fusion.11), channel_id=1, source_target_pairs={{0,16},{4,20},{8,24},{12,28},{16,0},{20,4},{24,8},{28,12},{1,17},{... | collective-permute-start | bytes 294920 | tf_op jit(solution)/shard_map/ppermute | solution.py:58
  424.6 10.0 %collective-permute-start.31 = (bf16[4,32,384]{2,1,0:T(8,128)(2,1)S(1)}, bf16[4,32,384]{2,1,0:T(8,128)(2,1)S(1)}, u32[]{:S(2)}, u32[]{:S(2)}) collective-permute-start(bf16[4,32,384]{2,1,0:T(8,128)(2,1)S(1)} %pad_maximum_fusion.10), channel_id=1, source_target_pairs={{0,16},{4,20},{8,24},{12,28},{16,0},{20,4},{24,8},{28,12},{1,17},{... | collective-permute-start | bytes 294920 | tf_op jit(solution)/shard_map/ppermute | solution.py:58
  433.1 7.9 %collective-permute-start.41 = (bf16[4,64,384]{2,1,0:T(8,128)(2,1)S(1)}, bf16[4,64,384]{2,1,0:T(8,128)(2,1)S(1)}, u32[]{:S(2)}, u32[]{:S(2)}) collective-permute-start(bf16[4,64,384]{2,1,0:T(8,128)(2,1)S(1)} %maximum_select_fusion.11), channel_id=1, source_target_pairs={{0,8},{4,12},{8,0},{12,4},{16,24},{20,28},{24,16},{28,20},{1,9},{5... | collective-permute-start | bytes 589832 | tf_op jit(solution)/shard_map/ppermute | solution.py:58
  434.6 10.6 %collective-permute-start.32 = (bf16[4,64,384]{2,1,0:T(8,128)(2,1)S(1)}, bf16[4,64,384]{2,1,0:T(8,128)(2,1)S(1)}, u32[]{:S(2)}, u32[]{:S(2)}) collective-permute-start(bf16[4,64,384]{2,1,0:T(8,128)(2,1)S(1)} %maximum_select_fusion.10), channel_id=1, source_target_pairs={{0,8},{4,12},{8,0},{12,4},{16,24},{20,28},{24,16},{28,20},{1,9},{5... | collective-permute-start | bytes 589832 | tf_op jit(solution)/shard_map/ppermute | solution.py:58
  435.9 17.7 %collective-permute-start.50 = (bf16[320,1024]{1,0:T(8,128)(2,1)S(1)}, bf16[320,1024]{1,0:T(8,128)(2,1)S(1)}, u32[]{:S(2)}, u32[]{:S(2)}) collective-permute-start(bf16[320,1024]{1,0:T(8,128)(2,1)S(1)} %constant_dynamic-slice_fusion.13), channel_id=1, source_target_pairs={{0,4},{4,0},{8,12},{12,8},{16,20},{20,16},{24,28},{28,24},{1,5},{5... | collective-permute-start | bytes 1966088 | tf_op jit(solution)/shard_map/ppermute | solution.py:58
  438.1 21.2 %collective-permute-start.57 = (bf16[2,160,1024]{2,1,0:T(8,128)(2,1)S(1)}, bf16[2,160,1024]{2,1,0:T(8,128)(2,1)S(1)}, u32[]{:S(2)}, u32[]{:S(2)}) collective-permute-start(bf16[2,160,1024]{2,1,0:T(8,128)(2,1)S(1)} %constant_dynamic-slice_fusion.9), channel_id=1, source_target_pairs={{0,8},{4,12},{8,0},{12,4},{16,24},{20,28},{24,16},{28,20},{1,9},{5... | collective-permute-start | bytes 1966088 | tf_op jit(solution)/shard_map/ppermute | solution.py:58
  441.1 44.2 %collective-permute-start.42 = (bf16[4,128,384]{2,1,0:T(8,128)(2,1)S(1)}, bf16[4,128,384]{2,1,0:T(8,128)(2,1)S(1)}, u32[]{:S(2)}, u32[]{:S(2)}) collective-permute-start(bf16[4,128,384]{2,1,0:T(8,128)(2,1)S(1)} %maximum_select_fusion.7), channel_id=1, source_target_pairs={{0,4},{4,0},{8,12},{12,8},{16,20},{20,16},{24,28},{28,24},{1,5},{5... | collective-permute-start | bytes 1179656 | tf_op jit(solution)/shard_map/ppermute | solution.py:58
  445.3 53.0 %collective-permute-start.33 = (bf16[4,128,384]{2,1,0:T(8,128)(2,1)S(1)}, bf16[4,128,384]{2,1,0:T(8,128)(2,1)S(1)}, u32[]{:S(2)}, u32[]{:S(2)}) collective-permute-start(bf16[4,128,384]{2,1,0:T(8,128)(2,1)S(1)} %maximum_select_fusion.6), channel_id=1, source_target_pairs={{0,4},{4,0},{8,12},{12,8},{16,20},{20,16},{24,28},{28,24},{1,5},{5... | collective-permute-start | bytes 1179656 | tf_op jit(solution)/shard_map/ppermute | solution.py:58
  453.9 15.9 %collective-permute-start.51 = (bf16[160,1024]{1,0:T(8,128)(2,1)S(1)}, bf16[160,1024]{1,0:T(8,128)(2,1)S(1)}, u32[]{:S(2)}, u32[]{:S(2)}) collective-permute-start(bf16[160,1024]{1,0:T(8,128)(2,1)S(1)} %constant_dynamic-slice_fusion.12), channel_id=1, source_target_pairs={{0,8},{4,12},{8,0},{12,4},{16,24},{20,28},{24,16},{28,20},{1,9},{5... | collective-permute-start | bytes 983048 | tf_op jit(solution)/shard_map/ppermute | solution.py:58
  459.5 20.2 %collective-permute-start.58 = (bf16[2,80,1024]{2,1,0:T(8,128)(2,1)S(1)}, bf16[2,80,1024]{2,1,0:T(8,128)(2,1)S(1)}, u32[]{:S(2)}, u32[]{:S(2)}) collective-permute-start(bf16[2,80,1024]{2,1,0:T(8,128)(2,1)S(1)} %constant_dynamic-slice_fusion.8), channel_id=1, source_target_pairs={{0,16},{4,20},{8,24},{12,28},{16,0},{20,4},{24,8},{28,12},{1,17},{... | collective-permute-start | bytes 983048 | tf_op jit(solution)/shard_map/ppermute | solution.py:58
  469.9 11.9 %collective-permute-start.52 = (bf16[80,1024]{1,0:T(8,128)(2,1)S(1)}, bf16[80,1024]{1,0:T(8,128)(2,1)S(1)}, u32[]{:S(2)}, u32[]{:S(2)}) collective-permute-start(bf16[80,1024]{1,0:T(8,128)(2,1)S(1)} %constant_dynamic-slice_fusion.11), channel_id=1, source_target_pairs={{0,16},{4,20},{8,24},{12,28},{16,0},{20,4},{24,8},{28,12},{1,17},{... | collective-permute-start | bytes 491528 | tf_op jit(solution)/shard_map/ppermute | solution.py:58
  481.8 13.5 %collective-permute-start.53 = (bf16[80,1024]{1,0:T(8,128)(2,1)S(1)}, bf16[80,1024]{1,0:T(8,128)(2,1)S(1)}, u32[]{:S(2)}, u32[]{:S(2)}) collective-permute-start(bf16[80,1024]{1,0:T(8,128)(2,1)S(1)} %add_convert_fusion.11), channel_id=1, source_target_pairs={{0,16},{4,20},{8,24},{12,28},{16,0},{20,4},{24,8},{28,12},{1,17},{... | collective-permute-start | bytes 491528 | tf_op jit(solution)/shard_map/ppermute | solution.py:58
  485.2 12.9 %collective-permute-start.60 = (bf16[80,1024]{1,0:T(8,128)(2,1)S(1)}, bf16[80,1024]{1,0:T(8,128)(2,1)S(1)}, u32[]{:S(2)}, u32[]{:S(2)}) collective-permute-start(bf16[80,1024]{1,0:T(8,128)(2,1)S(1)} %fusion.38), channel_id=1, source_target_pairs={{0,16},{4,20},{8,24},{12,28},{16,0},{20,4},{24,8},{28,12},{1,17},{... | collective-permute-start | bytes 491528 | tf_op jit(solution)/shard_map/ppermute | solution.py:58
  496.2 11.0 %collective-permute-start.54 = (bf16[160,1024]{1,0:T(8,128)(2,1)}, bf16[160,1024]{1,0:T(8,128)(2,1)}, u32[]{:S(2)}, u32[]{:S(2)}) collective-permute-start(bf16[160,1024]{1,0:T(8,128)(2,1)} %maximum_select_fusion.8), channel_id=1, source_target_pairs={{0,8},{4,12},{8,0},{12,4},{16,24},{20,28},{24,16},{28,20},{1,9},{5... | collective-permute-start | bytes 983048 | tf_op jit(solution)/shard_map/ppermute | solution.py:58
  498.2 14.0 %collective-permute-start.61 = (bf16[160,1024]{1,0:T(8,128)(2,1)S(1)}, bf16[160,1024]{1,0:T(8,128)(2,1)}, u32[]{:S(2)}, u32[]{:S(2)}) collective-permute-start(bf16[160,1024]{1,0:T(8,128)(2,1)S(1)} %maximum_select_fusion.9), channel_id=1, source_target_pairs={{0,8},{4,12},{8,0},{12,4},{16,24},{20,28},{24,16},{28,20},{1,9},{5... | collective-permute-start | bytes 983048 | tf_op jit(solution)/shard_map/ppermute | solution.py:58
  509.6 18.0 %collective-permute-start.55 = (bf16[320,1024]{1,0:T(8,128)(2,1)}, bf16[320,1024]{1,0:T(8,128)(2,1)}, u32[]{:S(2)}, u32[]{:S(2)}) collective-permute-start(bf16[320,1024]{1,0:T(8,128)(2,1)} %maximum_select_fusion.4), channel_id=1, source_target_pairs={{0,4},{4,0},{8,12},{12,8},{16,20},{20,16},{24,28},{28,24},{1,5},{5... | collective-permute-start | bytes 1966088 | tf_op jit(solution)/shard_map/ppermute | solution.py:58
  514.4 22.4 %collective-permute-start.62 = (bf16[320,1024]{1,0:T(8,128)(2,1)}, bf16[320,1024]{1,0:T(8,128)(2,1)}, u32[]{:S(2)}, u32[]{:S(2)}) collective-permute-start(bf16[320,1024]{1,0:T(8,128)(2,1)} %maximum_select_fusion.5), channel_id=1, source_target_pairs={{0,4},{4,0},{8,12},{12,8},{16,20},{20,16},{24,28},{28,24},{1,5},{5... | collective-permute-start | bytes 1966088 | tf_op jit(solution)/shard_map/ppermute | solution.py:58
  (96 other events, 688.0 us)

commit v3 on v1

--- a/solution.py
+++ b/solution.py
@@ -20,6 +20,8 @@
 VMEM = pltpu.VMEM
 SMEM = pltpu.SMEM
 LIMIT = 60 << 20
+MESH = pl.DeviceIdType.MESH
+BACK_SPANS = [(0, 896), (896, 896)]
 
 
 def matdot(left, right, left_dim, right_dim):
@@ -59,27 +61,6 @@
 
 def add_low(left, right):
     return (left.astype(F32) + right.astype(F32)).astype(BF)
-
-
-def grp_bit(bit):
-    return (lax.axis_index("grp") // bit) % 2
-
-
-def halve(tensor, dim, bit):
-    side = grp_bit(bit)
-    half = tensor.shape[dim] // 2
-    send = lax.dynamic_slice_in_dim(tensor, (1 - side) * half, half, dim)
-    keep = lax.dynamic_slice_in_dim(tensor, side * half, half, dim)
-    return add_low(keep, exchange(send, "grp", bit))
-
-
-def grow(tensor, dim, bit):
-    other = exchange(tensor, "grp", bit)
-    return jnp.where(
-        grp_bit(bit) == 0,
-        jnp.concatenate([tensor, other], dim),
-        jnp.concatenate([other, tensor], dim),
-    )
 
 
 def bits_of(count):
@@ -183,13 +164,13 @@
     return jnp.concatenate([part, empty] if head == 0 else [empty, part], 0)
 
 
-def unroll(outs, rolled_ref, place, block):
+def unroll(outs, rolled_ref, my_row, offset, block):
     total = 4 * block
     rolled_ref[:, pl.ds(0, TILE)] = rolled_ref[:, pl.ds(total, TILE)]
-    back = roll_matrix(TILE - place[1])
+    back = roll_matrix(TILE - offset)
     for j, out in enumerate(outs):
         for part in range(block // TILE):
-            at = pl.multiple_of((place[0] ^ j) * block + part * TILE, TILE)
+            at = pl.multiple_of((my_row ^ j) * block + part * TILE, TILE)
             rows = matdot(back, rolled_ref[:, pl.ds(at, 2 * TILE)], 1, 1)
             out[part * TILE : (part + 1) * TILE, :] = rows.astype(BF)
 
@@ -232,7 +213,7 @@
     @pl.when(last)
     def _():
         run(LONGEST, total - LONGEST, seg_col[...] == seg_row[...])
-        unroll((o0, o1, o2, o3), rolled_ref, place, block)
+        unroll((o0, o1, o2, o3), rolled_ref, place[0], place[1], block)
 
 
 def attend(place, pair, qt, k, vt, seg_col, seg_row):
@@ -271,73 +252,264 @@
     )(place, qt, k, vt, seg_col, seg_row)
 
 
-def attend_back_kernel(
-    place, qt, k, kt, v, ot, lse, g0, g1, g2, g3, seg_col, seg_row, cos_t, sin_t,
-    rolled_out, bias_out, s0, s1, s2, s3,
-    grad_rows, grad_t, row_dots, dqt, dkt, dvt, nat_ref,
+def back_kernel(
+    n_grp, place, qt, k, kt, v, ot0, ot1, lse0, lse1, seg_col, seg_row, cos_t, sin_t,
+    early_in, member, member_t, scale_rows,
+    g0, g1, g2, g3, mixed_hbm, packed_hbm, wq_hbm, wk_hbm, wv_hbm, frames_hbm, middle_hbm,
+    frames_grad, upper_out, lower_out, qg0, qg1, early_out, late_out,
+    grad_t, row_dots, dqt, dkt, dvt, nat_ref, rolled, mixed, packed, weights, frames, middle,
+    from_x, lower_x, dw, send_d, got_d, early_got, late_got, summed_low, summed_up, summed_q, q_extra,
+    send_sem, recv_sem, load_sem,
 ):
-    step = pl.program_id(0)
+    my_row, my_grp = lax.axis_index("row"), lax.axis_index("grp")
     total = k.shape[0]
     block = total // 4
     steps = total // TILE
-    last = step == steps - 1
     half = HEAD_DIM // 2
-
-    @pl.when(step == 0)
-    def _():
-        for j, source in enumerate((g0, g1, g2, g3)):
-            at = pl.multiple_of((place[0] ^ j) * block, block)
-            grad_rows[pl.ds(at, block), :] = source[...]
-        grad_rows[pl.ds(total, TILE), :] = grad_rows[pl.ds(0, TILE), :]
-        dkt[...] = jnp.zeros_like(dkt)
-        dvt[...] = jnp.zeros_like(dvt)
-
-        ahead = roll_matrix(place[1])
-
-        def turn(i, carry):
-            cols = pl.ds(pl.multiple_of(i * TILE, TILE), TILE)
-            two = grad_rows[pl.ds(pl.multiple_of(i * TILE, TILE), 2 * TILE), :]
-            part = matdot(ahead, two, 1, 0).T
-            grad_t[:, cols] = part.astype(BF)
-            crossed = part * ot[:, cols].astype(F32)
-            row_dots[0:1, cols] = jnp.sum(crossed[:HEAD_DIM], axis=0, keepdims=True)
-            row_dots[1:2, cols] = jnp.sum(crossed[HEAD_DIM:], axis=0, keepdims=True)
-            return carry
-
-        lax.fori_loop(0, steps, turn, 0)
-
-    here = pl.ds(pl.multiple_of(step * TILE, TILE), TILE)
-
-    def run(first, count, allowed):
-        keys = pl.ds(first, count)
+    bits = bits_of(n_grp)
+    halving, extra = bits[:3], bits[3:]
+    side = lambda bit: (my_grp // bit) % 2
+    by_row = lambda j: {"row": my_row ^ j}
+    by_grp = lambda bit: {"grp": my_grp ^ bit}
+    cut = from_x.shape[0]
+    low_rows = packed.shape[1] - cut
+
+    numbers = {}
+
+    def remote(name, src, dst, device):
+        number = numbers.setdefault(name, len(numbers))
+        return pltpu.make_async_remote_copy(
+            src, dst, send_sem.at[number], recv_sem.at[number], device_id=device, device_id_type=MESH
+        )
+
+    sent = {}
+
+    class Copy:
+        def __init__(self, name, parts):
+            self.describe = lambda: remote(name, *parts())
+            self.start = lambda: self.describe().start()
+            self.wait_recv = lambda: self.describe().wait_recv()
+            self.wait_send = lambda: self.describe().wait_send()
+            self.wait = lambda: self.describe().wait()
+
+    def start(name, parts):
+        sent[name] = Copy(name, parts)
+        sent[name].start()
+
+    def regions(size):
+        out = [(0, size)]
+        for bit in halving:
+            offset, size = out[-1]
+            out.append((offset + side(bit) * (size // 2), size // 2))
+        return out
+
+    def away(region, bit):
+        offset, size = region
+        return pl.ds(pl.multiple_of(offset + (1 - side(bit)) * (size // 2), 16), size // 2)
+
+    def at(region):
+        return pl.ds(pl.multiple_of(region[0], 16), region[1])
+
+    loads = [
+        pltpu.make_async_copy(src, dst, load_sem.at[i])
+        for i, (src, dst) in enumerate(
+            (
+                (packed_hbm, packed),
+                (mixed_hbm, mixed),
+                (wq_hbm, mixed.at[pl.ds(0, D)]),
+                (wk_hbm, mixed.at[pl.ds(D, D)]),
+                (wv_hbm, weights),
+                (frames_hbm, frames),
+                (middle_hbm, middle),
+            )
+        )
+    ]
+    for load in loads[:1] + loads[4:]:
+        load.start()
+
+    barrier = pltpu.get_barrier_semaphore()
+    for device in [by_row(j) for j in (1, 2, 3)] + [by_grp(bit) for bit in bits]:
+        pl.semaphore_signal(barrier, inc=1, device_id=device, device_id_type=MESH)
+    pl.semaphore_wait(barrier, 3 + len(bits))
+
+    up_at, low_at = regions(cut), [(cut + o, s) for o, s in regions(low_rows)]
+    q_at = regions(256)
+
+    def upper_x():
+        start("a0", lambda: (packed_hbm.at[1, pl.ds(0, cut)], from_x, by_row(2)))
+
+    def upper_x_done():
+        loads[0].wait()
+        sent["a0"].wait_recv()
+        packed[0, :cut] = add_low(packed[0, :cut], from_x[...])
+
+    def upper_send(i):
+        start(f"a{i + 1}", lambda i=i: (packed.at[0, away(up_at[i], halving[i])], summed_up.at[at((cut - 2 * up_at[i + 1][1], up_at[i + 1][1]))], by_grp(halving[i])))
+
+    def upper_take(i):
+        sent[f"a{i + 1}"].wait_recv()
+        mine, size = at(up_at[i + 1]), up_at[i + 1][1]
+        got = summed_up[cut - 2 * size : cut - size]
+        packed[0, mine] = add_low(packed[0, mine], got)
+
+    def lower_send(i):
+        source = packed_hbm if i == 0 else packed
+        size = low_at[i + 1][1]
+        start(f"b{i + 1}", lambda i=i, size=size, source=source: (source.at[:, away(low_at[i], halving[i])], summed_low.at[:, at((low_rows - 2 * size, size))], by_grp(halving[i])))
+
+    def lower_take(i):
+        sent[f"b{i + 1}"].wait_recv()
+        mine, size = at(low_at[i + 1]), low_at[i + 1][1]
+        got = summed_low[:, low_rows - 2 * size : low_rows - size]
+        packed[:, mine] = add_low(packed[:, mine], got)
+
+    def whole_sum(name, ref, region, first):
+        for number, bit in enumerate(extra):
+            start(f"{name}{number}", lambda bit=bit, number=number, ref=ref, region=region: (ref.at[at(region)], lower_x.at[first + number], by_grp(bit)))
+            sent[f"{name}{number}"].wait()
+            ref[at(region)] = add_low(ref[at(region)], lower_x[first + number])
+
+    def lower_x_send():
+        start("bx", lambda: (packed.at[1, at(low_at[-1])], lower_x.at[0], by_row(2)))
+
+    def lower_x_take():
+        sent["bx"].wait_recv()
+        packed[0, at(low_at[-1])] = add_low(packed[0, at(low_at[-1])], lower_x[0])
+
+    def spread_send(name, ref, areas, i):
+        part = at(areas[i + 1])
+        start(f"{name}{i}", lambda i=i, part=part, ref=ref: (ref.at[part], ref.at[part], by_grp(halving[i])))
+
+    def spread_take(name, i):
+        sent[f"{name}{i}"].wait_recv()
+
+    lower_areas = regions(low_rows)
+
+    def upper_own():
+        whole_sum("ax", packed.at[0], up_at[-1], 1)
+        upper_out[at(up_at[-1])] = packed[0, at(up_at[-1])]
+
+    def lower_own():
+        whole_sum("by", packed.at[0], low_at[-1], 1 + len(extra))
+        lower_out[at(lower_areas[-1])] = packed[0, at(low_at[-1])]
+
+    q_out = (qg0, qg1)
+
+    def heads_send(pair, i):
+        size = q_at[i + 1][1]
+        start(f"q{pair}{i}", lambda i=i, pair=pair, size=size: (dw.at[pair, :, away(q_at[i], halving[i])], summed_q.at[pair, :, at((256 - 2 * size, size))], by_grp(halving[i])))
+
+    def heads_take(pair, i):
+        sent[f"q{pair}{i}"].wait_recv()
+        mine, size = at(q_at[i + 1]), q_at[i + 1][1]
+        got = summed_q[pair, :, 256 - 2 * size : 256 - size]
+        dw[pair, :, mine] = add_low(dw[pair, :, mine], got)
+
+    def heads_shard_send(pair):
+        part, size = at(q_at[-1]), q_at[-1][1]
+        for number, bit in enumerate(extra):
+            name, slot = f"qe{pair}{number}", 4 * (pair * len(extra) + number)
+            landing = q_extra.at[pl.ds(slot, 4)]
+            start(name, lambda: (dw.at[pair, :, part], landing, by_grp(bit)))
+            sent[name].wait()
+            dw[pair, :, part] = add_low(dw[pair, :, part], q_extra[slot : slot + 4])
+        q_out[pair][0, part] = dw[pair, my_row, part]
+        for j in (1, 2, 3):
+            start(f"qs{pair}{j}", lambda j=j, pair=pair, part=part: (dw.at[pair, my_row ^ j, part], q_out[pair].at[j, part], by_row(j)))
+
+    def heads_shard_take(pair):
+        for j in (1, 2, 3):
+            sent[f"qs{pair}{j}"].wait_recv()
+
+    def heads_spread_send(pair, i):
+        part = at(q_at[i + 1])
+        ref = q_out[pair]
+        start(f"qg{pair}{i}", lambda i=i, part=part, ref=ref: (ref.at[:, part], ref.at[:, part], by_grp(halving[i])))
+
+    def heads_spread_take(pair, i):
+        sent[f"qg{pair}{i}"].wait_recv()
+
+    def row_sum_send(name, got):
+        for j in (1, 2, 3):
+            start(f"{name}{j}", lambda j=j: (got.at[my_row], got.at[my_row], by_row(j)))
+
+    def row_sum_take(name, got):
+        for j in (1, 2, 3):
+            sent[f"{name}{j}"].wait_recv()
+        return (got[0] + got[1]) + (got[2] + got[3])
+
+    def fold(sums):
+        width = sums.shape[1] // 2
+        return jnp.concatenate([sums[:, :width], sums[:, width:]], 0).astype(BF)
+
+    def gather_send(name, ref, i):
+        start(f"{name}{i}", lambda i=i, ref=ref: (ref.at[pl.ds(0, 1 << i)], ref.at[pl.ds(1 << i, 1 << i)], by_grp(bits[i])))
+
+    def gather_take(name, i):
+        sent[f"{name}{i}"].wait_recv()
+
+    def early_fold():
+        early_out[0] = fold(row_sum_take("es", early_got))
+
+    upper_x()
+    lower_send(0)
+    early_got[my_row] = early_in[...]
+    row_sum_send("es", early_got)
+
+    lanes_of = slice(0, 256)
+    for j, source in enumerate((g0, g1, g2, g3)):
+        mixed[pl.ds(pl.multiple_of((my_row ^ j) * block, block), block), lanes_of] = source[...]
+    ahead = roll_matrix(place[1])
+
+    def turn(i, carry):
+        cols = pl.ds(pl.multiple_of(i * TILE, TILE), TILE)
+        after = pl.ds(pl.multiple_of((i + 1) % steps * TILE, TILE), TILE)
+        part = matdot(ahead[:, :TILE], mixed[cols, lanes_of], 1, 0)
+        part = (part + matdot(ahead[:, TILE:], mixed[after, lanes_of], 1, 0)).T
+        grad_t[:, cols] = part.astype(BF)
+        for head in range(4):
+            mine = slice((head % 2) * HEAD_DIM, (head % 2 + 1) * HEAD_DIM)
+            crossed = part[head * HEAD_DIM : (head + 1) * HEAD_DIM] * (ot0, ot1)[head // 2][
+                mine, cols
+            ].astype(F32)
+            row_dots[head : head + 1, cols] = jnp.sum(crossed, axis=0, keepdims=True)
+        return carry
+
+    lax.fori_loop(0, steps, turn, 0)
+    loads[1].start()
+
+    def run(pair, here, spans, allowed):
+        lanes = slice(pair * 128, (pair + 1) * 128)
+        lse = (lse0, lse1)[pair]
         for head in range(2):
             mine = slice(head * HEAD_DIM, (head + 1) * HEAD_DIM)
-            scores = matdot(k[keys, :], one_head(qt[:, here], head), 1, 0)
-            if allowed is not None:
-                scores = jnp.where(allowed, scores, -1e30)
-            probs = jnp.exp(scores - lse[head : head + 1, here])
-            grad_probs = matdot(v[keys, :], one_head(grad_t[:, here], head), 1, 0)
-            grad_scores = (probs * (grad_probs - row_dots[head : head + 1, here])).astype(BF)
-            dqt[mine, here] = matdot(kt[mine, keys], grad_scores, 1, 0) * HEAD_DIM**-0.5
-            dkt[mine, keys] += matdot(qt[mine, here], grad_scores, 1, 1)
-            dvt[mine, keys] += matdot(grad_t[mine, here], probs.astype(BF), 1, 1)
-
-    @pl.when(jnp.logical_not(last))
-    def _():
-        run(0, LONGEST, None)
-
-    @pl.when(last)
-    def _():
-        run(LONGEST, total - LONGEST, seg_col[...] == seg_row[...])
-
-        def finish(i, sums):
+            wide = slice(pair * 128 + head * HEAD_DIM, pair * 128 + (head + 1) * HEAD_DIM)
+            dots = slice(2 * pair + head, 2 * pair + head + 1)
+            grad_query = None
+            for first, count in spans:
+                keys = pl.ds(first, count)
+                scores = matdot(k[keys, lanes], one_head(qt[lanes, here], head), 1, 0)
+                if allowed is not None:
+                    scores = jnp.where(allowed, scores, -1e30)
+                probs = jnp.exp(scores - lse[head : head + 1, here])
+                grad_probs = matdot(v[keys, lanes], one_head(grad_t[lanes, here], head), 1, 0)
+                grad_scores = (probs * (grad_probs - row_dots[dots, here])).astype(BF)
+                part = matdot(kt[wide, keys], grad_scores, 1, 0)
+                grad_query = part if grad_query is None else grad_query + part
+                dkt[mine, keys] += matdot(qt[wide, here], grad_scores, 1, 1)
+                dvt[mine, keys] += matdot(grad_t[wide, here], probs.astype(BF), 1, 1)
+            dqt[mine, here] = grad_query * HEAD_DIM**-0.5
+
+    def finish(pair):
+        def part(i, sums):
             cols = pl.ds(pl.multiple_of(i * TILE, TILE), TILE)
             cosine, sine = cos_t[:, cols], sin_t[:, cols]
 
             def turned(ref):
                 parts = []
-                for at in range(0, 128, HEAD_DIM):
-                    first, second = ref[at : at + half, cols], ref[at + half : at + HEAD_DIM, cols]
+                for at_row in range(0, 128, HEAD_DIM):
+                    first = ref[at_row : at_row + half, cols]
+                    second = ref[at_row + half : at_row + HEAD_DIM, cols]
                     parts.append(first * cosine + second * sine)
                     parts.append(second * cosine - first * sine)
                 return jnp.concatenate(parts, 0)
@@ -345,61 +517,208 @@
             columns = jnp.concatenate([turned(dqt), turned(dkt), dvt[:, cols]], 0)
             nat_ref[:, pl.ds(pl.multiple_of(TILE + i * TILE, TILE), TILE)] = columns.astype(BF)
             low = columns.T.astype(BF)
-            rolled_out[cols, :] = low
+            rolled[cols, :] = low
             return sums + jnp.sum(low.astype(F32), axis=0, keepdims=True)
 
-        sums = lax.fori_loop(0, steps, finish, jnp.zeros((1, 384), F32))
-        bias_out[...] = jnp.broadcast_to(sums, bias_out.shape)
-        unroll((s0, s1, s2, s3), nat_ref, place, block)
-
-
-def attend_back(place, pair, qt, k, kt, v, ot, lse, grads, seg_col, seg_row, cos_t, sin_t):
+        sums = lax.fori_loop(0, steps, part, jnp.zeros((1, 384), F32))
+        if pair == 1:
+            for j in (1, 2, 3):
+                sent[f"d0{j}"].wait_send()
+        outs = [got_d.at[my_row, pair]] + [send_d.at[j] for j in range(3)]
+        unroll(outs, nat_ref, my_row, place[1], block)
+        for j in (1, 2, 3):
+            start(f"d{pair}{j}", lambda j=j, pair=pair: (send_d.at[j - 1], got_d.at[my_row, pair], by_row(j)))
+        if pair == 0:
+            loads[1].wait()
+        for shard in range(4):
+            columns = mixed[:, shard * 256 : (shard + 1) * 256]
+            dw[pair, shard] = contract_rows(columns, rolled[...]).astype(BF)
+        heads_send(pair, 0)
+        return sums
+
+    bias_sums = []
+    hooks = (
+        {
+            2: lambda: (early_fold(), gather_send("eg", early_out, 0)),
+            4: lambda: (gather_take("eg", 0), gather_send("eg", early_out, 1)),
+            6: lambda: (gather_take("eg", 1), gather_send("eg", early_out, 2)),
+        },
+        {
+            0: lambda: (upper_x_done(), upper_send(0)),
+            1: lambda: (lower_take(0), lower_send(1)),
+            4: lambda: (heads_take(0, 0), heads_send(0, 1)),
+            5: lambda: (upper_take(0), upper_send(1)),
+            6: lambda: (lower_take(1), lower_send(2)),
+        },
+    )
+    for pair in range(2):
+        dkt[...] = jnp.zeros_like(dkt)
+        dvt[...] = jnp.zeros_like(dvt)
+
+        def tile(i, carry):
+            run(pair, pl.ds(pl.multiple_of(i * TILE, TILE), TILE), BACK_SPANS, None)
+            for when, hook in hooks[pair].items():
+                pl.when(i == when)(lambda: (hook(), None)[1])
+            return carry
+
+        lax.fori_loop(0, steps - 1, tile, 0)
+        tail = total - LONGEST
+        run(pair, pl.ds(LONGEST, tail), [(LONGEST, tail)], seg_col[...] == seg_row[...])
+        bias_sums.append(finish(pair))
+
+    for load in loads[2:4]:
+        load.start()
+    for number in range(2, len(bits)):
+        gather_take("eg", number)
+        if number + 1 < len(bits):
+            gather_send("eg", early_out, number + 1)
+    heads_take(0, 1), heads_send(0, 2)
+    upper_take(1), upper_send(2)
+    lower_take(2), lower_x_send()
+    heads_take(0, 2), heads_shard_send(0)
+    upper_take(2), upper_own(), spread_send("ag", upper_out, up_at, 2)
+    heads_take(1, 0), heads_send(1, 1)
+    lower_x_take(), lower_own(), spread_send("bg", lower_out, lower_areas, 2)
+    heads_shard_take(0), heads_spread_send(0, 2)
+
+    for pair in range(2):
+        for j in (1, 2, 3):
+            sent[f"d{pair}{j}"].wait_recv()
+    for load in loads[2:]:
+        load.wait()
+    late = jnp.zeros((8, 2 * D), F32)
+    for part in range(block // TILE):
+        rows = slice(part * TILE, (part + 1) * TILE)
+        grad = jnp.zeros((TILE, D), F32)
+        for kind in range(3):
+            pieces = [
+                got_d[owner, pair, rows, kind * 128 : (kind + 1) * 128]
+                for owner in range(4)
+                for pair in range(2)
+            ]
+            weight = weights[...] if kind == 2 else mixed[kind * D : (kind + 1) * D]
+            grad = grad + against(jnp.concatenate(pieces, 1), weight)
+        normed, factor = normalize(frames[rows, :].astype(F32))
+        scale = jnp.ones((TILE, D), F32)
+        for u in range(scale_rows.shape[0]):
+            scale = scale + member[rows, u : u + 1] * scale_rows[u : u + 1, :]
+        back = normalize_back(grad * scale, normed, factor)
+        frames_grad[rows, :] = (middle[rows, :] + back).astype(BF)
+        late = late + lax.dot_general(
+            member_t[:, rows],
+            jnp.concatenate([grad, grad * normed], 1),
+            (((1,), (0,)), ((), ())),
+            precision=highest,
+            preferred_element_type=F32,
+        )
+    late_got[my_row] = late
+    row_sum_send("ls", late_got)
+    heads_take(1, 1), heads_send(1, 2)
+    spread_take("ag", 2), spread_send("ag", upper_out, up_at, 1)
+    spread_take("bg", 2), spread_send("bg", lower_out, lower_areas, 1)
+    heads_spread_take(0, 2), heads_spread_send(0, 1)
+    late_sum = row_sum_take("ls", late_got)
+    widths = [slice(kind * 128, (kind + 1) * 128) for kind in range(3)]
+    bias_row = jnp.concatenate(
+        [bias_sums[pair][:, w] for w in widths for pair in range(2)]
+        + [jnp.zeros((1, 2 * D - 768), F32)],
+        1,
+    )
+    index = lax.broadcasted_iota(jnp.int32, (8, 2 * D), 0)
+    late_out[0] = fold(jnp.where(index == 4, bias_row, late_sum))
+    gather_send("lg", late_out, 0)
+    heads_take(1, 2), heads_shard_send(1)
+    gather_take("lg", 0), gather_send("lg", late_out, 1)
+    heads_shard_take(1), heads_spread_send(1, 2)
+    spread_take("ag", 1), spread_send("ag", upper_out, up_at, 0)
+    spread_take("bg", 1), spread_send("bg", lower_out, lower_areas, 0)
+    gather_take("lg", 1), gather_send("lg", late_out, 2)
+    heads_spread_take(0, 1), heads_spread_send(0, 0)
+    heads_spread_take(1, 2), heads_spread_send(1, 1)
+    for number in range(2, len(bits)):
+        gather_take("lg", number)
+        if number + 1 < len(bits):
+            gather_send("lg", late_out, number + 1)
+    heads_spread_take(1, 1), heads_spread_send(1, 0)
+    spread_take("ag", 0)
+    spread_take("bg", 0)
+    heads_spread_take(0, 0)
+    heads_spread_take(1, 0)
+    waited = {f"{name}{i}" for name in ("ax", "by", "qe0", "qe1") for i in range(len(extra))}
+    waited |= {"d01", "d02", "d03"}
+    for name, copy in sent.items():
+        if name not in waited:
+            copy.wait_send()
+
+
+def attend_back(
+    n_grp, place, qt, k, kt, v, heads_t, lse, seg_col, seg_row, cos_t, sin_t, early, member, member_t,
+    scale_rows, grads, mixed, packed, weights, frames, middle,
+):
     total = k.shape[0]
     block = total // 4
-    whole = lambda a: pl.BlockSpec(a.shape, lambda i: (0, 0))
-    wide = pl.BlockSpec((128, total), lambda i: (pair, 0))
-    tall = pl.BlockSpec((total, 128), lambda i: (0, pair))
+    rows = packed.shape[1]
+    cut = rows // 2
+    extra = max(0, len(bits_of(n_grp)) - 3)
+    inputs = [
+        qt, k, kt, v, *heads_t, *lse, seg_col, seg_row, cos_t, sin_t, early, member, member_t, scale_rows,
+        *grads,
+    ]
+    far = [mixed, packed, *weights, frames, middle]
+    copies = 100
     return pl.pallas_call(
-        attend_back_kernel,
-        grid=(total // TILE,),
+        functools.partial(back_kernel, n_grp),
         out_shape=[
-            jax.ShapeDtypeStruct((total, 384), BF),
-            jax.ShapeDtypeStruct((8, 384), F32),
-        ]
-        + [jax.ShapeDtypeStruct((block, 384), BF)] * 4,
-        in_specs=[
-            pl.BlockSpec(memory_space=SMEM),
-            wide,
-            tall,
-            wide,
-            tall,
-            whole(ot),
-            whole(lse),
-        ]
-        + [whole(g) for g in grads]
-        + [whole(seg_col), whole(seg_row), whole(cos_t), whole(sin_t)],
-        out_specs=[
-            pl.BlockSpec((total, 384), lambda i: (0, 0)),
-            pl.BlockSpec((8, 384), lambda i: (0, 0)),
-        ]
-        + [pl.BlockSpec((block, 384), lambda i: (0, 0))] * 4,
+            jax.ShapeDtypeStruct((block, D), BF),
+            jax.ShapeDtypeStruct((cut, D), BF),
+            jax.ShapeDtypeStruct((rows - cut, D), BF),
+            jax.ShapeDtypeStruct((4, 256, 384), BF),
+            jax.ShapeDtypeStruct((4, 256, 384), BF),
+            jax.ShapeDtypeStruct((n_grp, 16, 2 * D), BF),
+            jax.ShapeDtypeStruct((n_grp, 16, D), BF),
+        ],
+        in_specs=[pl.BlockSpec(memory_space=SMEM)]
+        + [pl.BlockSpec(memory_space=VMEM)] * len(inputs)
+        + [pl.BlockSpec(memory_space=pl.ANY)] * len(far),
+        out_specs=[pl.BlockSpec(memory_space=VMEM)] * 7,
         scratch_shapes=[
-            VMEM((total + TILE, 128), BF),
-            VMEM((128, total), BF),
+            VMEM((256, total), BF),
             VMEM((8, total), F32),
             VMEM((128, total), F32),
             VMEM((128, total), F32),
             VMEM((128, total), F32),
             VMEM((384, total + TILE), BF),
+            VMEM((total, 384), BF),
+            VMEM((total, D), BF),
+            VMEM((2, rows, D), BF),
+            VMEM((D, D), BF),
+            VMEM((block, D), BF),
+            VMEM((block, D), F32),
+            VMEM((cut, D), BF),
+            VMEM((1 + 2 * extra, (rows - cut) // 8, D), BF),
+            VMEM((2, 4, 256, 384), BF),
+            VMEM((3, block, 384), BF),
+            VMEM((4, 2, block, 384), BF),
+            VMEM((4, 8, 4 * D), F32),
+            VMEM((4, 8, 2 * D), F32),
+            VMEM((2, rows - cut, D), BF),
+            VMEM((cut, D), BF),
+            VMEM((2, 4, 256, 384), BF),
+            VMEM((max(1, 8 * extra), 32, 384), BF),
+            pltpu.SemaphoreType.DMA((copies,)),
+            pltpu.SemaphoreType.DMA((copies,)),
+            pltpu.SemaphoreType.DMA((len(far),)),
         ],
-        compiler_params=pltpu.CompilerParams(vmem_limit_bytes=LIMIT),
+        compiler_params=pltpu.CompilerParams(
+            vmem_limit_bytes=62 << 20, collective_id=1, has_side_effects=True
+        ),
         cost_estimate=pl.CostEstimate(
-            flops=2 * 2 * 5 * total * LONGEST * 256,
-            bytes_accessed=8 << 20,
-            transcendentals=2 * total * LONGEST,
+            flops=4 * 2 * 5 * total * LONGEST * 256,
+            bytes_accessed=40 << 20,
+            transcendentals=4 * total * LONGEST,
         ),
         name="attend_back",
-    )(place, qt, k, kt, v, ot, lse, *grads, seg_col, seg_row, cos_t, sin_t)
+    )(place, *inputs, *far)
 
 
 def weight_grad_kernel(place, o, h, a, e_att, e_z, e_b, out):
@@ -478,21 +797,11 @@
     _, member, _ = layout(own_rows)
 
     col_part = lambda w, j: lax.dynamic_slice_in_dim(w, (my_row ^ j) * width, width, 1)
-    q_parts, k_parts, v_parts = (
-        [col_part(w, j) for j in range(4)] for w in (query_weight, key_weight, value_weight)
-    )
-    weight_t = jnp.concatenate([q_parts[0].T, k_parts[0].T, v_parts[0].T], 0)
+    weight_t = jnp.concatenate(
+        [col_part(w, 0).T for w in (query_weight, key_weight, value_weight)], 0
+    )
     own_part = lambda b: lax.dynamic_slice_in_dim(b, my_row * width, width, 0)
     bias_t = jnp.concatenate([own_part(query_bias), own_part(key_bias), own_part(value_bias)])[:, None]
-    back_weight = jnp.concatenate(
-        [
-            part[j][:, pair * 128 : (pair + 1) * 128]
-            for pair in range(2)
-            for j in range(4)
-            for part in (q_parts, k_parts, v_parts)
-        ],
-        1,
-    )
     out_perm = jnp.concatenate(
         [lax.dynamic_slice_in_dim(out_weight, (my_row ^ j) * width, width, 0) for j in range(4)], 0
     )
@@ -543,99 +852,57 @@
     grad_gate_attn = grad_middle * attended
     grad_heads = against(grad_attended, out_perm).astype(BF)
 
-    grad_pieces = []
-    for pair in range(2):
-        cut = [
-            grad_heads[:, j * width + pair * 128 : j * width + pair * 128 + 128] for j in range(4)
-        ]
-        grad_pieces.append([cut[0]] + [exchange(cut[j], "row", j) for j in range(1, 4)])
+    cut = [grad_heads[:, j * width : (j + 1) * width] for j in range(4)]
+    grad_pieces = [cut[0]] + [exchange(cut[j], "row", j) for j in range(1, 4)]
 
     operands = (attn_low, ffn_in, active_low, grad_attended, grad_hidden, grad_branch)
     to_core = exchange(weight_grads(place, (1, 3), *operands), "row", 1)
     packed = add_low(weight_grads(place, (0, 2), *operands), to_core)
-    cut_row = packed.shape[1] // 2
-    upper = add_low(packed[0, :cut_row], exchange(packed[1, :cut_row], "row", 2))
-    lower = packed[:, cut_row:]
-    for bit in bits_of(n_grp):
-        upper = halve(upper, 0, bit)
-        lower = halve(lower, 1, bit)
-    lower = add_low(lower[0], exchange(lower[1], "row", 2))
-    for bit in reversed(bits_of(n_grp)):
-        upper = grow(upper, 0, bit)
-        lower = grow(lower, 0, bit)
+
+    early = lax.dot_general(
+        member,
+        jnp.concatenate([grad_gate_attn, grad_ffn_in, grad_scale_ffn, grad_gate_ffn], 1),
+        (((0,), (0,)), ((), ())),
+        precision=highest,
+        preferred_element_type=F32,
+    )
+    ffn_bias = jnp.concatenate(
+        [column_sum(grad_attended), column_sum(grad_hidden), column_sum(grad_branch)]
+    )
+    early = jnp.concatenate([early, ffn_bias[None], jnp.zeros((3, 4 * D), F32)], 0)
+    pad = ((0, 0), (0, 4))
+    member_8 = jnp.pad(member, pad)
+    grad_frames, upper, lower, heads_0, heads_1, early_all, late_all = attend_back(
+        n_grp, place, qt, k_rows, kt, v_rows, heads_t, log_totals, seg_col, seg_row, cos_t, sin_t,
+        early, member_8, member_8.T, modulation[:, D : 2 * D], grad_pieces, mixed, packed,
+        (query_weight, key_weight, value_weight), frames, grad_middle,
+    )
+
     packed_total = jnp.concatenate([upper, lower], 0).astype(F32)
     out_grad = packed_total[:256]
     up_grad = jnp.concatenate([packed_total[256:512], packed_total[512:768]], 1)
     down_grad = packed_total[768:]
-
-    back_pieces, qkv_grads, qkv_bias = [], [], []
-    for pair in range(2):
-        rolled, sums, *outs = attend_back(
-            place, pair, qt, k_rows, kt, v_rows, heads_t[pair], log_totals[pair], grad_pieces[pair],
-            seg_col, seg_row, cos_t, sin_t,
-        )
-        back_pieces += [outs[0]] + [exchange(outs[j], "row", j) for j in range(1, 4)]
-        qkv_bias.append(sums[0].reshape(3, 128))
-        total = contract_rows(mixed, rolled).astype(BF).reshape(4, width, 384)
-        for bit in bits_of(n_grp):
-            total = halve(total, 1, bit)
-        shard = lambda j: lax.dynamic_index_in_dim(total, my_row ^ j, 0, keepdims=False)
-        total = jnp.stack([shard(0)] + [exchange(shard(j), "row", j) for j in range(1, 4)])
-        for bit in reversed(bits_of(n_grp)):
-            total = grow(total, 1, bit)
-        qkv_grads.append(total)
-    by_owner = jnp.stack(qkv_grads)[:, my_row ^ jnp.arange(4)]
+    by_owner = jnp.stack([heads_0, heads_1])[:, my_row ^ jnp.arange(4)]
     qkv_full = by_owner.transpose(2, 1, 0, 3).reshape(width, 4, 2, 3, 128).astype(F32)
     query_grad, key_grad, value_grad = (qkv_full[:, :, :, i].reshape(width, D) for i in range(3))
 
-    grad_mixed_in = against(jnp.concatenate(back_pieces, 1), back_weight)
-    grad_frames = grad_middle + normalize_back(
-        grad_mixed_in * (1.0 + scale_attn), normed_attn, factor_attn
-    )
-
-    def by_utterance(parts):
-        return lax.dot_general(
-            member,
-            jnp.concatenate(parts, 1),
-            (((0,), (0,)), ((), ())),
-            precision=highest,
-            preferred_element_type=F32,
-        )
-
-    def group_sum(tensor):
-        for bit in (1, 2):
-            tensor = tensor + exchange(tensor, "row", bit)
-        return tensor
-
-    late = group_sum(by_utterance([grad_mixed_in, grad_mixed_in * normed_attn]))
-    early = group_sum(
-        by_utterance([grad_gate_attn, grad_ffn_in, grad_scale_ffn, grad_gate_ffn])
-    )
-    grad_modulation = jnp.concatenate([late, early], 1).astype(BF)
-    grad_activated = against(grad_modulation, mod_weight)
+    unfold = lambda t: jnp.concatenate([t[:, :8], t[:, 8:]], 2)
+    late_all, early_all = unfold(late_all), unfold(early_all)
+    mod_all = jnp.concatenate([late_all[:, :4], early_all[:, :4]], 2)
+    grad_activated = against(mod_all[0], mod_weight)
     _, silu_pull = jax.vjp(jax.nn.silu, embedding)
     grad_embedding = silu_pull(grad_activated)[0]
-    mod_all = grad_modulation
-    for bit in bits_of(n_grp):
-        mod_all = jnp.concatenate([mod_all, exchange(mod_all, "grp", bit)], 0)
+    mod_all = mod_all.reshape(n_grp * 4, 6 * D)
     act_slice = lax.dynamic_slice_in_dim(act_all, my_row * width, width, 1)
     mod_weight_grad = contract_rows(act_slice, mod_all)
     mod_bias_grad = lax.dynamic_slice_in_dim(column_sum(mod_all), my_row * 6 * width, 6 * width, 0)
-
-    ffn_bias = group_sum(
-        jnp.concatenate([column_sum(grad_attended), column_sum(grad_hidden), column_sum(grad_branch)])
-    )
+    ffn_bias = column_sum(early_all[:, 4])
     mine = lambda start, size: lax.dynamic_slice_in_dim(ffn_bias, start + my_row * size, size, 0)
-    qkv_sum = jnp.stack(qkv_bias, 1).reshape(3 * width)
-    biases = jnp.concatenate([qkv_sum, mine(0, width), mine(D, 2 * width), mine(3 * D, width)])
-    for bit in bits_of(n_grp):
-        biases = biases + exchange(biases, "grp", bit)
-    query_b, key_b, value_b, out_b, up_b, down_b = jnp.split(
-        biases, [width, 2 * width, 3 * width, 4 * width, 6 * width]
-    )
+    out_b, up_b, down_b = mine(0, width), mine(D, 2 * width), mine(3 * D, width)
+    query_b, key_b, value_b = jnp.split(column_sum(late_all[:, 4, : 3 * width]), 3)
     return (
         output,
-        grad_frames.astype(BF),
+        grad_frames,
         grad_embedding[None],
         mod_weight_grad,
         mod_bias_grad,

time: 539 us -> 435 us (0.81)
  waiting for transfers between devices: 159 us -> 10.8 us
  Pallas kernels: 126 us -> 259 us
  starting transfers between devices: 53.1 us -> 16.4 us
  local copies, waits for them, and re-layouts: 68.5 us -> 32.9 us
  other arithmetic: 49.4 us -> 38.8 us
    ppermute x69 -> x16, waiting for transfers between devices: 159 us -> 10.8 us  [exchange(): return lax.ppermute(tensor, axis, [(i, i ^ bit) for i in range(size)])]
    pallas_call x2 -> x1, Pallas kernels: 54.5 us -> 187 us  [attend_back(): pl.pallas_call(functools.partial(back_kernel, n_grp), out_shape=[jax.Shap...]
    ppermute x69 -> x16, starting transfers between devices: 53.1 us -> 16.4 us  [exchange(): return lax.ppermute(tensor, axis, [(i, i ^ bit) for i in range(size)])]
    unnamed x219 -> x120, local copies, waits for them, and re-layouts: 41.5 us -> 11.2 us
    select_n x13 -> x1, other arithmetic: 11.3 us -> 0.01 us  [local(): by_owner = jnp.stack([heads_0, heads_1])[:, my_row ^ jnp.arange(4)]]
    slice x6 -> x4, local copies, waits for them, and re-layouts: 8.52 us -> 2.07 us  [the longest x1 0.78 us: local(): cut = [grad_heads[:, j * width:(j + 1) * width] for j in range(4)]]
    dot_general x8 -> x5, matrix products: 34.3 us -> 30 us  [matdot(): lax.dot_general(left, right, (((left_dim,), (right_dim,)), ((), ())), pre...]
  transfers between devices with their start and end apart: 69 -> 16, of which waited for: 31 -> 6; matrix products, arithmetic and copies ran while one was open for 25% -> 22% of each run, Pallas kernels for 12% -> 46%
where the time goes in v3:
time: 435 us; the launch traced here: 426 us
  Pallas kernels  259 us (60%)
  matrix products  64.4 us (15%)
  other arithmetic  38.8 us (9%)
  local copies, waits for them, and re-layouts  32.9 us (8%)
  starting transfers between devices  16.4 us (4%)
  waiting for transfers between devices  10.8 us (2%)
    pallas_call x1, Pallas kernels, attend_back(): pl.pallas_call(functools.partial(back_kernel, n_grp), out_shape=[jax.Shap...  187 us
    pallas_call x2, Pallas kernels, attend(): pl.pallas_call(attend_kernel, grid=(total // TILE,), out_shape=[jax.Shape...  38.9 us
    dot_general x5, matrix products, matdot(): lax.dot_general(left, right, (((left_dim,), (right_dim,)), ((), ())), pre...  30 us
    pallas_call x1, Pallas kernels, project(): pl.pallas_call(project_kernel, grid=(total // TILE,), out_shape=[jax.Shap...  16.9 us
    ppermute x16, starting transfers between devices, exchange(): return lax.ppermute(tensor, axis, [(i, i ^ bit) for i in range(size)])  16.4 us
    pallas_call x2, Pallas kernels, weight_grads(): pl.pallas_call(weight_grad_kernel, grid_spec=pltpu.PrefetchScalarGridSpec...  16.2 us
    unnamed x120, local copies, waits for them, and re-layouts  11.2 us
    ppermute x16, waiting for transfers between devices, exchange(): return lax.ppermute(tensor, axis, [(i, i ^ bit) for i in range(size)])  10.8 us
  transfers between devices with their start and end apart: 16, of which 6 were waited for; matrix products, arithmetic and copies ran while one was open for 22% of the time, Pallas kernels for 46%

profile of v3, /device:TPU:0, one launch (start us, length us, event | category | flops | bytes accessed | tf_op | source)
XLA Modules:
  0.0 426.5 jit_solution(11646913344894758017)
XLA Ops:
  0.7 3.0 collective-permute-start.1
  3.7 1.3 bitcast_reduce_fusion
  7.1 1.3 constant_dynamic-slice_fusion.4
  16.4 6.3 %convolution_add_fusion = f32[4,6144]{1,0:T(4,128)S(1)} fusion(bf16[4,1024]{1,0:T(4,128)(2,1)S(1)} %fusion.37, bf16[1024,6144]{1,0:T(8,128)(2,1)} %param.21, f32[6144]{0:T(1024)S(1)} %copy-done.33), kind=kOutput, calls=%fused_computation.10 | convolution fusion | flops 50356224 | bytes 12713984 | tf_op jit(solution)/shard_map/dot_general | solution.py:811
  23.6 2.3 pad_maximum_fusion.2.weight_t
  25.9 1.2 constant_dynamic-slice_fusion.3
  32.9 1.8 multiply_sine_fusion
  34.7 8.0 %fusion.50 = f32[512,6144]{1,0:T(8,128)} fusion(f32[4,6144]{1,0:T(4,128)S(1)} %convolution_add_fusion, s32[512]{0:T(512)S(1)} %convert_reduce_fusion.6), kind=kOutput, calls=%fused_computation.141 | convolution fusion | flops 150996992 | bytes 12683264 | tf_op jit(solution)/shard_map/dot_general | solution.py:830
  43.7 16.9 %project.1 = (bf16[2048,1024]{1,0:T(8,128)(2,1)}, bf16[256,2048]{1,0:T(8,128)(2,1)}, bf16[256,2048]{1,0:T(8,128)(2,1)}, bf16[256,2048]{1,0:T(8,128)(2,1)}, bf16[...) custom-call(s32[2]{0:T(128)} %pad_add_fusion.place, bf16[512,1024]{1,0:T(8,128)(2,1)} %frames_hbm.1, ...), custom_call_target="tpu_custom_call" | custom-call | flops 3221225472 | bytes 16777216 | tf_op jit(solution)/shard_map/project/pallas_call | solution.py:136
  60.6 19.5 %attend.3 = (bf16[128,2048]{1,0:T(8,128)(2,1)}, f32[8,2048]{1,0:T(8,128)}, bf16[512,128]{1,0:T(8,128)(2,1)}, bf16[512,128]{1,0:T(8,128)(2,1)}, bf16[512,128]{1,0:T(8,128)(2,1)}, /*index=5*/bf16[512,128]{1,0:T(8,128)(2,1)}) custom-call(s32[2]{0:T(128)} %pad_add_fusion.place, bf16[256,2048]{1,0:T(8,128)(2,1)} %get-tuple-element.44.qt, ...), custom_call_target="tpu_custom_call" | custom-call | flops 7516192768 | bytes 4194304 | tf_op jit(solution)/shard_map/attend/pallas_call | solution.py:223
  80.1 19.4 %attend.2 = (bf16[128,2048]{1,0:T(8,128)(2,1)}, f32[8,2048]{1,0:T(8,128)}, bf16[512,128]{1,0:T(8,128)(2,1)}, bf16[512,128]{1,0:T(8,128)(2,1)}, bf16[512,128]{1,0:T(8,128)(2,1)}, /*index=5*/bf16[512,128]{1,0:T(8,128)(2,1)}) custom-call(s32[2]{0:T(128)} %pad_add_fusion.place, bf16[256,2048]{1,0:T(8,128)(2,1)} %get-tuple-element.44.qt, ...), custom_call_target="tpu_custom_call" | custom-call | flops 7516192768 | bytes 4194304 | tf_op jit(solution)/shard_map/attend/pallas_call | solution.py:223
  101.3 1.9 collective-permute-start.6
  103.3 1.8 collective-permute-start.8
  105.2 2.6 collective-permute-done.5
  107.8 2.8 collective-permute-done.6
  111.7 2.8 collective-permute-done.8
  114.6 4.1 fusion.55
  119.9 3.9 convert_reduce_fusion.1
  124.0 4.5 %fusion.62 = f32[512,2048]{1,0:T(8,128)} fusion(bf16[512,1024]{1,0:T(8,128)(2,1)S(1)} %get-tuple-element.118.h, bf16[1024,2048]{1,0:T(8,128)(2,1)S(1)} %copy-done.38), kind=kOutput, calls=%fused_computation.150 | convolution fusion | flops 2147483648 | bytes 9437184 | tf_op jit(solution)/shard_map/dot_general | solution.py:838
  128.5 7.6 %convert_reduce_fusion = (f32[2048]{0:T(1024)S(1)}, bf16[512,2048]{1,0:T(8,128)(2,1)S(1)}, bf16[512,2048]{1,0:T(8,128)(2,1)S(1)}) fusion(f32[512,2048]{1,0:T(8,128)} %fusion.62, f32[2048]{0:T(1024)S(1)} %copy-done.47, bf16[512,1024]{1,0:T(8,128)(2,1)S(1)} %get-tuple-element.114.e_b, bf16[2048,1024]{1,0:T(8,128)(2,1)S(1)} %copy-done.12), kind=kOutput, calls=%fused_computation.20 | convolution fusion | flops 2173696000 | bytes 13647872 | tf_op jit(solution)/shard_map/dot_general | solution.py:28
  136.2 6.4 %fusion.51 = (f32[512]{0:T(512)S(1)}, f32[512]{0:T(512)S(1)}, f32[512,1024]{1,0:T(8,128)S(1)}) fusion(f32[512,6144]{1,0:T(8,128)S(1)} %bitcast.73, f32[512]{0:T(512)S(1)} %add_rsqrt_fusion, f32[512,1024]{1,0:T(8,128)S(1)} %get-tuple-element.116, f32[512]{0:T(512)S(1)} %broadcast_multiply_fusion.2, bf16[512,2048]{1,0:T(8,128)(2,1)S(1)} %get-tuple-element.112.e_z, ...), kind=kOutput, calls=%fused_computation.142 | convolution fusion | flops 2151152640 | bytes 12591104 | tf_op jit(solution)/shard_map/dot_general | solution.py:28
  142.6 6.4 %add_multiply_fusion = (f32[512,1024]{1,0:T(8,128)}, f32[512,1024]{1,0:T(8,128)S(1)}, bf16[512,1024]{1,0:T(8,128)(2,1)}, f32[512,1024]{1,0:T(8,128)}, f32[512,1024]{1,0:T(8,128)}) fusion(f32[512,1024]{1,0:T(8,128)} %get-tuple-element.149, f32[1024]{0:T(1024)S(1)} %copy-done.36, f32[512]{0:T(512)S(1)} %broadcast_multiply_fusion, f32[512]{0:T(512)S(1)} %add_rsqrt_fusion, ...), kind=kOutput, calls=%fused_computation.40 | convolution fusion | flops 2156920832 | bytes 27279360 | tf_op jit(solution)/shard_map/dot_general | solution.py:840
  149.0 1.7 convert_reduce_fusion.2
  150.7 8.2 %weight_grads.3 = bf16[2,1280,1024]{2,1,0:T(8,128)(2,1)} custom-call(s32[2]{0:T(128)} %pad_add_fusion.place, bf16[512,1024]{1,0:T(8,128)(2,1)} %copy-done.8, bf16[512,1024]{1,0:T(8,128)(2,1)} %copy-done.2, bf16[512,2048]{1,0:T(8,128)(2,1)} %copy-done, bf16[512,1024]{1,0:T(8,128)(2,1)} %get-tuple-element.110.e_att, bf16[512,2048]{1,0:T(8,128)(2,1)} %copy-done.4, ...), custom_call_target="tpu_custom_call" | custom-call | flops 2684354560 | bytes 12582912 | tf_op jit(solution)/shard_map/weight_grads/pallas_call | solution.py:736
  159.5 1.5 collective-permute-start.13
  161.7 1.5 collective-permute-done.13
  163.2 1.6 collective-permute-start.14
  167.6 2.6 collective-permute-start.15
  170.2 2.8 convolution_convert_fusion
  174.5 1.5 collective-permute-start.9
  176.0 8.0 %weight_grads.2 = bf16[2,1280,1024]{2,1,0:T(8,128)(2,1)} custom-call(s32[2]{0:T(128)} %pad_add_fusion.place, bf16[512,1024]{1,0:T(8,128)(2,1)} %copy-done.8, bf16[512,1024]{1,0:T(8,128)(2,1)} %copy-done.2, bf16[512,2048]{1,0:T(8,128)(2,1)} %copy-done, bf16[512,1024]{1,0:T(8,128)(2,1)} %get-tuple-element.110.e_att, bf16[512,2048]{1,0:T(8,128)(2,1)} %copy-done.4, ...), custom_call_target="tpu_custom_call" | custom-call | flops 2684354560 | bytes 12582912 | tf_op jit(solution)/shard_map/weight_grads/pallas_call | solution.py:736
  184.0 5.1 %fusion = f32[4,4096]{1,0:T(4,128)S(1)} fusion(f32[512,1024]{1,0:T(8,128)} %get-tuple-element.121, f32[512,1024]{1,0:T(8,128)} %get-tuple-element.120, f32[512,1024]{1,0:T(8,128)S(1)} %get-tuple-element.150, f32[512,1024]{1,0:T(8,128)} %get-tuple-element.107, s32[512]{0:T(512)S(1)} %convert_reduce_fusion.6), kind=kOutput, calls=%fused_computation.2 | convolution fusion | flops 106956800 | bytes 8456192 | tf_op jit(solution)/shard_map/dot_general | solution.py:862
  189.8 7.5 %add_convert_fusion.packed_hbm = bf16[2,1280,1024]{2,1,0:T(8,128)(2,1)} fusion(bf16[2,1280,1024]{2,1,0:T(8,128)(2,1)} %collective-permute-done.12, bf16[2,1280,1024]{2,1,0:T(8,128)(2,1)S(1)} %bitcast.75), kind=kLoop, calls=%fused_computation.1 | loop fusion | flops 10485760 | bytes 15728640 | tf_op jit(solution)/shard_map/convert_element_type | solution.py:63
  198.7 187.4 %attend_back.1 = (bf16[512,1024]{1,0:T(8,128)(2,1)}, bf16[640,1024]{1,0:T(8,128)(2,1)}, bf16[640,1024]{1,0:T(8,128)(2,1)}, bf16[4,256,384]{2,1,0:T(8,128)(2,1)},...) custom-call(s32[2]{0:T(128)} %pad_add_fusion.place, ...), custom_call_target="tpu_custom_call" | custom-call | flops 37580963840 | bytes 41943040 | tf_op jit(solution)/shard_map/attend_back/pallas_call | solution.py:669
  386.2 2.9 fusion.19
  389.2 1.8 maximum_convert_fusion.1
  394.7 1.9 convert_bitcast_fusion
  396.5 2.4 copy.62
  398.9 1.8 fusion.56
  401.6 8.7 %fusion.28 = f32[1,4,1024]{2,1,0:T(4,128)} fusion(f32[1,4,1024]{2,1,0:T(4,128)S(1)} %copy-done.29, bf16[1024,6144]{1,0:T(8,128)(2,1)} %param.21, bf16[8,4,6144]{2,1,0:T(4,128)(2,1)S(1)} %get-tuple-element.106), kind=kOutput, calls=%fused_computation.79 | convolution fusion | flops 50368512 | bytes 12664832 | tf_op jit(solution)/shard_map/dot_general | solution.py:28
  410.9 1.5 pad_maximum_fusion.1
  412.4 1.4 fusion.60
  413.9 1.3 dynamic_slice.66
  415.2 1.3 copy.63
  416.5 1.3 copy.64
  417.8 1.3 copy.65
  419.1 1.4 dynamic_slice.64
  420.5 4.6 %fusion.32 = f32[256,6144]{1,0:T(8,128)} fusion(bf16[32,6144]{1,0:T(8,128)(2,1)S(1)} %reshape.139, s32[]{:T(128)S(6)} %select_n.70, bf16[4,1024]{1,0:T(4,128)(2,1)S(1)} %fusion.37, bf16[4,1024]{1,0:T(4,128)(2,1)S(1)} %collective-permute-done.13, bf16[8,1024]{1,0:T(8,128)(2,1)S(1)} %copy-done.31, bf16[16,1024]{1,0:T(8,128)(2,1)} %collective-permute-done.15), kind=kOutput, calls=%fused_computation.83 | convolution fusion | flops 100728832 | bytes 6750212 | tf_op jit(solution)/shard_map/dot_general | solution.py:28
  (194 shorter events, 34.2 us)
Async XLA Ops:
  0.7 28.8 %collective-permute-start.1 = (bf16[512,1024]{1,0:T(8,128)(2,1)}, bf16[512,1024]{1,0:T(8,128)(2,1)}, u32[]{:S(2)}, u32[]{:S(2)}) collective-permute-start(bf16[512,1024]{1,0:T(8,128)(2,1)} %frames_hbm.1), channel_id=1, source_target_pairs={{0,2},{1,3},{2,0},{3,1},{4,6},{5,7},{6,4},{7,5},{8,10},{9,11},{10,... | collective-permute-start | bytes 3145736 | tf_op jit(solution)/shard_map/ppermute | solution.py:59
  3.7 39.1 %collective-permute-start = (bf16[512,1024]{1,0:T(8,128)(2,1)}, bf16[512,1024]{1,0:T(8,128)(2,1)}, u32[]{:S(2)}, u32[]{:S(2)}) collective-permute-start(bf16[512,1024]{1,0:T(8,128)(2,1)} %frames_hbm.1), channel_id=1, source_target_pairs={{0,1},{1,0},{2,3},{3,2},{4,5},{5,4},{6,7},{7,6},{8,9},{9,8},{10,11... | collective-permute-start | bytes 3145736 | tf_op jit(solution)/shard_map/ppermute | solution.py:59
  8.4 8.0 %copy-start.28 = (f32[1,4,1024]{2,1,0:T(4,128)S(1)}, f32[1,4,1024]{2,1,0:T(4,128)}, u32[]{:S(2)}) copy-start(f32[1,4,1024]{2,1,0:T(4,128)} %param.19) | copy-start | bytes 49156
  8.4 8.0 %copy-start.33 = (f32[6144]{0:T(1024)S(1)}, f32[6144]{0:T(1024)}, u32[]{:S(2)}) copy-start(f32[6144]{0:T(1024)} %param.22) | copy-start | bytes 73732
  22.8 4.4 %copy-start.32 = (f32[4,2048]{1,0:T(4,128)}, f32[4,2048]{1,0:T(4,128)S(1)}, u32[]{:S(2)}) copy-start(f32[4,2048]{1,0:T(4,128)S(1)} %slice.103.mod_all) | copy-start | bytes 98308
  27.1 87.4 %copy-start.22 = (bf16[256,1024]{1,0:T(8,128)(2,1)}, bf16[256,1024]{1,0:T(8,128)(2,1)S(1)}, u32[]{:S(2)}) copy-start(bf16[256,1024]{1,0:T(8,128)(2,1)S(1)} %get-tuple-element.128) | copy-start | bytes 1572868
  27.1 87.4 %copy-start.23 = (bf16[256,1024]{1,0:T(8,128)(2,1)}, bf16[256,1024]{1,0:T(8,128)(2,1)S(1)}, u32[]{:S(2)}) copy-start(bf16[256,1024]{1,0:T(8,128)(2,1)S(1)} %get-tuple-element.129) | copy-start | bytes 1572868
  29.5 13.3 %collective-permute-start.2 = (bf16[512,1024]{1,0:T(8,128)(2,1)}, bf16[512,1024]{1,0:T(8,128)(2,1)S(1)}, u32[]{:S(2)}, u32[]{:S(2)}) collective-permute-start(bf16[512,1024]{1,0:T(8,128)(2,1)} %collective-permute-done.1.x2), channel_id=1, source_target_pairs={{0,1},{1,0},{2,3},{3,2},{4,5},{5,4},{6,7},{7,6},{8,9},{9,8},{10,11... | collective-permute-start | bytes 3145736 | tf_op jit(solution)/shard_map/ppermute | solution.py:59
  31.2 11.5 %copy-start.35 = (s32[256]{0:T(256)}, s32[256]{0:T(256)S(1)}, u32[]{:S(2)}) copy-start(s32[256]{0:T(256)S(1)} %slice.105) | copy-start | bytes 3076
  80.1 20.6 %copy-start.46 = (bf16[512,128]{1,0:T(8,128)(2,1)S(1)}, bf16[512,128]{1,0:T(8,128)(2,1)}, u32[]{:S(2)}) copy-start(bf16[512,128]{1,0:T(8,128)(2,1)} %get-tuple-element.50) | copy-start | bytes 393220
  80.1 21.2 %copy-start.45 = (bf16[512,128]{1,0:T(8,128)(2,1)S(1)}, bf16[512,128]{1,0:T(8,128)(2,1)}, u32[]{:S(2)}) copy-start(bf16[512,128]{1,0:T(8,128)(2,1)} %get-tuple-element.52) | copy-start | bytes 393220
  80.1 23.1 %copy-start.27 = (bf16[512,128]{1,0:T(8,128)(2,1)S(1)}, bf16[512,128]{1,0:T(8,128)(2,1)}, u32[]{:S(2)}) copy-start(bf16[512,128]{1,0:T(8,128)(2,1)} %get-tuple-element.48) | copy-start | bytes 393220
  80.1 23.2 %copy-start.44 = (bf16[512,128]{1,0:T(8,128)(2,1)S(1)}, bf16[512,128]{1,0:T(8,128)(2,1)}, u32[]{:S(2)}) copy-start(bf16[512,128]{1,0:T(8,128)(2,1)} %get-tuple-element.54) | copy-start | bytes 393220
  99.5 15.0 %copy-start.24 = (bf16[256,1024]{1,0:T(8,128)(2,1)S(1)}, bf16[256,1024]{1,0:T(8,128)(2,1)}, u32[]{:S(2)}) copy-start(bf16[256,1024]{1,0:T(8,128)(2,1)} %get-tuple-element.130) | copy-start | bytes 1572868
  99.5 15.0 %copy-start.25 = (bf16[256,1024]{1,0:T(8,128)(2,1)S(1)}, bf16[256,1024]{1,0:T(8,128)(2,1)}, u32[]{:S(2)}) copy-start(bf16[256,1024]{1,0:T(8,128)(2,1)} %get-tuple-element.131) | copy-start | bytes 1572868
  99.5 15.0 %copy-start.36 = (f32[1024]{0:T(1024)S(1)}, f32[1024]{0:T(1024)}, u32[]{:S(2)}) copy-start(f32[1024]{0:T(1024)} %param.30) | copy-start | bytes 12292
  99.5 15.0 %copy-start.39 = (bf16[512,1024]{1,0:T(8,128)(2,1)S(1)}, bf16[512,1024]{1,0:T(8,128)(2,1)}, u32[]{:S(2)}) copy-start(bf16[512,1024]{1,0:T(8,128)(2,1)} %frames_hbm.1) | copy-start | bytes 3145732
  99.5 3.7 collective-permute-start.3
  100.7 4.4 %collective-permute-start.4 = (bf16[512,128]{1,0:T(8,128)(2,1)S(1)}, bf16[512,128]{1,0:T(8,128)(2,1)S(1)}, u32[]{:S(2)}, u32[]{:S(2)}) collective-permute-start(bf16[512,128]{1,0:T(8,128)(2,1)S(1)} %copy-done.46), channel_id=1, source_target_pairs={{0,1},{1,0},{2,3},{3,2},{4,5},{5,4},{6,7},{7,6},{8,9},{9,8},{10,11... | collective-permute-start | bytes 393224 | tf_op jit(solution)/shard_map/ppermute | solution.py:59
  101.2 6.6 %collective-permute-start.5 = (bf16[512,128]{1,0:T(8,128)(2,1)}, bf16[512,128]{1,0:T(8,128)(2,1)S(1)}, u32[]{:S(2)}, u32[]{:S(2)}) collective-permute-start(bf16[512,128]{1,0:T(8,128)(2,1)} %get-tuple-element.51), channel_id=1, source_target_pairs={{0,2},{1,3},{2,0},{3,1},{4,6},{5,7},{6,4},{7,5},{8,10},{9,11},{10,... | collective-permute-start | bytes 393224 | tf_op jit(solution)/shard_map/ppermute | solution.py:59
  101.3 9.3 %collective-permute-start.6 = (bf16[512,128]{1,0:T(8,128)(2,1)S(1)}, bf16[512,128]{1,0:T(8,128)(2,1)S(1)}, u32[]{:S(2)}, u32[]{:S(2)}) collective-permute-start(bf16[512,128]{1,0:T(8,128)(2,1)S(1)} %copy-done.45), channel_id=1, source_target_pairs={{0,2},{1,3},{2,0},{3,1},{4,6},{5,7},{6,4},{7,5},{8,10},{9,11},{10,... | collective-permute-start | bytes 393224 | tf_op jit(solution)/shard_map/ppermute | solution.py:59
  103.2 8.5 %collective-permute-start.7 = (bf16[512,128]{1,0:T(8,128)(2,1)}, bf16[512,128]{1,0:T(8,128)(2,1)S(1)}, u32[]{:S(2)}, u32[]{:S(2)}) collective-permute-start(bf16[512,128]{1,0:T(8,128)(2,1)} %get-tuple-element.53), channel_id=1, source_target_pairs={{0,3},{1,2},{2,1},{3,0},{4,7},{5,6},{6,5},{7,4},{8,11},{9,10},{10,... | collective-permute-start | bytes 393224 | tf_op jit(solution)/shard_map/ppermute | solution.py:59
  103.3 11.2 %collective-permute-start.8 = (bf16[512,128]{1,0:T(8,128)(2,1)S(1)}, bf16[512,128]{1,0:T(8,128)(2,1)S(1)}, u32[]{:S(2)}, u32[]{:S(2)}) collective-permute-start(bf16[512,128]{1,0:T(8,128)(2,1)S(1)} %copy-done.44), channel_id=1, source_target_pairs={{0,3},{1,2},{2,1},{3,0},{4,7},{5,6},{6,5},{7,4},{8,11},{9,10},{10,... | collective-permute-start | bytes 393224 | tf_op jit(solution)/shard_map/ppermute | solution.py:59
  123.8 4.7 %copy-start.2 = (bf16[512,1024]{1,0:T(8,128)(2,1)}, bf16[512,1024]{1,0:T(8,128)(2,1)S(1)}, u32[]{:S(2)}) copy-start(bf16[512,1024]{1,0:T(8,128)(2,1)S(1)} %get-tuple-element.118.h) | copy-start | bytes 3145732
  123.8 4.7 %copy-start.1 = (bf16[512,1024]{1,0:T(8,128)(2,1)}, bf16[512,1024]{1,0:T(8,128)(2,1)S(1)}, u32[]{:S(2)}) copy-start(bf16[512,1024]{1,0:T(8,128)(2,1)S(1)} %get-tuple-element.114.e_b) | copy-start | bytes 3145732
  124.0 4.5 %copy-start.12 = (bf16[2048,1024]{1,0:T(8,128)(2,1)S(1)}, bf16[2048,1024]{1,0:T(8,128)(2,1)}, u32[]{:S(2)}) copy-start(bf16[2048,1024]{1,0:T(8,128)(2,1)} %param.33) | copy-start | bytes 12582916
  124.0 4.5 %copy-start.47 = (f32[2048]{0:T(1024)S(1)}, f32[2048]{0:T(1024)}, u32[]{:S(2)}) copy-start(f32[2048]{0:T(1024)} %param.32) | copy-start | bytes 24580
  124.0 12.1 %slice-start = ((s8[12582912]{0:T(1024)(128)(4,1)}), s8[4194304]{0:T(1024)(128)(4,1)S(1)}, s32[]{:S(2)}) async-start(s8[12582912]{0:T(1024)(128)(4,1)} %bitcast.72), calls=%async_computation | async-start | bytes 8388608
  128.5 7.7 %slice-start.1 = ((s8[12582912]{0:T(1024)(128)(4,1)}), s8[4194304]{0:T(1024)(128)(4,1)S(1)}, s32[]{:S(2)}) async-start(s8[12582912]{0:T(1024)(128)(4,1)} %bitcast.72), calls=%async_computation.1 | async-start | bytes 8388608
  128.5 7.7 %slice-start.2 = ((s8[12582912]{0:T(1024)(128)(4,1)}), s8[4194304]{0:T(1024)(128)(4,1)S(1)}, s32[]{:S(2)}) async-start(s8[12582912]{0:T(1024)(128)(4,1)} %bitcast.72), calls=%async_computation.2 | async-start | bytes 8388608
  136.1 6.5 %copy-start.4 = (bf16[512,2048]{1,0:T(8,128)(2,1)}, bf16[512,2048]{1,0:T(8,128)(2,1)S(1)}, u32[]{:S(2)}) copy-start(bf16[512,2048]{1,0:T(8,128)(2,1)S(1)} %get-tuple-element.112.e_z) | copy-start | bytes 6291460
  136.1 6.5 %copy-start = (bf16[512,2048]{1,0:T(8,128)(2,1)}, bf16[512,2048]{1,0:T(8,128)(2,1)S(1)}, u32[]{:S(2)}) copy-start(bf16[512,2048]{1,0:T(8,128)(2,1)S(1)} %get-tuple-element.119.a) | copy-start | bytes 6291460
  136.2 6.5 %copy-start.37 = (f32[1024]{0:T(1024)S(1)}, f32[1024]{0:T(1024)}, u32[]{:S(2)}) copy-start(f32[1024]{0:T(1024)} %param.34) | copy-start | bytes 12292
  150.7 19.6 %copy-start.3 = (bf16[512,1024]{1,0:T(8,128)(2,1)S(1)}, bf16[512,1024]{1,0:T(8,128)(2,1)}, u32[]{:S(2)}) copy-start(bf16[512,1024]{1,0:T(8,128)(2,1)} %get-tuple-element.110.e_att) | copy-start | bytes 3145732
  158.9 30.9 %collective-permute-start.12 = (bf16[2,1280,1024]{2,1,0:T(8,128)(2,1)}, bf16[2,1280,1024]{2,1,0:T(8,128)(2,1)}, u32[]{:S(2)}, u32[]{:S(2)}) collective-permute-start(bf16[2,1280,1024]{2,1,0:T(8,128)(2,1)} %weight_grads.3), channel_id=1, source_target_pairs={{0,1},{1,0},{2,3},{3,2},{4,5},{5,4},{6,7},{7,6},{8,9},{9,8},{10,11... | collective-permute-start | bytes 15728648 | tf_op jit(solution)/shard_map/ppermute | solution.py:59
  159.5 3.7 collective-permute-start.13
  163.2 3.8 collective-permute-start.14
  167.0 6.0 %copy-start.30 = (bf16[8,1024]{1,0:T(8,128)(2,1)}, bf16[8,1024]{1,0:T(8,128)(2,1)S(1)}, u32[]{:S(2)}) copy-start(bf16[8,1024]{1,0:T(8,128)(2,1)S(1)} %collective-permute-done.14) | copy-start | bytes 49156
  167.6 252.9 %collective-permute-start.15 = (bf16[16,1024]{1,0:T(8,128)(2,1)}, bf16[16,1024]{1,0:T(8,128)(2,1)}, u32[]{:S(2)}, u32[]{:S(2)}) collective-permute-start(bf16[16,1024]{1,0:T(8,128)(2,1)} %pad_maximum_fusion.9), channel_id=1, source_target_pairs={{0,16},{4,20},{8,24},{12,28},{16,0},{20,4},{24,8},{28,12},{1,17},{... | collective-permute-start | bytes 98312 | tf_op jit(solution)/shard_map/ppermute | solution.py:59
  173.8 23.5 %collective-permute-start.10 = (bf16[512,256]{1,0:T(8,128)(2,1)S(1)}, bf16[512,256]{1,0:T(8,128)(2,1)S(1)}, u32[]{:S(2)}, u32[]{:S(2)}) collective-permute-start(bf16[512,256]{1,0:T(8,128)(2,1)S(1)} %get-tuple-element.133), channel_id=1, source_target_pairs={{0,2},{1,3},{2,0},{3,1},{4,6},{5,7},{6,4},{7,5},{8,10},{9,11},{10,... | collective-permute-start | bytes 786440 | tf_op jit(solution)/shard_map/ppermute | solution.py:59
  174.5 22.9 %collective-permute-start.11 = (bf16[512,256]{1,0:T(8,128)(2,1)S(1)}, bf16[512,256]{1,0:T(8,128)(2,1)S(1)}, u32[]{:S(2)}, u32[]{:S(2)}) collective-permute-start(bf16[512,256]{1,0:T(8,128)(2,1)S(1)} %get-tuple-element.132), channel_id=1, source_target_pairs={{0,3},{1,2},{2,1},{3,0},{4,7},{5,6},{6,5},{7,4},{8,11},{9,10},{10,... | collective-permute-start | bytes 786440 | tf_op jit(solution)/shard_map/ppermute | solution.py:59
  174.5 22.9 %collective-permute-start.9 = (bf16[512,256]{1,0:T(8,128)(2,1)S(1)}, bf16[512,256]{1,0:T(8,128)(2,1)S(1)}, u32[]{:S(2)}, u32[]{:S(2)}) collective-permute-start(bf16[512,256]{1,0:T(8,128)(2,1)S(1)} %get-tuple-element.134), channel_id=1, source_target_pairs={{0,1},{1,0},{2,3},{3,2},{4,5},{5,4},{6,7},{7,6},{8,9},{9,8},{10,11... | collective-permute-start | bytes 786440 | tf_op jit(solution)/shard_map/ppermute | solution.py:59
  184.0 5.8 %slice-start.3 = ((s8[5242880]{0:T(1024)(128)(4,1)}), s8[4194304]{0:T(1024)(128)(4,1)S(1)}, s32[]{:S(2)}) async-start(s8[5242880]{0:T(1024)(128)(4,1)} %bitcast.74), calls=%async_computation.3 | async-start | bytes 8388608
  184.0 5.8 %slice-start.4 = ((s8[5242880]{0:T(1024)(128)(4,1)}), s8[1048576]{0:T(1024)(128)(4,1)S(1)}, s32[]{:S(2)}) async-start(s8[5242880]{0:T(1024)(128)(4,1)} %bitcast.74), calls=%async_computation.4 | async-start | bytes 2097152
  401.6 8.7 %copy-start.34 = (f32[768]{0:T(1024)S(1)}, f32[768]{0:T(1024)}, u32[]{:S(2)}) copy-start(f32[768]{0:T(1024)} %convert_reduce_fusion.5) | copy-start | bytes 9220
  401.6 9.3 %copy-start.13 = (f32[256,1024]{1,0:T(8,128)S(1)}, f32[256,1024]{1,0:T(8,128)}, u32[]{:S(2)}) copy-start(f32[256,1024]{1,0:T(8,128)} %get-tuple-element.125) | copy-start | bytes 3145732
  401.6 9.3 %copy-start.14 = (f32[256,1024]{1,0:T(8,128)S(1)}, f32[256,1024]{1,0:T(8,128)}, u32[]{:S(2)}) copy-start(f32[256,1024]{1,0:T(8,128)} %get-tuple-element.126) | copy-start | bytes 3145732
  420.5 4.6 %copy-start.17 = (bf16[512,1024]{1,0:T(8,128)(2,1)S(1)}, bf16[512,1024]{1,0:T(8,128)(2,1)}, u32[]{:S(2)}) copy-start(bf16[512,1024]{1,0:T(8,128)(2,1)} %get-tuple-element.171) | copy-start | bytes 3145732
  (21 other events, 50.2 us)
